TPU v7x, 256 devices: a whole 4x4x8 slice. The times are simulated.
256 devices in a mesh: gx: 32 (over x, y, core), gy: 8 (over z).
Axes of the slice: x: 4, y: 4, z: 8, core: 2. Of those that a mesh axis runs over, the one named last changes fastest.
Arguments:
- cotangent: float32 [256, 512, 512], P('gx', 'gy'), may hold values from -6 to 6
- coefficient: float32 [256, 512, 512], P('gx', 'gy'), may hold values from 0.5 to 6
Outputs:
- rhs_cotangent: float32 [256, 512, 512], P('gx', 'gy')
All inputs are finite; a program needn't handle non-finite values.
Results may differ from a plain program's by a relative error of at most 0.00024.
Values sent between devices are 32-bit elements; how exact they have to be, the bound alone decides.
No kernel may reach another device: no remote copies, remote signals or barrier semaphores. Data moves between devices by JAX's collectives and lax.ppermute only.
A program may use at most 64 MiB of HBM per device.

v0:
```python
import math

import jax
import jax.numpy as jnp
from jax import lax
from jax.sharding import PartitionSpec as P

screen = 0.02
first_weight = 1.0 / (1.25 + 0.75 * math.cos(math.pi / 4.0))
second_weight = 1.0 / (1.25 - 0.75 * math.cos(math.pi / 4.0))


def padded_2(block, sides, width):
    for axis, dim in sides:
        count = lax.axis_size(axis)
        forward = [(i, i + 1) for i in range(count - 1)]
        forward.append((count - 1, 0))
        backward = [(target, source) for source, target in forward]
        low = lax.ppermute(
            lax.slice_in_dim(block, block.shape[dim] - width, None, axis=dim), axis, forward
        )
        high = lax.ppermute(lax.slice_in_dim(block, 0, width, axis=dim), axis, backward)
        block = jnp.concatenate([low, block, high], axis=dim)
    return block


def stencil(padded, coefficient):
    middle = padded[1:-1, 1:-1]
    beside = padded[2:, 1:-1] + padded[:-2, 1:-1]
    beside = beside + padded[1:-1, 2:] + padded[1:-1, :-2]
    beside = beside + jnp.roll(middle, 1, 2) + jnp.roll(middle, -1, 2)
    return (6.0 + coefficient) * middle - beside


def widened(field):
    return padded_2(field, (("gx", 0), ("gy", 1)), 1)


def symbol(index, length):
    return 2.0 - 2.0 * jnp.cos(2.0 * math.pi * index.astype(jnp.float32) / length)


def phase_table(length, out_index):
    source = jnp.arange(length)
    product = source[:, None] * out_index[None, :] % length
    angle = 2.0 * math.pi / length * product.astype(jnp.float32)
    return (jnp.cos(angle), jnp.sin(angle))


def contract(field, matrix, dim_index):
    moved = jnp.moveaxis(field, dim_index, -1)
    result = jnp.dot(moved, matrix, precision=lax.Precision.HIGHEST)
    return jnp.moveaxis(result, -1, dim_index)


def transform(real_part, imag_part, dim_index, direction, out_index):
    cosines, sines = phase_table(real_part.shape[dim_index], out_index)
    real_cos = contract(real_part, cosines, dim_index)
    real_sin = contract(real_part, sines, dim_index)
    imag_cos = contract(imag_part, cosines, dim_index)
    imag_sin = contract(imag_part, sines, dim_index)
    if direction < 0:
        return (real_cos + imag_sin, imag_cos - real_sin)
    return (real_cos - imag_sin, imag_cos + real_sin)


def spectrum_of(freq_x, length_x, freq_y, length_y, freq_z, length_z):
    return (
        screen
        + symbol(freq_x, length_x)[:, None, None]
        + symbol(freq_y, length_y)[None, :, None]
        + symbol(freq_z, length_z)[None, None, :]
    )


def pencil_solve(sums):
    block_x, block_y, length_z = sums.shape
    real_part, imag_part = transform(sums, jnp.zeros_like(sums), 2, -1, jnp.arange(length_z))
    stacked = lax.all_to_all(
        jnp.stack([real_part, imag_part]), "gy", split_axis=3, concat_axis=2, tiled=True
    )
    length_y = stacked.shape[2]
    slab_z = stacked.shape[3]
    real_part, imag_part = transform(stacked[0], stacked[1], 1, -1, jnp.arange(length_y))
    stacked = lax.all_to_all(
        jnp.stack([real_part, imag_part]), "gx", split_axis=2, concat_axis=1, tiled=True
    )
    length_x = stacked.shape[1]
    slab_y = stacked.shape[2]
    real_part, imag_part = transform(stacked[0], stacked[1], 0, -1, jnp.arange(length_x))
    freq_y = lax.axis_index("gx") * slab_y + jnp.arange(slab_y)
    freq_z = lax.axis_index("gy") * slab_z + jnp.arange(slab_z)
    spectrum = spectrum_of(jnp.arange(length_x), length_x, freq_y, length_y, freq_z, length_z)
    real_part = real_part / spectrum
    imag_part = imag_part / spectrum
    real_part, imag_part = transform(real_part, imag_part, 0, 1, jnp.arange(length_x))
    stacked = lax.all_to_all(
        jnp.stack([real_part, imag_part]), "gx", split_axis=1, concat_axis=2, tiled=True
    )
    real_part, imag_part = transform(stacked[0], stacked[1], 1, 1, jnp.arange(length_y))
    stacked = lax.all_to_all(
        jnp.stack([real_part, imag_part]), "gy", split_axis=2, concat_axis=3, tiled=True
    )
    real_part, imag_part = transform(stacked[0], stacked[1], 2, 1, jnp.arange(length_z))
    return real_part / float(length_x * length_y * length_z)


def body(cotangent, coefficient):
    inverse = 1.0 / (6.0 + coefficient)
    weight_five = second_weight * cotangent * inverse
    carried_four = cotangent - stencil(widened(weight_five), coefficient)
    weight_four = first_weight * carried_four * inverse
    carried_three = carried_four - stencil(widened(weight_four), coefficient)
    summed = weight_five + weight_four
    size_x, size_y, size_z = carried_three.shape
    block_sums = carried_three.reshape(size_x // 8, 8, size_y // 8, 8, size_z // 8, 8).sum(
        axis=(1, 3, 5)
    )
    coarse = pencil_solve(block_sums)
    spread = jnp.broadcast_to(
        coarse[:, None, :, None, :, None], (size_x // 8, 8, size_y // 8, 8, size_z // 8, 8)
    )
    spread = spread.reshape(size_x, size_y, size_z) / 8.0
    carried_two = carried_three - stencil(widened(spread), coefficient)
    weight_two = second_weight * carried_two * inverse
    carried_one = carried_two - stencil(widened(weight_two), coefficient)
    summed = summed + spread + weight_two
    return summed + first_weight * carried_one * inverse


def solution(mesh):
    placed = (P("gx", "gy", None), P("gx", "gy", None))
    return jax.shard_map(
        body, mesh=mesh, in_specs=placed, out_specs=P("gx", "gy", None), check_vma=False
    )
```

profile of v0, /device:TPU:31, one launch (start us, length us, event | category | flops | bytes accessed | tf_op | source)
XLA Modules:
  0.0 130.5 jit_solution(7559760594773242592)
XLA Ops:
  0.0 1.8 %multiply_multiply_fusion.2 = f32[8,64,512]{2,1,0:T(8,128)S(1)} fusion(f32[8,64,512]{2,1,0:T(8,128)} %param.2, f32[8,64,512]{2,1,0:T(8,128)} %param.3), kind=kLoop, calls=%fused_computation.87 | loop fusion | flops 1048576 | bytes 3145728 | tf_op jit(solution)/shard_map/mul | solution.py:110
  1.8 0.7 fusion.208
  2.5 2.2 %collective-permute-start.1 = (f32[1,64,512]{2,1,0:T(8,128)}, f32[1,64,512]{2,1,0:T(8,128)S(1)}, u32[]{:S(2)}, u32[]{:S(2)}) collective-permute-start(f32[1,64,512]{2,1,0:T(8,128)} %get-tuple-element.31), channel_id=1, source_target_pairs={{0,8},{8,16},{16,24},{24,32},{32,40},{40,48},{48,56},{56,64},{64,7... | collective-permute-start | bytes 393224 | tf_op jit(solution)/shard_map/ppermute | solution.py:19
  4.6 0.8 fusion.209
  5.4 1.7 %fusion.210 = (f32[8,64,511]{2,1,0:T(8,128)}, f32[8,64,511]{2,1,0:T(8,128)}) fusion(f32[8,64,512]{2,1,0:T(8,128)S(1)} %multiply_multiply_fusion.2), kind=kLoop, calls=%fused_computation.263 | loop fusion | bytes 4186112 | tf_op jit(solution)/shard_map/jit(_roll_static)/slice | solution.py:31
  7.5 5.2 %collective-permute-done = f32[1,64,512]{2,1,0:T(8,128)} collective-permute-done((f32[1,64,512]{2,1,0:T(8,128)}, f32[1,64,512]{2,1,0:T(8,128)}, u32[]{:S(2)}, u32[]{:S(2)}) %collective-permute-start) | collective-permute-done | bytes 131104 | tf_op jit(solution)/shard_map/ppermute | solution.py:22
  12.7 0.8 pad_maximum_fusion.43
  13.4 3.9 %collective-permute-start.2 = (f32[10,1,512]{2,1,0:T(1,128)S(1)}, f32[10,1,512]{2,1,0:T(1,128)S(1)}, u32[]{:S(2)}, u32[]{:S(2)}) collective-permute-start(f32[10,1,512]{2,1,0:T(1,128)S(1)} %get-tuple-element.17), channel_id=1, source_target_pairs={{1,0},{2,1},{3,2},{4,3},{5,4},{6,5},{7,6},{0,7},{9,8},{10,9},{11,1... | collective-permute-start | bytes 61448 | tf_op jit(solution)/shard_map/ppermute | solution.py:22
  17.4 0.9 collective-permute-done.2
  18.3 2.9 %collective-permute-done.3 = f32[10,1,512]{2,1,0:T(1,128)S(1)} collective-permute-done((f32[10,1,512]{2,1,0:T(1,128)S(1)}, f32[10,1,512]{2,1,0:T(1,128)S(1)}, u32[]{:S(2)}, u32[]{:S(2)}) %collective-permute-start.3) | collective-permute-done | bytes 20512 | tf_op jit(solution)/shard_map/ppermute | solution.py:19
  21.2 2.1 %multiply_multiply_fusion.1 = (f32[8,64,512]{2,1,0:T(8,128)S(1)}, f32[8,64,512]{2,1,0:T(8,128)S(1)}) fusion(f32[8,64,512]{2,1,0:T(8,128)S(1)} %copy-done, f32[8,64,512]{2,1,0:T(8,128)S(1)} %copy-done.1, f32[8,64,1]{2,1,0:T(8,128)} %get-tuple-element.34, f32[8,64,511]{2,1,0:T(8,128)} %get-tuple-element.36, f32[8,64,511]{2,1,0:T(8,128)S(1)} %copy-done.6, ...), kind=kLoop, calls=%fused_computation.86 | loop fusion | flops 5767168 | bytes 7643136 | tf_op jit(solution)/shard_map/mul | solution.py:112
  23.4 1.4 %collective-permute-start.5 = (f32[1,64,512]{2,1,0:T(8,128)S(1)}, f32[1,64,512]{2,1,0:T(8,128)S(1)}, u32[]{:S(2)}, u32[]{:S(2)}) collective-permute-start(f32[1,64,512]{2,1,0:T(8,128)S(1)} %get-tuple-element.25), channel_id=1, source_target_pairs={{0,8},{8,16},{16,24},{24,32},{32,40},{40,48},{48,56},{56,64},{64,7... | collective-permute-start | bytes 393224 | tf_op jit(solution)/shard_map/ppermute | solution.py:19
  25.2 1.6 %collective-permute-done.5 = f32[1,64,512]{2,1,0:T(8,128)S(1)} collective-permute-done((f32[1,64,512]{2,1,0:T(8,128)S(1)}, f32[1,64,512]{2,1,0:T(8,128)S(1)}, u32[]{:S(2)}, u32[]{:S(2)}) %collective-permute-start.5) | collective-permute-done | bytes 131104 | tf_op jit(solution)/shard_map/ppermute | solution.py:19
  26.8 5.8 %collective-permute-done.4 = f32[1,64,512]{2,1,0:T(8,128)S(1)} collective-permute-done((f32[1,64,512]{2,1,0:T(8,128)S(1)}, f32[1,64,512]{2,1,0:T(8,128)S(1)}, u32[]{:S(2)}, u32[]{:S(2)}) %collective-permute-start.4) | collective-permute-done | bytes 131104 | tf_op jit(solution)/shard_map/ppermute | solution.py:22
  32.7 1.5 %collective-permute-start.7 = (f32[10,1,512]{2,1,0:T(1,128)S(1)}, f32[10,1,512]{2,1,0:T(1,128)S(1)}, u32[]{:S(2)}, u32[]{:S(2)}) collective-permute-start(f32[10,1,512]{2,1,0:T(1,128)S(1)} %get-tuple-element.16), channel_id=1, source_target_pairs={{0,1},{1,2},{2,3},{3,4},{4,5},{5,6},{6,7},{7,0},{8,9},{9,10},{10,1... | collective-permute-start | bytes 61448 | tf_op jit(solution)/shard_map/ppermute | solution.py:19
  34.3 1.0 collective-permute-done.6
  35.3 1.3 collective-permute-done.7
  36.6 1.8 %fusion.199 = (f32[64,512]{1,0:T(8,128)S(1)}, f32[8,64,512]{2,1,0:T(8,128)}) fusion(f32[8,64,512]{2,1,0:T(8,128)S(1)} %get-tuple-element.10, f32[8,64,1]{2,1,0:T(8,128)S(1)} %get-tuple-element.28, f32[8,64,511]{2,1,0:T(8,128)S(1)} %get-tuple-element.30, f32[8,64,511]{2,1,0:T(8,128)S(1)} %get-tuple-element.29, f32[8,64,1]{2,1,0:T(8,128)S(1)} %get-tuple-element.27, ...), kind=kLoop, calls=%fused_computation.254 | loop fusion | flops 5210112 | bytes 6725632 | tf_op jit(solution)/shard_map/reduce_sum | solution.py:116
  38.4 1.1 reduce_sum.14
  40.7 0.5 broadcast.300
  41.3 0.8 reduce.7
  42.1 0.7 reshape.173
  42.8 3.5 %all-to-all-start = ((f32[8,1,128]{2,1,0:T(1,128)}), f32[8,1,128]{2,1,0:T(1,128)S(1)}, u32[]{:S(2)}, u32[]{:S(2)}) async-start(f32[8,1,128]{2,1,0:T(1,128)} %reshape.173), calls=%async_computation | async-start | bytes 8192 | tf_op jit(solution)/shard_map/all_to_all | solution.py:79
  46.4 6.2 %all-to-all-done = f32[8,1,128]{2,1,0:T(1,128)S(1)} async-done(((f32[8,1,128]{2,1,0:T(1,128)}), f32[8,1,128]{2,1,0:T(1,128)S(1)}, u32[]{:S(2)}, u32[]{:S(2)}) %all-to-all-start) | async-done | bytes 4128 | tf_op jit(solution)/shard_map/all_to_all | solution.py:79
  52.6 0.7 reduce.8
  54.8 0.7 copy.27
  55.5 6.6 %all-to-all-start.1 = ((f32[2,1,64,8]{3,1,0,2:T(1,128)}), f32[2,1,64,8]{3,1,0,2:T(1,128)S(1)}, u32[]{:S(2)}, u32[]{:S(2)}) async-start(f32[2,1,64,8]{3,1,0,2:T(1,128)} %copy.27), calls=%async_computation.1 | async-start | bytes 131072 | tf_op jit(solution)/shard_map/all_to_all | solution.py:85
  62.2 4.0 %all-to-all-done.1 = f32[2,1,64,8]{3,1,0,2:T(1,128)S(1)} async-done(((f32[2,1,64,8]{3,1,0,2:T(1,128)}), f32[2,1,64,8]{3,1,0,2:T(1,128)S(1)}, u32[]{:S(2)}, u32[]{:S(2)}) %all-to-all-start.1) | async-done | bytes 4128 | tf_op jit(solution)/shard_map/all_to_all | solution.py:85
  68.3 10.9 %all_to_all.48 = f32[2,32,2,8]{3,2,0,1:T(2,128)S(1)} all-to-all(f32[2,32,2,8]{3,2,0,1:T(2,128)S(1)} %copy.30), channel_id=1, replica_groups=mesh['gx'=32,'gy'=8] {'gx'}, dimensions={1} | all-to-all | bytes 8192 | tf_op jit(solution)/shard_map/all_to_all | solution.py:97
  80.5 0.8 reduce.9
  81.4 8.9 %all_to_all.49 = f32[8,1,128]{2,1,0:T(1,128)S(1)} all-to-all(f32[8,1,128]{2,1,0:T(1,128)S(1)} %reshape.175), channel_id=1, replica_groups=mesh['gx'=32,'gy'=8] {'gy'}, dimensions={0} | all-to-all | bytes 8192 | tf_op jit(solution)/shard_map/all_to_all | solution.py:101
  90.3 0.7 reduce.10
  92.2 1.2 div.54
  93.4 1.2 div.55
  94.6 4.8 %collective-permute-start.9 = (f32[1,64,512]{2,1,0:T(8,128)S(1)}, f32[1,64,512]{2,1,0:T(8,128)S(1)}, u32[]{:S(2)}, u32[]{:S(2)}) collective-permute-start(f32[1,64,512]{2,1,0:T(8,128)S(1)} %div.55), channel_id=1, source_target_pairs={{0,8},{8,16},{16,24},{24,32},{32,40},{40,48},{48,56},{56,64},{64,7... | collective-permute-start | bytes 393224 | tf_op jit(solution)/shard_map/ppermute | solution.py:19
  99.5 1.8 %collective-permute-done.9 = f32[1,64,512]{2,1,0:T(8,128)S(1)} collective-permute-done((f32[1,64,512]{2,1,0:T(8,128)S(1)}, f32[1,64,512]{2,1,0:T(8,128)S(1)}, u32[]{:S(2)}, u32[]{:S(2)}) %collective-permute-start.9) | collective-permute-done | bytes 131104 | tf_op jit(solution)/shard_map/ppermute | solution.py:19
  101.4 5.8 %collective-permute-done.8 = f32[1,64,512]{2,1,0:T(8,128)S(1)} collective-permute-done((f32[1,64,512]{2,1,0:T(8,128)S(1)}, f32[1,64,512]{2,1,0:T(8,128)S(1)}, u32[]{:S(2)}, u32[]{:S(2)}) %collective-permute-start.8) | collective-permute-done | bytes 131104 | tf_op jit(solution)/shard_map/ppermute | solution.py:22
  107.6 1.2 collective-permute-start.11
  109.0 1.0 collective-permute-done.10
  110.0 1.5 %collective-permute-done.11 = f32[10,1,512]{2,1,0:T(1,128)S(1)} collective-permute-done((f32[10,1,512]{2,1,0:T(1,128)S(1)}, f32[10,1,512]{2,1,0:T(1,128)S(1)}, u32[]{:S(2)}, u32[]{:S(2)}) %collective-permute-start.11) | collective-permute-done | bytes 20512 | tf_op jit(solution)/shard_map/ppermute | solution.py:19
  111.9 0.8 multiply_multiply_fusion
  112.8 1.7 %collective-permute-start.13 = (f32[1,64,512]{2,1,0:T(8,128)S(1)}, f32[1,64,512]{2,1,0:T(8,128)S(1)}, u32[]{:S(2)}, u32[]{:S(2)}) collective-permute-start(f32[1,64,512]{2,1,0:T(8,128)S(1)} %get-tuple-element.23), channel_id=1, source_target_pairs={{0,8},{8,16},{16,24},{24,32},{32,40},{40,48},{48,56},{56,64},{64,7... | collective-permute-start | bytes 393224 | tf_op jit(solution)/shard_map/ppermute | solution.py:19
  114.9 1.5 %collective-permute-done.13 = f32[1,64,512]{2,1,0:T(8,128)S(1)} collective-permute-done((f32[1,64,512]{2,1,0:T(8,128)S(1)}, f32[1,64,512]{2,1,0:T(8,128)S(1)}, u32[]{:S(2)}, u32[]{:S(2)}) %collective-permute-start.13) | collective-permute-done | bytes 131104 | tf_op jit(solution)/shard_map/ppermute | solution.py:19
  116.5 5.8 %collective-permute-done.12 = f32[1,64,512]{2,1,0:T(8,128)S(1)} collective-permute-done((f32[1,64,512]{2,1,0:T(8,128)S(1)}, f32[1,64,512]{2,1,0:T(8,128)S(1)}, u32[]{:S(2)}, u32[]{:S(2)}) %collective-permute-start.12) | collective-permute-done | bytes 131104 | tf_op jit(solution)/shard_map/ppermute | solution.py:22
  122.3 1.5 %collective-permute-start.15 = (f32[10,1,512]{2,1,0:T(1,128)S(1)}, f32[10,1,512]{2,1,0:T(1,128)S(1)}, u32[]{:S(2)}, u32[]{:S(2)}) collective-permute-start(f32[10,1,512]{2,1,0:T(1,128)S(1)} %get-tuple-element.12), channel_id=1, source_target_pairs={{0,1},{1,2},{2,3},{3,4},{4,5},{5,6},{6,7},{7,0},{8,9},{9,10},{10,1... | collective-permute-start | bytes 61448 | tf_op jit(solution)/shard_map/ppermute | solution.py:19
  123.9 1.0 collective-permute-done.14
  125.0 1.3 collective-permute-done.15
  126.3 4.2 %fusion.18 = f32[8,64,512]{2,1,0:T(8,128)} fusion(f32[10,1,512]{2,1,0:T(1,128)S(1)} %collective-permute-done.15, f32[1,64,512]{2,1,0:T(8,128)S(1)} %collective-permute-done.12, f32[8,64,512]{2,1,0:T(8,128)S(1)} %multiply_multiply_fusion, f32[1,64,512]{2,1,0:T(8,128)S(1)} %collective-permute-done.13, f32[10,1,512]{2,1,0:T(1,128)S(1)} %collective-permute-done.14, ...), kind=kLoop, calls=%fused_computation.30 | loop fusion | flops 12582912 | bytes 12271616 | tf_op jit(solution)/shard_map/add | solution.py:128
  (89 shorter events, 10.3 us)
Async XLA Ops:
  2.5 5.0 %collective-permute-start.1 = (f32[1,64,512]{2,1,0:T(8,128)}, f32[1,64,512]{2,1,0:T(8,128)S(1)}, u32[]{:S(2)}, u32[]{:S(2)}) collective-permute-start(f32[1,64,512]{2,1,0:T(8,128)} %get-tuple-element.31), channel_id=1, source_target_pairs={{0,8},{8,16},{16,24},{24,32},{32,40},{40,48},{48,56},{56,64},{64,7... | collective-permute-start | bytes 393224 | tf_op jit(solution)/shard_map/ppermute | solution.py:19
  4.6 8.0 %collective-permute-start = (f32[1,64,512]{2,1,0:T(8,128)}, f32[1,64,512]{2,1,0:T(8,128)}, u32[]{:S(2)}, u32[]{:S(2)}) collective-permute-start(f32[1,64,512]{2,1,0:T(8,128)} %get-tuple-element.32), channel_id=1, source_target_pairs={{8,0},{16,8},{24,16},{32,24},{40,32},{48,40},{56,48},{64,56},{72,6... | collective-permute-start | bytes 393224 | tf_op jit(solution)/shard_map/ppermute | solution.py:22
  5.4 15.8 %copy-start = (f32[8,64,512]{2,1,0:T(8,128)S(1)}, f32[8,64,512]{2,1,0:T(8,128)}, u32[]{:S(2)}) copy-start(f32[8,64,512]{2,1,0:T(8,128)} %param.3) | copy-start | bytes 3145732
  5.4 15.8 %copy-start.1 = (f32[8,64,512]{2,1,0:T(8,128)S(1)}, f32[8,64,512]{2,1,0:T(8,128)}, u32[]{:S(2)}) copy-start(f32[8,64,512]{2,1,0:T(8,128)} %param.2) | copy-start | bytes 3145732
  7.2 14.0 %copy-start.6 = (f32[8,64,511]{2,1,0:T(8,128)S(1)}, f32[8,64,511]{2,1,0:T(8,128)}, u32[]{:S(2)}) copy-start(f32[8,64,511]{2,1,0:T(8,128)} %get-tuple-element.35) | copy-start | bytes 3139588
  13.4 4.8 %collective-permute-start.2 = (f32[10,1,512]{2,1,0:T(1,128)S(1)}, f32[10,1,512]{2,1,0:T(1,128)S(1)}, u32[]{:S(2)}, u32[]{:S(2)}) collective-permute-start(f32[10,1,512]{2,1,0:T(1,128)S(1)} %get-tuple-element.17), channel_id=1, source_target_pairs={{1,0},{2,1},{3,2},{4,3},{5,4},{6,5},{7,6},{0,7},{9,8},{10,9},{11,1... | collective-permute-start | bytes 61448 | tf_op jit(solution)/shard_map/ppermute | solution.py:22
  17.4 3.8 %collective-permute-start.3 = (f32[10,1,512]{2,1,0:T(1,128)S(1)}, f32[10,1,512]{2,1,0:T(1,128)S(1)}, u32[]{:S(2)}, u32[]{:S(2)}) collective-permute-start(f32[10,1,512]{2,1,0:T(1,128)S(1)} %get-tuple-element.18), channel_id=1, source_target_pairs={{0,1},{1,2},{2,3},{3,4},{4,5},{5,6},{6,7},{7,0},{8,9},{9,10},{10,1... | collective-permute-start | bytes 61448 | tf_op jit(solution)/shard_map/ppermute | solution.py:19
  23.3 13.2 %copy-start.3 = (f32[8,64,512]{2,1,0:T(8,128)}, f32[8,64,512]{2,1,0:T(8,128)S(1)}, u32[]{:S(2)}) copy-start(f32[8,64,512]{2,1,0:T(8,128)S(1)} %get-tuple-element.10) | copy-start | bytes 3145732
  23.4 3.4 %collective-permute-start.5 = (f32[1,64,512]{2,1,0:T(8,128)S(1)}, f32[1,64,512]{2,1,0:T(8,128)S(1)}, u32[]{:S(2)}, u32[]{:S(2)}) collective-permute-start(f32[1,64,512]{2,1,0:T(8,128)S(1)} %get-tuple-element.25), channel_id=1, source_target_pairs={{0,8},{8,16},{16,24},{24,32},{32,40},{40,48},{48,56},{56,64},{64,7... | collective-permute-start | bytes 393224 | tf_op jit(solution)/shard_map/ppermute | solution.py:19
  24.8 7.7 %collective-permute-start.4 = (f32[1,64,512]{2,1,0:T(8,128)S(1)}, f32[1,64,512]{2,1,0:T(8,128)S(1)}, u32[]{:S(2)}, u32[]{:S(2)}) collective-permute-start(f32[1,64,512]{2,1,0:T(8,128)S(1)} %get-tuple-element.26), channel_id=1, source_target_pairs={{8,0},{16,8},{24,16},{32,24},{40,32},{48,40},{56,48},{64,56},{72,6... | collective-permute-start | bytes 393224 | tf_op jit(solution)/shard_map/ppermute | solution.py:22
  32.6 2.7 %collective-permute-start.6 = (f32[10,1,512]{2,1,0:T(1,128)S(1)}, f32[10,1,512]{2,1,0:T(1,128)S(1)}, u32[]{:S(2)}, u32[]{:S(2)}) collective-permute-start(f32[10,1,512]{2,1,0:T(1,128)S(1)} %get-tuple-element.15), channel_id=1, source_target_pairs={{1,0},{2,1},{3,2},{4,3},{5,4},{6,5},{7,6},{0,7},{9,8},{10,9},{11,1... | collective-permute-start | bytes 61448 | tf_op jit(solution)/shard_map/ppermute | solution.py:22
  32.7 3.9 %collective-permute-start.7 = (f32[10,1,512]{2,1,0:T(1,128)S(1)}, f32[10,1,512]{2,1,0:T(1,128)S(1)}, u32[]{:S(2)}, u32[]{:S(2)}) collective-permute-start(f32[10,1,512]{2,1,0:T(1,128)S(1)} %get-tuple-element.16), channel_id=1, source_target_pairs={{0,1},{1,2},{2,3},{3,4},{4,5},{5,6},{6,7},{7,0},{8,9},{9,10},{10,1... | collective-permute-start | bytes 61448 | tf_op jit(solution)/shard_map/ppermute | solution.py:19
  42.8 9.8 %all-to-all-start = ((f32[8,1,128]{2,1,0:T(1,128)}), f32[8,1,128]{2,1,0:T(1,128)S(1)}, u32[]{:S(2)}, u32[]{:S(2)}) async-start(f32[8,1,128]{2,1,0:T(1,128)} %reshape.173), calls=%async_computation | async-start | bytes 8192 | tf_op jit(solution)/shard_map/all_to_all | solution.py:79
  55.5 10.7 %all-to-all-start.1 = ((f32[2,1,64,8]{3,1,0,2:T(1,128)}), f32[2,1,64,8]{3,1,0,2:T(1,128)S(1)}, u32[]{:S(2)}, u32[]{:S(2)}) async-start(f32[2,1,64,8]{3,1,0,2:T(1,128)} %copy.27), calls=%async_computation.1 | async-start | bytes 131072 | tf_op jit(solution)/shard_map/all_to_all | solution.py:85
  94.6 6.7 %collective-permute-start.9 = (f32[1,64,512]{2,1,0:T(8,128)S(1)}, f32[1,64,512]{2,1,0:T(8,128)S(1)}, u32[]{:S(2)}, u32[]{:S(2)}) collective-permute-start(f32[1,64,512]{2,1,0:T(8,128)S(1)} %div.55), channel_id=1, source_target_pairs={{0,8},{8,16},{16,24},{24,32},{32,40},{40,48},{48,56},{56,64},{64,7... | collective-permute-start | bytes 393224 | tf_op jit(solution)/shard_map/ppermute | solution.py:19
  99.4 7.7 %collective-permute-start.8 = (f32[1,64,512]{2,1,0:T(8,128)S(1)}, f32[1,64,512]{2,1,0:T(8,128)S(1)}, u32[]{:S(2)}, u32[]{:S(2)}) collective-permute-start(f32[1,64,512]{2,1,0:T(8,128)S(1)} %div.55), channel_id=1, source_target_pairs={{8,0},{16,8},{24,16},{32,24},{40,32},{48,40},{56,48},{64,56},{72,6... | collective-permute-start | bytes 393224 | tf_op jit(solution)/shard_map/ppermute | solution.py:22
  107.2 4.7 %copy-start.5 = (f32[8,64,512]{2,1,0:T(8,128)S(1)}, f32[8,64,512]{2,1,0:T(8,128)}, u32[]{:S(2)}) copy-start(f32[8,64,512]{2,1,0:T(8,128)} %get-tuple-element.8) | copy-start | bytes 3145732
  107.3 2.7 %collective-permute-start.10 = (f32[10,1,512]{2,1,0:T(1,128)S(1)}, f32[10,1,512]{2,1,0:T(1,128)S(1)}, u32[]{:S(2)}, u32[]{:S(2)}) collective-permute-start(f32[10,1,512]{2,1,0:T(1,128)S(1)} %get-tuple-element.13), channel_id=1, source_target_pairs={{1,0},{2,1},{3,2},{4,3},{5,4},{6,5},{7,6},{0,7},{9,8},{10,9},{11,1... | collective-permute-start | bytes 61448 | tf_op jit(solution)/shard_map/ppermute | solution.py:22
  107.6 3.8 %collective-permute-start.11 = (f32[10,1,512]{2,1,0:T(1,128)S(1)}, f32[10,1,512]{2,1,0:T(1,128)S(1)}, u32[]{:S(2)}, u32[]{:S(2)}) collective-permute-start(f32[10,1,512]{2,1,0:T(1,128)S(1)} %get-tuple-element.14), channel_id=1, source_target_pairs={{0,1},{1,2},{2,3},{3,4},{4,5},{5,6},{6,7},{7,0},{8,9},{9,10},{10,1... | collective-permute-start | bytes 61448 | tf_op jit(solution)/shard_map/ppermute | solution.py:19
  112.8 3.7 %collective-permute-start.13 = (f32[1,64,512]{2,1,0:T(8,128)S(1)}, f32[1,64,512]{2,1,0:T(8,128)S(1)}, u32[]{:S(2)}, u32[]{:S(2)}) collective-permute-start(f32[1,64,512]{2,1,0:T(8,128)S(1)} %get-tuple-element.23), channel_id=1, source_target_pairs={{0,8},{8,16},{16,24},{24,32},{32,40},{40,48},{48,56},{56,64},{64,7... | collective-permute-start | bytes 393224 | tf_op jit(solution)/shard_map/ppermute | solution.py:19
  114.5 7.7 %collective-permute-start.12 = (f32[1,64,512]{2,1,0:T(8,128)S(1)}, f32[1,64,512]{2,1,0:T(8,128)S(1)}, u32[]{:S(2)}, u32[]{:S(2)}) collective-permute-start(f32[1,64,512]{2,1,0:T(8,128)S(1)} %get-tuple-element.24), channel_id=1, source_target_pairs={{8,0},{16,8},{24,16},{32,24},{40,32},{48,40},{56,48},{64,56},{72,6... | collective-permute-start | bytes 393224 | tf_op jit(solution)/shard_map/ppermute | solution.py:22
  114.9 11.4 %copy-start.2 = (f32[8,64,512]{2,1,0:T(8,128)S(1)}, f32[8,64,512]{2,1,0:T(8,128)}, u32[]{:S(2)}) copy-start(f32[8,64,512]{2,1,0:T(8,128)} %param.2) | copy-start | bytes 3145732
  114.9 11.4 %copy-start.4 = (f32[8,64,512]{2,1,0:T(8,128)S(1)}, f32[8,64,512]{2,1,0:T(8,128)}, u32[]{:S(2)}) copy-start(f32[8,64,512]{2,1,0:T(8,128)} %copy-done.3) | copy-start | bytes 3145732
  122.3 2.7 %collective-permute-start.14 = (f32[10,1,512]{2,1,0:T(1,128)S(1)}, f32[10,1,512]{2,1,0:T(1,128)S(1)}, u32[]{:S(2)}, u32[]{:S(2)}) collective-permute-start(f32[10,1,512]{2,1,0:T(1,128)S(1)} %get-tuple-element.11), channel_id=1, source_target_pairs={{1,0},{2,1},{3,2},{4,3},{5,4},{6,5},{7,6},{0,7},{9,8},{10,9},{11,1... | collective-permute-start | bytes 61448 | tf_op jit(solution)/shard_map/ppermute | solution.py:22
  122.3 3.9 %collective-permute-start.15 = (f32[10,1,512]{2,1,0:T(1,128)S(1)}, f32[10,1,512]{2,1,0:T(1,128)S(1)}, u32[]{:S(2)}, u32[]{:S(2)}) collective-permute-start(f32[10,1,512]{2,1,0:T(1,128)S(1)} %get-tuple-element.12), channel_id=1, source_target_pairs={{0,1},{1,2},{2,3},{3,4},{4,5},{5,6},{6,7},{7,0},{8,9},{9,10},{10,1... | collective-permute-start | bytes 61448 | tf_op jit(solution)/shard_map/ppermute | solution.py:19
where the time goes:
time: 131 us; the launch traced here: 130 us
  waiting for transfers between devices  48.6 us (37%)
  starting transfers between devices  28.8 us (22%)
  blocking collectives  19.8 us (15%)
  other arithmetic  15 us (11%)
  local copies, waits for them, and re-layouts  12.3 us (9%)
  matrix products  5.72 us (4%)
    ppermute x8, waiting for transfers between devices, padded_2(): lax.ppermute(lax.slice_in_dim(block, 0, width, axis=dim), axis, backward)  26.4 us
    ppermute x8, starting transfers between devices, padded_2(): lax.ppermute(lax.slice_in_dim(block, block.shape[dim] - width, None, axis...  14.2 us
    ppermute x8, waiting for transfers between devices, padded_2(): lax.ppermute(lax.slice_in_dim(block, block.shape[dim] - width, None, axis...  12 us
    all_to_all x1, blocking collectives, pencil_solve(): lax.all_to_all(jnp.stack([real_part, imag_part]), 'gx', split_axis=1, con...  10.9 us
    all_to_all x1, blocking collectives, pencil_solve(): lax.all_to_all(jnp.stack([real_part, imag_part]), 'gy', split_axis=2, con...  8.89 us
    all_to_all x1, starting transfers between devices, pencil_solve(): lax.all_to_all(jnp.stack([real_part, imag_part]), 'gx', split_axis=2, con...  6.61 us
    all_to_all x1, waiting for transfers between devices, pencil_solve(): lax.all_to_all(jnp.stack([real_part, imag_part]), 'gy', split_axis=3, con...  6.19 us
    dot_general x22, matrix products, contract(): result = jnp.dot(moved, matrix, precision=lax.Precision.HIGHEST)  5.72 us
  transfers between devices with their start and end apart: 18, of which 17 were waited for; matrix products, arithmetic and copies ran while one was open for 3% of the time, Pallas kernels for 0%

commit v1 on v0

v1 whole, which is shorter than its diff:
```python
import functools
import math

import jax
import jax.numpy as jnp
import numpy as np
from jax import lax
from jax.experimental import pallas as pl
from jax.experimental.pallas import tpu as pltpu
from jax.sharding import Mesh
from jax.sharding import PartitionSpec as P

screen = 0.02
w1 = 1.0 / (1.25 + 0.75 * math.cos(math.pi / 4.0))
w2 = 1.0 / (1.25 - 0.75 * math.cos(math.pi / 4.0))

BX, BY, NZ = 8, 64, 512
CX, CY, CZ = 32, 64, 64
GX, GY = 32, 8
CHIPS = GX // 2
ROWS = CY // 2
OUT_Y = BY // 8 + 2
OUT_X = 4

VMEM = pl.BlockSpec(memory_space=pltpu.VMEM)
SMEM = pl.BlockSpec(memory_space=pltpu.SMEM)
F32 = jnp.float32


def basis():
    place = np.arange(CZ)
    columns, freq = [], []
    for k in range(CZ // 2 + 1):
        scale = math.sqrt((1.0 if k in (0, CZ // 2) else 2.0) / CZ)
        columns.append(scale * np.cos(2.0 * math.pi * k * place / CZ))
        freq.append(k)
    for k in range(1, CZ // 2):
        columns.append(math.sqrt(2.0 / CZ) * np.sin(2.0 * math.pi * k * place / CZ))
        freq.append(k)
    return np.stack(columns, 1), np.array(freq)


def symbol(length):
    return 2.0 - 2.0 * np.cos(2.0 * math.pi * np.arange(length) / length)


def tables():
    columns, freq = basis()
    spectrum = (
        screen
        + symbol(CX)[:, None, None]
        + symbol(CY)[None, :, None]
        + symbol(CZ)[freq][None, None, :]
    )
    green = np.real(np.fft.ifft2(1.0 / spectrum, axes=(0, 1)))
    d, r, h = np.meshgrid(np.arange(GY), np.arange(4), np.arange(2), indexing="ij")
    slabs = []
    for j in range(-1, OUT_Y - 1):
        shift = (j - (8 * d + 4 * h + r)) % CY
        slabs.append(green[: CX // 2 + 1][:, shift].reshape(CX // 2 + 1, ROWS, 2 * CZ))
    table = np.stack(slabs, 1).astype(np.float32)
    into = np.repeat(columns, NZ // CZ, axis=0).astype(np.float32)
    out = np.concatenate([into.T, into.T], 0) / 8.0
    return table, into, out.astype(np.float32)


def zsum(v):
    return pltpu.roll(v, 1, 1) + pltpu.roll(v, NZ - 1, 1)


def shifted_sum(v, low, high):
    size = v.shape[0]
    row = lax.broadcasted_iota(jnp.int32, v.shape, 0)
    before = jnp.where(row == 0, low, pltpu.roll(v, 1, 0))
    after = jnp.where(row == size - 1, high, pltpu.roll(v, size - 1, 0))
    return before + after


def pack_kernel(core_ref, cot_ref, coef_ref, near_ref, far_ref, tnear_ref, tfar_ref, ylow_ref, yhigh_ref):
    core = core_ref[0]
    edges = (
        (near_ref, tnear_ref, (BX - 1) * (1 - core), 2 * core - 1),
        (far_ref, tfar_ref, (BX - 1) * core, 1 - 2 * core),
    )
    for out, tiny, edge, step in edges:
        cot = cot_ref[edge]
        inverse = 1.0 / (6.0 + coef_ref[edge])
        w5 = w2 * cot * inverse
        tiny[0:1, :] = w5[0:1, :]
        tiny[1:2, :] = w5[BY - 1 : BY, :]
        out[0] = w5
        out[1] = inverse
        out[2] = (1.0 - w2) * cot + w2 * cot_ref[edge + step] / (6.0 + coef_ref[edge + step])
    for out, edge, inner in ((ylow_ref, 0, 1), (yhigh_ref, BY - 1, BY - 2)):
        cot = cot_ref[:, edge, :]
        inverse = 1.0 / (6.0 + coef_ref[:, edge, :])
        out[0:8, :] = w2 * cot * inverse
        out[8:16, :] = inverse
        out[16:24, :] = (1.0 - w2) * cot + w2 * cot_ref[:, inner, :] / (6.0 + coef_ref[:, inner, :])


def first_kernel(
    core_ref, cot_ref, coef_ref, near_ref, far_ref, ylow_ref, yhigh_ref, into_ref,
    c3_ref, base_ref, inverse_ref, cnear_ref, cfar_ref, cylow_ref, cyhigh_ref, send_ref,
    w5_ref, w4_ref,
):
    core = core_ref[0]
    halos = ((near_ref, (BX + 1) * (1 - core), core == 0), (far_ref, (BX + 1) * core, core == 1))
    for x in range(BX):
        inverse = 1.0 / (6.0 + coef_ref[x])
        inverse_ref[x] = inverse
        w5_ref[x + 1] = w2 * cot_ref[x] * inverse
    for halo, place, _ in halos:
        w5_ref[place] = halo[0]
    y4 = []
    for packet, edge in ((ylow_ref, 0), (yhigh_ref, BY - 1)):
        w5 = packet[0:8, :]
        c4 = packet[16:24, :] + w5_ref[1 : BX + 1, edge, :] + zsum(w5)
        c4 = c4 + shifted_sum(w5, packet[24:25, :], packet[25:26, :])
        y4.append(w1 * packet[8:16, :] * c4)
    for halo, place, at_high in halos:
        inner = jnp.where(at_high, BX, 1)
        low = jnp.where(at_high, ylow_ref[25:26, :], ylow_ref[24:25, :])
        high = jnp.where(at_high, yhigh_ref[25:26, :], yhigh_ref[24:25, :])
        w5 = halo[0]
        c4 = halo[2] + w5_ref[inner] + zsum(w5) + shifted_sum(w5, low, high)
        w4_ref[place] = w1 * halo[1] * c4
    for x in range(BX):
        w5 = w5_ref[x + 1]
        c4 = (1.0 - w2) * cot_ref[x] + w5_ref[x] + w5_ref[x + 2] + zsum(w5)
        c4 = c4 + shifted_sum(w5, ylow_ref[x : x + 1, :], yhigh_ref[x : x + 1, :])
        w4 = w1 * inverse_ref[x] * c4
        w4_ref[x + 1] = w4
        base_ref[x] = w5 + w4
        c3_ref[x] = c4
    total = jnp.zeros((BY, NZ), F32)
    for x in range(BX):
        w4 = w4_ref[x + 1]
        c3 = (1.0 - w1) * c3_ref[x] + w4_ref[x] + w4_ref[x + 2] + zsum(w4)
        c3 = c3 + shifted_sum(w4, y4[0][x : x + 1, :], y4[1][x : x + 1, :])
        c3_ref[x] = c3
        cylow_ref[x : x + 1, :] = c3[0:1, :]
        cyhigh_ref[x : x + 1, :] = c3[BY - 1 : BY, :]
        total = total + c3
    sums = jnp.sum(total.reshape(BY // 8, 8, NZ), axis=1)
    modes = jnp.dot(sums, into_ref[...], precision=lax.Precision.HIGHEST, preferred_element_type=F32)
    packed = jnp.concatenate([modes[0:4, :], modes[4:8, :]], axis=1)
    send_ref[...] = jnp.broadcast_to(packed[None], send_ref.shape)
    cnear_ref[...] = c3_ref[(BX - 1) * (1 - core)]
    cfar_ref[...] = c3_ref[(BX - 1) * core]


def coarse_kernel(place_ref, got_ref, table_ref, own_ref, other_ref, rolled_ref):
    core, chip, gy = place_ref[0], place_ref[1], place_ref[2]
    turn = lax.rem(ROWS - 4 * gy, ROWS)
    for q in range(CHIPS):
        plane = lax.rem(chip + (1 - 2 * core) * q + CHIPS, CHIPS)
        rolled_ref[q] = pltpu.roll(got_ref[plane], turn, 0)

    def step(q, totals):
        totals = list(totals)
        for m in range(-1, OUT_X - 1):
            away = lax.rem(2 * CX - 2 * q + m, CX)
            away = jnp.minimum(away, CX - away)
            for j in range(OUT_Y):
                at = (m + 1) * OUT_Y + j
                for part in range(ROWS // 8):
                    rows = slice(8 * part, 8 * part + 8)
                    totals[at] = totals[at] + table_ref[away, j, rows, :] * rolled_ref[q, rows, :]
        return tuple(totals)

    zero = jnp.zeros((8, 2 * CZ), F32)
    totals = lax.fori_loop(0, CHIPS, step, (zero,) * (OUT_X * OUT_Y))
    for m in range(3):
        for j in range(OUT_Y):
            at = m * OUT_Y + j
            own_ref[at : at + 1, :] = jnp.sum(totals[at], axis=0, keepdims=True)
            at_other = (OUT_X - 1 - m) * OUT_Y + j
            other_ref[at : at + 1, :] = jnp.sum(totals[at_other], axis=0, keepdims=True)


def last_kernel(
    core_ref, own_ref, other_ref, out_table_ref, c3_ref, base_ref, inverse_ref,
    cnear_ref, cfar_ref, near_ref, far_ref, cylow_ref, cyhigh_ref, ylow_ref, yhigh_ref,
    out_ref, w_ref,
):
    core = core_ref[0]
    modes = own_ref[...] + other_ref[...]
    coarse = jnp.dot(modes, out_table_ref[...], precision=lax.Precision.HIGHEST, preferred_element_type=F32)
    outer, middle, inner = (coarse[m * OUT_Y : (m + 1) * OUT_Y, :] for m in range(3))
    low = jnp.where(core == 0, outer, inner)
    high = jnp.where(core == 0, inner, outer)

    def rows_of(plane):
        return jnp.concatenate([jnp.broadcast_to(plane[j : j + 1, :], (8, NZ)) for j in range(1, OUT_Y - 1)], 0)

    def side_sum(plane, fine):
        return shifted_sum(fine, plane[0:1, :], plane[OUT_Y - 1 : OUT_Y, :]) + zsum(fine)

    s, s_low, s_high = rows_of(middle), rows_of(low), rows_of(high)
    beside = side_sum(middle, s)
    for fine, plane, is_low in ((s_low, low, True), (s_high, high, False)):
        c3 = jnp.where((core == 0) == is_low, cfar_ref[...], cnear_ref[...])
        inverse = jnp.where((core == 0) == is_low, far_ref[1], near_ref[1])
        value = c3 + fine + s + side_sum(plane, fine)
        w_ref[0 if is_low else BX + 1] = w2 * (inverse * value - fine)
    y_w = []
    for c3_rows, packet, edge, near_edge in (
        (cylow_ref, ylow_ref, 0, 1),
        (cyhigh_ref, yhigh_ref, OUT_Y - 1, OUT_Y - 2),
    ):
        fine = jnp.broadcast_to(middle[edge : edge + 1, :], (BX, NZ))
        value = c3_rows[...] + fine + middle[near_edge : near_edge + 1, :] + zsum(fine)
        value = value + shifted_sum(fine, low[edge : edge + 1, :], high[edge : edge + 1, :])
        y_w.append(w2 * (packet[8:16, :] * value - fine))
    for x in range(BX):
        around = beside + (s_low if x == 0 else s) + (s_high if x == BX - 1 else s)
        w_ref[x + 1] = w2 * (inverse_ref[x] * (c3_ref[x] + around) - s)
    for x in range(BX):
        w = w_ref[x + 1]
        inverse = inverse_ref[x]
        near = w_ref[x] + w_ref[x + 2] + zsum(w)
        near = near + shifted_sum(w, y_w[0][x : x + 1, :], y_w[1][x : x + 1, :])
        out_ref[x] = base_ref[x] + s + w + w1 * ((1.0 - w2) / w2 * w + inverse * near)


def call(kernel, outs, ins, scratch=(), smem=1):
    return pl.pallas_call(
        kernel,
        out_shape=[jax.ShapeDtypeStruct(shape, F32) for shape in outs],
        in_specs=[SMEM] * smem + [VMEM] * (len(ins) - smem),
        out_specs=[VMEM] * len(outs),
        scratch_shapes=[pltpu.VMEM(shape, F32) for shape in scratch],
        compiler_params=pltpu.CompilerParams(vmem_limit_bytes=40 * 1024 * 1024),
    )(*ins)


def body(cotangent, coefficient):
    table, into, out_table = tables()
    along_x = ("x", "y", "core")
    core = lax.axis_index("core")
    place = jnp.stack([core, lax.axis_index("x") * 4 + lax.axis_index("y"), lax.axis_index("gy")])
    place = place.astype(jnp.int32)
    near_pairs = [(i, i ^ 1) for i in range(GX)]
    far_pairs = [(i, (i + 1) % GX if i % 2 else (i - 1) % GX) for i in range(GX)]
    up = [(i, (i + 1) % GY) for i in range(GY)]
    down = [(i, (i - 1) % GY) for i in range(GY)]

    def near_swap(v):
        return lax.ppermute(v, along_x, near_pairs)

    def far_swap(v):
        return lax.ppermute(v, along_x, far_pairs)

    plane, rows = (BY, NZ), (BX, NZ)
    near, far, tiny_near, tiny_far, y_low, y_high = call(
        pack_kernel,
        [(3,) + plane, (3,) + plane, (2, NZ), (2, NZ), (24, NZ), (24, NZ)],
        [place, cotangent, coefficient],
    )
    tiny_near, tiny_far = near_swap(tiny_near), far_swap(tiny_far)
    near, far = near_swap(near), far_swap(far)
    corner_low = jnp.where(core == 0, tiny_far, tiny_near)
    corner_high = jnp.where(core == 0, tiny_near, tiny_far)
    y_low = jnp.concatenate([y_low, corner_low[0:1], corner_high[0:1]], 0)
    y_high = jnp.concatenate([y_high, corner_low[1:2], corner_high[1:2]], 0)
    from_low = lax.ppermute(y_high, "gy", up)
    from_high = lax.ppermute(y_low, "gy", down)
    brick = (BX, BY, NZ)
    c3, base, inverse, c_near, c_far, cy_low, cy_high, send = call(
        first_kernel,
        [brick, brick, brick, plane, plane, rows, rows, (CHIPS * GY, 4, 2 * CZ)],
        [place, cotangent, coefficient, near, far, from_low, from_high, jnp.asarray(into)],
        scratch=[(BX + 2,) + plane, (BX + 2,) + plane],
    )
    got = lax.all_to_all(send, ("x", "y", "gy"), 0, 0, tiled=True)
    c_near, c_far = near_swap(c_near), far_swap(c_far)
    c_from_low = lax.ppermute(cy_high, "gy", up)
    c_from_high = lax.ppermute(cy_low, "gy", down)
    own, other = call(
        coarse_kernel,
        [(3 * OUT_Y, 2 * CZ), (3 * OUT_Y, 2 * CZ)],
        [place, got.reshape(CHIPS, ROWS, 2 * CZ), jnp.asarray(table)],
        scratch=[(CHIPS, ROWS, 2 * CZ)],
    )
    other = near_swap(other)
    return call(
        last_kernel,
        [brick],
        [
            place, own, other, jnp.asarray(out_table), c3, base, inverse,
            c_near, c_far, near, far, c_from_low, c_from_high, from_low, from_high,
        ],
        scratch=[(BX + 2,) + plane],
    )[0]


def solution(mesh):
    split = Mesh(np.asarray(mesh.devices).reshape(4, 4, 2, GY), ("x", "y", "core", "gy"))
    spec = P(("x", "y", "core"), "gy", None)
    return jax.shard_map(body, mesh=split, in_specs=(spec, spec), out_specs=spec, check_vma=False)
```

time: 131 us -> 65.3 us (0.50)
  the two profiles are of different devices: /device:TPU:31 before, /device:TPU:1 now
where the time goes in v1:
time: 65.3 us; the launch traced here: 65 us
  starting transfers between devices  31 us (47%)
  waiting for transfers between devices  13.6 us (21%)
  local copies, waits for them, and re-layouts  10.6 us (16%)
  Pallas kernels  9.63 us (15%)
    all_to_all x1, starting transfers between devices, body(): got = lax.all_to_all(send, ('x', 'y', 'gy'), 0, 0, tiled=True)  12.9 us
    unnamed x30, local copies, waits for them, and re-layouts  10.5 us
    all_to_all x1, waiting for transfers between devices, body(): got = lax.all_to_all(send, ('x', 'y', 'gy'), 0, 0, tiled=True)  10.1 us
    pallas_call x4, Pallas kernels, call(): pl.pallas_call(kernel, out_shape=[jax.ShapeDtypeStruct(shape, F32) for sh...  9.63 us
    ppermute x4, starting transfers between devices, near_swap(): return lax.ppermute(v, along_x, near_pairs)  6.11 us
    ppermute x1, starting transfers between devices, body(): from_high = lax.ppermute(y_low, 'gy', down)  4.03 us
    ppermute x3, starting transfers between devices, far_swap(): return lax.ppermute(v, along_x, far_pairs)  3.53 us
    ppermute x1, waiting for transfers between devices, body(): from_low = lax.ppermute(y_high, 'gy', up)  1.83 us
  transfers between devices with their start and end apart: 12, of which 4 were waited for; matrix products, arithmetic and copies ran while one was open for 0% of the time, Pallas kernels for 2%

profile of v1, /device:TPU:1, one launch (start us, length us, event | category | flops | bytes accessed | tf_op | source)
XLA Modules:
  0.0 65.0 jit_solution(6124918407517195126)
XLA Ops:
  0.0 0.1 pad_add_fusion.core_ref.place_ref
  0.1 1.2 %copy-done = f32[8,64,512]{2,1,0:T(8,128)S(1)} copy-done((f32[8,64,512]{2,1,0:T(8,128)S(1)}, f32[8,64,512]{2,1,0:T(8,128)}, u32[]{:S(2)}) %copy-start) | copy-done | bytes 1048600
  1.3 0.0 copy-start.2
  1.3 1.2 %copy-done.2 = f32[8,64,512]{2,1,0:T(8,128)S(1)} copy-done((f32[8,64,512]{2,1,0:T(8,128)S(1)}, f32[8,64,512]{2,1,0:T(8,128)}, u32[]{:S(2)}) %copy-start.2) | copy-done | bytes 1048600
  2.5 0.0 copy-start.1
  2.5 1.5 %shard_map.55 = (f32[3,64,512]{2,1,0:T(8,128)}, f32[3,64,512]{2,1,0:T(8,128)}, f32[2,512]{1,0:T(2,128)S(1)}, f32[2,512]{1,0:T(2,128)S(1)}, f32[24,512]{1,0:T(8,128)S(1)}, /*index=5*/f32[24,512]{1,0:T(8,128)S(1)}) custom-call(s32[3]{0:T(128)S(1)} %pad_add_fusion.core_ref.place_ref, f32[8,64,512]{2,1,0:T(8,128)S(1)} %copy-done, f32[8,64,512]{2,1,0:T(8,128)S(1)} %copy-done.2), custom_call_target="tpu_custom_call" | custom-call | tf_op jit(solution)/shard_map/pallas_call | solution.py:228
  4.0 2.7 %collective-permute-start.2 = (f32[2,512]{1,0:T(2,128)S(1)}, f32[2,512]{1,0:T(2,128)S(1)}, u32[]{:S(2)}, u32[]{:S(2)}) collective-permute-start(f32[2,512]{1,0:T(2,128)S(1)} %get-tuple-element.24), channel_id=1, source_target_pairs={{0,248},{8,16},{16,8},{24,32},{32,24},{40,48},{48,40},{56,64},{64,... | collective-permute-start | bytes 12296 | tf_op jit(solution)/shard_map/ppermute | solution.py:253
  6.7 3.5 %collective-permute-start.3 = (f32[2,512]{1,0:T(2,128)S(1)}, f32[2,512]{1,0:T(2,128)S(1)}, u32[]{:S(2)}, u32[]{:S(2)}) collective-permute-start(f32[2,512]{1,0:T(2,128)S(1)} %get-tuple-element.25), channel_id=1, source_target_pairs={{0,8},{8,0},{16,24},{24,16},{32,40},{40,32},{48,56},{56,48},{64,72... | collective-permute-start | bytes 12296 | tf_op jit(solution)/shard_map/ppermute | solution.py:250
  10.2 0.0 collective-permute-start
  10.2 0.0 collective-permute-start.1
  10.2 0.0 collective-permute-done.2
  10.2 0.8 %collective-permute-done.3 = f32[2,512]{1,0:T(2,128)S(1)} collective-permute-done((f32[2,512]{1,0:T(2,128)S(1)}, f32[2,512]{1,0:T(2,128)S(1)}, u32[]{:S(2)}, u32[]{:S(2)}) %collective-permute-start.3) | collective-permute-done | bytes 4128 | tf_op jit(solution)/shard_map/ppermute | solution.py:250
  11.0 1.7 %collective-permute-start.4 = (f32[26,512]{1,0:T(8,128)S(1)}, f32[26,512]{1,0:T(8,128)S(1)}, u32[]{:S(2)}, u32[]{:S(2)}) collective-permute-start(f32[26,512]{1,0:T(8,128)S(1)} %pad_maximum_fusion), channel_id=1, source_target_pairs={{0,1},{1,2},{2,3},{3,4},{4,5},{5,6},{6,7},{7,0},{8,9},{9,10},{10,1... | collective-permute-start | bytes 159752 | tf_op jit(solution)/shard_map/ppermute | solution.py:267
  12.8 0.0 copy-start.11
  12.8 4.0 %collective-permute-start.5 = (f32[26,512]{1,0:T(8,128)S(1)}, f32[26,512]{1,0:T(8,128)S(1)}, u32[]{:S(2)}, u32[]{:S(2)}) collective-permute-start(f32[26,512]{1,0:T(8,128)S(1)} %pad_maximum_fusion.1), channel_id=1, source_target_pairs={{0,7},{1,0},{2,1},{3,2},{4,3},{5,4},{6,5},{7,6},{8,15},{9,8},{10,9... | collective-permute-start | bytes 159752 | tf_op jit(solution)/shard_map/ppermute | solution.py:268
  16.8 1.8 %collective-permute-done.4.ylow_ref = f32[26,512]{1,0:T(8,128)S(1)} collective-permute-done((f32[26,512]{1,0:T(8,128)S(1)}, f32[26,512]{1,0:T(8,128)S(1)}, u32[]{:S(2)}, u32[]{:S(2)}) %collective-permute-start.4) | collective-permute-done | bytes 53280 | tf_op jit(solution)/shard_map/ppermute | solution.py:267
  18.7 0.0 collective-permute-done.5.yhigh_ref
  18.7 0.0 collective-permute-done.near_ref
  18.7 0.0 collective-permute-done.1.far_ref
  18.7 0.0 copy-done.1
  18.7 0.0 copy-done.3
  18.7 0.0 copy-start.12
  18.7 0.9 %copy-done.12 = f32[512,64]{1,0:T(8,128)S(1)} copy-done((f32[512,64]{1,0:T(8,128)S(1)}, f32[512,64]{1,0:T(8,128)}, u32[]{:S(2)}) %copy-start.12) | copy-done | bytes 131096
  19.6 3.6 %shard_map.56 = (f32[8,64,512]{2,1,0:T(8,128)S(1)}, f32[8,64,512]{2,1,0:T(8,128)S(1)}, f32[8,64,512]{2,1,0:T(8,128)S(1)}, f32[64,512]{1,0:T(8,128)S(1)}, f32[64,...) custom-call(s32[3]{0:T(128)S(1)} %pad_add_fusion.core_ref.place_ref, ...), custom_call_target="tpu_custom_call" | custom-call | tf_op jit(solution)/shard_map/pallas_call | solution.py:228
  23.2 1.0 %copy-done.5 = f32[8,64,512]{2,1,0:T(8,128)} copy-done((f32[8,64,512]{2,1,0:T(8,128)}, f32[8,64,512]{2,1,0:T(8,128)S(1)}, u32[]{:S(2)}) %copy-start.5) | copy-done | bytes 1048600
  24.2 1.0 %copy-done.7 = f32[8,64,512]{2,1,0:T(8,128)} copy-done((f32[8,64,512]{2,1,0:T(8,128)}, f32[8,64,512]{2,1,0:T(8,128)S(1)}, u32[]{:S(2)}) %copy-start.7) | copy-done | bytes 1048600
  25.2 1.0 %copy-done.9 = f32[8,64,512]{2,1,0:T(8,128)} copy-done((f32[8,64,512]{2,1,0:T(8,128)}, f32[8,64,512]{2,1,0:T(8,128)S(1)}, u32[]{:S(2)}) %copy-start.9) | copy-done | bytes 1048600
  26.1 0.6 copy-done.13
  26.7 0.6 copy-done.14
  27.3 12.9 %all-to-all-start = ((f32[128,4,128]{2,1,0:T(4,128)}), f32[128,4,128]{2,1,0:T(4,128)S(1)}, u32[]{:S(2)}, u32[]{:S(2)}) async-start(f32[128,4,128]{2,1,0:T(4,128)} %get-tuple-element.27), calls=%async_computation | async-start | bytes 524288 | tf_op jit(solution)/shard_map/all_to_all | solution.py:276
  40.2 0.6 collective-permute-start.7
  40.9 0.8 %collective-permute-start.8 = (f32[64,512]{1,0:T(8,128)S(1)}, f32[64,512]{1,0:T(8,128)S(1)}, u32[]{:S(2)}, u32[]{:S(2)}) collective-permute-start(f32[64,512]{1,0:T(8,128)S(1)} %get-tuple-element.34), channel_id=1, source_target_pairs={{0,248},{8,16},{16,8},{24,32},{32,24},{40,48},{48,40},{56,64},{64,... | collective-permute-start | bytes 393224 | tf_op jit(solution)/shard_map/ppermute | solution.py:253
  41.7 1.2 %collective-permute-start.9 = (f32[8,512]{1,0:T(8,128)}, f32[8,512]{1,0:T(8,128)S(1)}, u32[]{:S(2)}, u32[]{:S(2)}) collective-permute-start(f32[8,512]{1,0:T(8,128)} %copy-done.14), channel_id=1, source_target_pairs={{0,1},{1,2},{2,3},{3,4},{4,5},{5,6},{6,7},{7,0},{8,9},{9,10},{10,1... | collective-permute-start | bytes 49160 | tf_op jit(solution)/shard_map/ppermute | solution.py:278
  42.9 1.5 %collective-permute-start.10 = (f32[8,512]{1,0:T(8,128)}, f32[8,512]{1,0:T(8,128)S(1)}, u32[]{:S(2)}, u32[]{:S(2)}) collective-permute-start(f32[8,512]{1,0:T(8,128)} %copy-done.13), channel_id=1, source_target_pairs={{0,7},{1,0},{2,1},{3,2},{4,3},{5,4},{6,5},{7,6},{8,15},{9,8},{10,9... | collective-permute-start | bytes 49160 | tf_op jit(solution)/shard_map/ppermute | solution.py:279
  44.4 10.1 %all-to-all-done = f32[128,4,128]{2,1,0:T(4,128)S(1)} async-done(((f32[128,4,128]{2,1,0:T(4,128)}), f32[128,4,128]{2,1,0:T(4,128)S(1)}, u32[]{:S(2)}, u32[]{:S(2)}) %all-to-all-start) | async-done | bytes 262176 | tf_op jit(solution)/shard_map/all_to_all | solution.py:276
  54.5 1.8 %copy-done.4 = f32[17,10,32,128]{3,2,1,0:T(8,128)S(1)} copy-done((f32[17,10,32,128]{3,2,1,0:T(8,128)S(1)}, f32[17,10,32,128]{3,2,1,0:T(8,128)}, u32[]{:S(2)}) %copy-start.4) | copy-done | bytes 2785304
  56.3 1.5 %shard_map.57 = (f32[30,128]{1,0:T(8,128)S(1)}, f32[30,128]{1,0:T(8,128)S(1)}) custom-call(s32[3]{0:T(128)S(1)} %pad_add_fusion.core_ref.place_ref, f32[16,32,128]{2,1,0:T(8,128)S(1)} %bitcast.4, f32[17,10,32,128]{3,2,1,0:T(8,128)S(1)} %copy-done.4), custom_call_target="tpu_custom_call" | custom-call | tf_op jit(solution)/shard_map/pallas_call | solution.py:228
  57.9 2.0 %collective-permute-start.6 = (f32[30,128]{1,0:T(8,128)S(1)}, f32[30,128]{1,0:T(8,128)S(1)}, u32[]{:S(2)}, u32[]{:S(2)}) collective-permute-start(f32[30,128]{1,0:T(8,128)S(1)} %get-tuple-element.29), channel_id=1, source_target_pairs={{0,8},{8,0},{16,24},{24,16},{32,40},{40,32},{48,56},{56,48},{64,72... | collective-permute-start | bytes 46088 | tf_op jit(solution)/shard_map/ppermute | solution.py:250
  59.9 0.0 collective-permute-done.9.cylow_ref
  59.9 0.0 collective-permute-done.10.cyhigh_ref
  59.9 0.0 collective-permute-done.7.cnear_ref
  59.9 0.0 collective-permute-done.8.cfar_ref
  59.9 0.8 %collective-permute-done.6.other_ref = f32[30,128]{1,0:T(8,128)S(1)} collective-permute-done((f32[30,128]{1,0:T(8,128)S(1)}, f32[30,128]{1,0:T(8,128)S(1)}, u32[]{:S(2)}, u32[]{:S(2)}) %collective-permute-start.6) | collective-permute-done | bytes 15392 | tf_op jit(solution)/shard_map/ppermute | solution.py:250
  60.7 0.0 copy-done.11
  60.7 0.0 copy-done.6
  60.7 0.0 copy-done.8
  60.7 1.2 %copy-done.10 = f32[8,64,512]{2,1,0:T(8,128)S(1)} copy-done((f32[8,64,512]{2,1,0:T(8,128)S(1)}, f32[8,64,512]{2,1,0:T(8,128)}, u32[]{:S(2)}) %copy-start.10) | copy-done | bytes 1048600
  61.9 3.0 %shard_map.58 = f32[8,64,512]{2,1,0:T(8,128)} custom-call(s32[3]{0:T(128)S(1)} %pad_add_fusion.core_ref.place_ref, f32[30,128]{1,0:T(8,128)S(1)} %get-tuple-element.28.own_ref, f32[30,128]{1,0:T(8,128)S(1)} %collective-permute-done.6.other_ref, f32[128,512]{1,0:T(8,128)S(1)} %copy-done.11, f32[8,64,512]{2,1,0:T(8,128)S(1)} %copy-done.6, ...), custom_call_target="tpu_custom_call" | custom-call | tf_op jit(solution)/shard_map/pallas_call | solution.py:228
  (15 shorter events, 0.1 us)
Async XLA Ops:
  0.1 1.2 %copy-start = (f32[8,64,512]{2,1,0:T(8,128)S(1)}, f32[8,64,512]{2,1,0:T(8,128)}, u32[]{:S(2)}) copy-start(f32[8,64,512]{2,1,0:T(8,128)} %cot_ref.3) | copy-start | bytes 3145732
  1.3 1.2 %copy-start.2 = (f32[8,64,512]{2,1,0:T(8,128)S(1)}, f32[8,64,512]{2,1,0:T(8,128)}, u32[]{:S(2)}) copy-start(f32[8,64,512]{2,1,0:T(8,128)} %coef_ref.3) | copy-start | bytes 3145732
  2.5 16.1 %copy-start.1 = (f32[8,64,512]{2,1,0:T(8,128)S(1)}, f32[8,64,512]{2,1,0:T(8,128)}, u32[]{:S(2)}) copy-start(f32[8,64,512]{2,1,0:T(8,128)} %cot_ref.3) | copy-start | bytes 3145732
  2.5 16.1 %copy-start.3 = (f32[8,64,512]{2,1,0:T(8,128)S(1)}, f32[8,64,512]{2,1,0:T(8,128)}, u32[]{:S(2)}) copy-start(f32[8,64,512]{2,1,0:T(8,128)} %coef_ref.3) | copy-start | bytes 3145732
  4.0 6.2 %collective-permute-start.2 = (f32[2,512]{1,0:T(2,128)S(1)}, f32[2,512]{1,0:T(2,128)S(1)}, u32[]{:S(2)}, u32[]{:S(2)}) collective-permute-start(f32[2,512]{1,0:T(2,128)S(1)} %get-tuple-element.24), channel_id=1, source_target_pairs={{0,248},{8,16},{16,8},{24,32},{32,24},{40,48},{48,40},{56,64},{64,... | collective-permute-start | bytes 12296 | tf_op jit(solution)/shard_map/ppermute | solution.py:253
  6.7 4.3 %collective-permute-start.3 = (f32[2,512]{1,0:T(2,128)S(1)}, f32[2,512]{1,0:T(2,128)S(1)}, u32[]{:S(2)}, u32[]{:S(2)}) collective-permute-start(f32[2,512]{1,0:T(2,128)S(1)} %get-tuple-element.25), channel_id=1, source_target_pairs={{0,8},{8,0},{16,24},{24,16},{32,40},{40,32},{48,56},{56,48},{64,72... | collective-permute-start | bytes 12296 | tf_op jit(solution)/shard_map/ppermute | solution.py:250
  10.2 8.5 %collective-permute-start = (f32[3,64,512]{2,1,0:T(8,128)}, f32[3,64,512]{2,1,0:T(8,128)S(1)}, u32[]{:S(2)}, u32[]{:S(2)}) collective-permute-start(f32[3,64,512]{2,1,0:T(8,128)} %get-tuple-element.21), channel_id=1, source_target_pairs={{0,8},{8,0},{16,24},{24,16},{32,40},{40,32},{48,56},{56,48},{64,72... | collective-permute-start | bytes 1179656 | tf_op jit(solution)/shard_map/ppermute | solution.py:250
  10.2 8.5 %collective-permute-start.1 = (f32[3,64,512]{2,1,0:T(8,128)}, f32[3,64,512]{2,1,0:T(8,128)S(1)}, u32[]{:S(2)}, u32[]{:S(2)}) collective-permute-start(f32[3,64,512]{2,1,0:T(8,128)} %get-tuple-element.22), channel_id=1, source_target_pairs={{0,248},{8,16},{16,8},{24,32},{32,24},{40,48},{48,40},{56,64},{64,... | collective-permute-start | bytes 1179656 | tf_op jit(solution)/shard_map/ppermute | solution.py:253
  11.0 7.6 %collective-permute-start.4 = (f32[26,512]{1,0:T(8,128)S(1)}, f32[26,512]{1,0:T(8,128)S(1)}, u32[]{:S(2)}, u32[]{:S(2)}) collective-permute-start(f32[26,512]{1,0:T(8,128)S(1)} %pad_maximum_fusion), channel_id=1, source_target_pairs={{0,1},{1,2},{2,3},{3,4},{4,5},{5,6},{6,7},{7,0},{8,9},{9,10},{10,1... | collective-permute-start | bytes 159752 | tf_op jit(solution)/shard_map/ppermute | solution.py:267
  12.8 47.9 %copy-start.11 = (f32[128,512]{1,0:T(8,128)S(1)}, f32[128,512]{1,0:T(8,128)}, u32[]{:S(2)}) copy-start(f32[128,512]{1,0:T(8,128)} %constant.30.clone.out_table_ref) | copy-start | bytes 786436
  12.8 5.9 %collective-permute-start.5 = (f32[26,512]{1,0:T(8,128)S(1)}, f32[26,512]{1,0:T(8,128)S(1)}, u32[]{:S(2)}, u32[]{:S(2)}) collective-permute-start(f32[26,512]{1,0:T(8,128)S(1)} %pad_maximum_fusion.1), channel_id=1, source_target_pairs={{0,7},{1,0},{2,1},{3,2},{4,3},{5,4},{6,5},{7,6},{8,15},{9,8},{10,9... | collective-permute-start | bytes 159752 | tf_op jit(solution)/shard_map/ppermute | solution.py:268
  18.7 1.0 %copy-start.12 = (f32[512,64]{1,0:T(8,128)S(1)}, f32[512,64]{1,0:T(8,128)}, u32[]{:S(2)}) copy-start(f32[512,64]{1,0:T(8,128)} %constant.28.clone.into_ref) | copy-start | bytes 393220
  23.2 1.0 %copy-start.5 = (f32[8,64,512]{2,1,0:T(8,128)}, f32[8,64,512]{2,1,0:T(8,128)S(1)}, u32[]{:S(2)}) copy-start(f32[8,64,512]{2,1,0:T(8,128)S(1)} %get-tuple-element.30.c3_ref) | copy-start | bytes 3145732
  24.2 1.0 %copy-start.7 = (f32[8,64,512]{2,1,0:T(8,128)}, f32[8,64,512]{2,1,0:T(8,128)S(1)}, u32[]{:S(2)}) copy-start(f32[8,64,512]{2,1,0:T(8,128)S(1)} %get-tuple-element.31.base_ref) | copy-start | bytes 3145732
  25.2 1.0 %copy-start.9 = (f32[8,64,512]{2,1,0:T(8,128)}, f32[8,64,512]{2,1,0:T(8,128)S(1)}, u32[]{:S(2)}) copy-start(f32[8,64,512]{2,1,0:T(8,128)S(1)} %get-tuple-element.32.inverse_ref) | copy-start | bytes 3145732
  26.1 0.6 copy-start.13
  26.7 0.6 copy-start.14
  27.3 27.2 %all-to-all-start = ((f32[128,4,128]{2,1,0:T(4,128)}), f32[128,4,128]{2,1,0:T(4,128)S(1)}, u32[]{:S(2)}, u32[]{:S(2)}) async-start(f32[128,4,128]{2,1,0:T(4,128)} %get-tuple-element.27), calls=%async_computation | async-start | bytes 524288 | tf_op jit(solution)/shard_map/all_to_all | solution.py:276
  40.2 19.6 %collective-permute-start.7 = (f32[64,512]{1,0:T(8,128)S(1)}, f32[64,512]{1,0:T(8,128)S(1)}, u32[]{:S(2)}, u32[]{:S(2)}) collective-permute-start(f32[64,512]{1,0:T(8,128)S(1)} %get-tuple-element.33), channel_id=1, source_target_pairs={{0,8},{8,0},{16,24},{24,16},{32,40},{40,32},{48,56},{56,48},{64,72... | collective-permute-start | bytes 393224 | tf_op jit(solution)/shard_map/ppermute | solution.py:250
  40.9 19.0 %collective-permute-start.8 = (f32[64,512]{1,0:T(8,128)S(1)}, f32[64,512]{1,0:T(8,128)S(1)}, u32[]{:S(2)}, u32[]{:S(2)}) collective-permute-start(f32[64,512]{1,0:T(8,128)S(1)} %get-tuple-element.34), channel_id=1, source_target_pairs={{0,248},{8,16},{16,8},{24,32},{32,24},{40,48},{48,40},{56,64},{64,... | collective-permute-start | bytes 393224 | tf_op jit(solution)/shard_map/ppermute | solution.py:253
  41.7 18.2 %collective-permute-start.9 = (f32[8,512]{1,0:T(8,128)}, f32[8,512]{1,0:T(8,128)S(1)}, u32[]{:S(2)}, u32[]{:S(2)}) collective-permute-start(f32[8,512]{1,0:T(8,128)} %copy-done.14), channel_id=1, source_target_pairs={{0,1},{1,2},{2,3},{3,4},{4,5},{5,6},{6,7},{7,0},{8,9},{9,10},{10,1... | collective-permute-start | bytes 49160 | tf_op jit(solution)/shard_map/ppermute | solution.py:278
  42.9 17.0 %collective-permute-start.10 = (f32[8,512]{1,0:T(8,128)}, f32[8,512]{1,0:T(8,128)S(1)}, u32[]{:S(2)}, u32[]{:S(2)}) collective-permute-start(f32[8,512]{1,0:T(8,128)} %copy-done.13), channel_id=1, source_target_pairs={{0,7},{1,0},{2,1},{3,2},{4,3},{5,4},{6,5},{7,6},{8,15},{9,8},{10,9... | collective-permute-start | bytes 49160 | tf_op jit(solution)/shard_map/ppermute | solution.py:279
  54.5 1.8 %copy-start.4 = (f32[17,10,32,128]{3,2,1,0:T(8,128)S(1)}, f32[17,10,32,128]{3,2,1,0:T(8,128)}, u32[]{:S(2)}) copy-start(f32[17,10,32,128]{3,2,1,0:T(8,128)} %constant.29.clone.table_ref) | copy-start | bytes 8355844
  56.3 4.4 %copy-start.6 = (f32[8,64,512]{2,1,0:T(8,128)S(1)}, f32[8,64,512]{2,1,0:T(8,128)}, u32[]{:S(2)}) copy-start(f32[8,64,512]{2,1,0:T(8,128)} %copy-done.5) | copy-start | bytes 3145732
  56.3 4.4 %copy-start.8 = (f32[8,64,512]{2,1,0:T(8,128)S(1)}, f32[8,64,512]{2,1,0:T(8,128)}, u32[]{:S(2)}) copy-start(f32[8,64,512]{2,1,0:T(8,128)} %copy-done.7) | copy-start | bytes 3145732
  57.9 2.9 %collective-permute-start.6 = (f32[30,128]{1,0:T(8,128)S(1)}, f32[30,128]{1,0:T(8,128)S(1)}, u32[]{:S(2)}, u32[]{:S(2)}) collective-permute-start(f32[30,128]{1,0:T(8,128)S(1)} %get-tuple-element.29), channel_id=1, source_target_pairs={{0,8},{8,0},{16,24},{24,16},{32,40},{40,32},{48,56},{56,48},{64,72... | collective-permute-start | bytes 46088 | tf_op jit(solution)/shard_map/ppermute | solution.py:250
  60.7 1.2 %copy-start.10 = (f32[8,64,512]{2,1,0:T(8,128)S(1)}, f32[8,64,512]{2,1,0:T(8,128)}, u32[]{:S(2)}) copy-start(f32[8,64,512]{2,1,0:T(8,128)} %copy-done.9) | copy-start | bytes 3145732

commit v2 on v1

v2 whole, which is shorter than its diff:
```python
import math

import jax
import jax.numpy as jnp
import numpy as np
from jax import lax
from jax.experimental import pallas as pl
from jax.experimental.pallas import tpu as pltpu
from jax.sharding import Mesh
from jax.sharding import PartitionSpec as P

screen = 0.02
w1 = 1.0 / (1.25 + 0.75 * math.cos(math.pi / 4.0))
w2 = 1.0 / (1.25 - 0.75 * math.cos(math.pi / 4.0))

BX, BY, NZ = 8, 64, 512
CX, CY, CZ = 32, 64, 64
GX, GY = 32, 8
CHIPS = GX // 2
ROWS = CY // 2
OUT_Y = BY // 8 + 2
OUT_X = 4

VMEM = pl.BlockSpec(memory_space=pltpu.VMEM)
SMEM = pl.BlockSpec(memory_space=pltpu.SMEM)
HBM = pl.BlockSpec(memory_space=pltpu.HBM)
F32 = jnp.float32


def basis():
    place = np.arange(CZ)
    columns, freq = [], []
    for k in range(CZ // 2 + 1):
        scale = math.sqrt((1.0 if k in (0, CZ // 2) else 2.0) / CZ)
        columns.append(scale * np.cos(2.0 * math.pi * k * place / CZ))
        freq.append(k)
    for k in range(1, CZ // 2):
        columns.append(math.sqrt(2.0 / CZ) * np.sin(2.0 * math.pi * k * place / CZ))
        freq.append(k)
    return np.stack(columns, 1), np.array(freq)


def symbol(length):
    return 2.0 - 2.0 * np.cos(2.0 * math.pi * np.arange(length) / length)


def tables():
    columns, freq = basis()
    spectrum = (
        screen
        + symbol(CX)[:, None, None]
        + symbol(CY)[None, :, None]
        + symbol(CZ)[freq][None, None, :]
    )
    green = np.real(np.fft.ifft2(1.0 / spectrum, axes=(0, 1)))
    t, d, h = np.meshgrid(np.arange(OUT_Y + 3), np.arange(GY), np.arange(2), indexing="ij")
    shift = (t - 4 - 8 * d - 4 * h) % CY
    table = green[: CX // 2 + 1][:, shift].reshape(CX // 2 + 1, OUT_Y + 3, GY, 2 * CZ)
    table = table.astype(np.float32)
    into = np.repeat(columns, NZ // CZ, axis=0).astype(np.float32)
    out = np.concatenate([into.T, into.T], 0) / 8.0
    return table, into, out.astype(np.float32)


def zsum(v):
    return pltpu.roll(v, 1, 1) + pltpu.roll(v, NZ - 1, 1)


def shifted_sum(v, low, high):
    size = v.shape[0]
    row = lax.broadcasted_iota(jnp.int32, v.shape, 0)
    before = jnp.where(row == 0, low, pltpu.roll(v, 1, 0))
    after = jnp.where(row == size - 1, high, pltpu.roll(v, size - 1, 0))
    return before + after


def fetch(pairs, sems, first=0):
    copies = [pltpu.make_async_copy(s, d, sems.at[first + i]) for i, (s, d) in enumerate(pairs)]
    for copy in copies:
        copy.start()
    return copies


def wait(copies):
    for copy in copies:
        copy.wait()


def pack_kernel(
    core_ref, cot_hbm, coef_hbm,
    near_ref, far_ref, tnear_ref, tfar_ref, ylow_ref, yhigh_ref, cot_ref, coef_ref, sems,
):
    core = core_ref[0]
    order = (0, 1, BX - 2, BX - 1) + tuple(range(2, BX - 2))
    copies = fetch(
        [(a.at[x], b.at[x]) for x in order for a, b in ((cot_hbm, cot_ref), (coef_hbm, coef_ref))],
        sems,
    )
    wait(copies[:8])
    edges = (
        (near_ref, tnear_ref, (BX - 1) * (1 - core), 2 * core - 1),
        (far_ref, tfar_ref, (BX - 1) * core, 1 - 2 * core),
    )
    for out, tiny, edge, step in edges:
        cot = cot_ref[edge]
        inverse = 1.0 / (6.0 + coef_ref[edge])
        w5 = w2 * cot * inverse
        tiny[0:1, :] = w5[0:1, :]
        tiny[1:2, :] = w5[BY - 1 : BY, :]
        out[0] = w5
        out[1] = inverse
        out[2] = (1.0 - w2) * cot + w2 * cot_ref[edge + step] / (6.0 + coef_ref[edge + step])
    wait(copies[8:])
    for out, edge, inner in ((ylow_ref, 0, 1), (yhigh_ref, BY - 1, BY - 2)):
        cot = cot_ref[:, edge, :]
        inverse = 1.0 / (6.0 + coef_ref[:, edge, :])
        out[0:8, :] = w2 * cot * inverse
        out[8:16, :] = inverse
        out[16:24, :] = (1.0 - w2) * cot + w2 * cot_ref[:, inner, :] / (6.0 + coef_ref[:, inner, :])


def local_kernel(cot_ref, coef_ref, w5_ref, inverse_ref, c4_ref):
    for x in range(BX):
        inverse = 1.0 / (6.0 + coef_ref[x])
        inverse_ref[x] = inverse
        w5_ref[x] = w2 * cot_ref[x] * inverse
    none = jnp.zeros((1, NZ), F32)
    for x in range(BX):
        w5 = w5_ref[x]
        c4 = (1.0 - w2) * cot_ref[x] + zsum(w5) + shifted_sum(w5, none, none)
        if x > 0:
            c4 = c4 + w5_ref[x - 1]
        if x < BX - 1:
            c4 = c4 + w5_ref[x + 1]
        c4_ref[x] = c4


def first_kernel(
    core_ref, w5_ref, inverse_ref, part_ref, near_ref, far_ref, ylow_ref, yhigh_ref, into_hbm,
    c3_hbm, base_hbm, inverse_hbm, planes_hbm, rows_hbm,
    cnear_ref, cfar_ref, cylow_ref, cyhigh_ref, send_ref,
    halo_ref, w4_ref, c3_ref, base_ref, into_ref, sems,
):
    core = core_ref[0]
    copies = fetch(
        [(into_hbm, into_ref)]
        + [(inverse_ref.at[x], inverse_hbm.at[x]) for x in range(BX)]
        + [
            (near_ref.at[1], planes_hbm.at[1 - core]),
            (far_ref.at[1], planes_hbm.at[core]),
            (ylow_ref.at[pl.ds(8, 8)], rows_hbm.at[0]),
            (yhigh_ref.at[pl.ds(8, 8)], rows_hbm.at[1]),
        ],
        sems,
    )
    halos = ((near_ref, 1 - core, core == 0), (far_ref, core, core == 1))
    y4 = []
    for packet, edge in ((ylow_ref, 0), (yhigh_ref, BY - 1)):
        w5 = packet[0:8, :]
        c4 = packet[16:24, :] + w5_ref[:, edge, :] + zsum(w5)
        c4 = c4 + shifted_sum(w5, packet[24:25, :], packet[25:26, :])
        y4.append(w1 * packet[8:16, :] * c4)
    for halo, side, at_high in halos:
        halo_ref[side] = halo[0]
        low = jnp.where(at_high, ylow_ref[25:26, :], ylow_ref[24:25, :])
        high = jnp.where(at_high, yhigh_ref[25:26, :], yhigh_ref[24:25, :])
        w5 = halo[0]
        c4 = halo[2] + w5_ref[(BX - 1) * side] + zsum(w5) + shifted_sum(w5, low, high)
        w4_ref[(BX + 1) * side] = w1 * halo[1] * c4
    row = lax.broadcasted_iota(jnp.int32, (8, NZ), 0)
    for x in range(BX):
        low = jnp.where(row == 0, ylow_ref[x : x + 1, :], 0.0)
        high = jnp.where(row == 7, yhigh_ref[x : x + 1, :], 0.0)
        part = part_ref[x]
        c4 = jnp.concatenate([part[0:8, :] + low, part[8 : BY - 8, :], part[BY - 8 : BY, :] + high], 0)
        if x == 0:
            c4 = c4 + halo_ref[0]
        if x == BX - 1:
            c4 = c4 + halo_ref[1]
        w4 = w1 * inverse_ref[x] * c4
        w4_ref[x + 1] = w4
        base_ref[x] = w5_ref[x] + w4
        c3_ref[x] = c4
        copies += fetch([(base_ref.at[x], base_hbm.at[x])], sems, BX + 5 + x)
    total = jnp.zeros((BY, NZ), F32)
    for x in range(BX):
        w4 = w4_ref[x + 1]
        c3 = (1.0 - w1) * c3_ref[x] + w4_ref[x] + w4_ref[x + 2] + zsum(w4)
        c3 = c3 + shifted_sum(w4, y4[0][x : x + 1, :], y4[1][x : x + 1, :])
        c3_ref[x] = c3
        copies += fetch([(c3_ref.at[x], c3_hbm.at[x])], sems, 2 * BX + 5 + x)
        cylow_ref[x : x + 1, :] = c3[0:1, :]
        cyhigh_ref[x : x + 1, :] = c3[BY - 1 : BY, :]
        total = total + c3
    sums = jnp.sum(total.reshape(BY // 8, 8, NZ), axis=1)
    copies[0].wait()
    modes = jnp.dot(sums, into_ref[...], precision=lax.Precision.HIGHEST, preferred_element_type=F32)
    packed = jnp.concatenate([modes[0:4, :], modes[4:8, :]], axis=1)
    send_ref[...] = jnp.broadcast_to(packed[None], send_ref.shape)
    cnear_ref[...] = c3_ref[(BX - 1) * (1 - core)]
    cfar_ref[...] = c3_ref[(BX - 1) * core]
    wait(copies[1:])


def coarse_kernel(
    place_ref, got_ref, table_hbm, out_table_hbm, c3_hbm, base_hbm, inverse_hbm, planes_hbm, rows_hbm,
    cnear_hbm, cfar_hbm, cylow_hbm, cyhigh_hbm,
    own_ref, other_ref, out_table_ref, c3_ref, base_ref, inverse_ref, planes_ref, rows_ref,
    cplanes_ref, crows_ref, table_ref, rolled_ref, sums_ref, sems,
):
    core, chip, gy = place_ref[0], place_ref[1], place_ref[2]
    first = fetch([(table_hbm.at[i], table_ref.at[i]) for i in range(CX // 2 + 1)], sems)
    later = fetch(
        [(a.at[x], b.at[x]) for a, b in ((c3_hbm, c3_ref), (inverse_hbm, inverse_ref)) for x in range(BX)]
        + [
            (out_table_hbm, out_table_ref),
            (planes_hbm, planes_ref),
            (rows_hbm, rows_ref),
            (cnear_hbm, cplanes_ref.at[1 - core]),
            (cfar_hbm, cplanes_ref.at[core]),
            (cylow_hbm, crows_ref.at[0]),
            (cyhigh_hbm, crows_ref.at[1]),
        ]
        + [(base_hbm.at[x], base_ref.at[x]) for x in range(BX)],
        sems,
        CX // 2 + 1,
    )
    turn = lax.rem(GY - gy, GY)
    for q in range(CHIPS):
        plane = lax.rem(chip + (1 - 2 * core) * q + CHIPS, CHIPS)
        for r in range(4):
            rolled_ref[q, r] = pltpu.roll(got_ref[plane, pl.ds(r, GY, stride=4), :], turn, 0)
    wait(first)

    def step(q, totals):
        totals = list(totals)
        source = [rolled_ref[q, r] for r in range(4)]
        for m in range(-1, OUT_X - 1):
            away = lax.rem(2 * CX - 2 * q + m, CX)
            away = jnp.minimum(away, CX - away)
            weight = [table_ref[away, t] for t in range(OUT_Y + 3)]
            for j in range(OUT_Y):
                at = (m + 1) * OUT_Y + j
                for r in range(4):
                    totals[at] = totals[at] + weight[j + 3 - r] * source[r]
        return tuple(totals)

    zero = jnp.zeros((8, 2 * CZ), F32)
    totals = lax.fori_loop(0, CHIPS, step, (zero,) * (OUT_X * OUT_Y), unroll=2)
    for at in range(OUT_X * OUT_Y):
        sums_ref[at : at + 1, :] = jnp.sum(totals[at], axis=0, keepdims=True)
    own_ref[...] = sums_ref[0 : 3 * OUT_Y, :]
    for m in range(3):
        start = (OUT_X - 1 - m) * OUT_Y
        other_ref[m * OUT_Y : (m + 1) * OUT_Y, :] = sums_ref[start : start + OUT_Y, :]
    wait(later)


def last_kernel(
    core_ref, own_ref, other_ref, out_table_ref, c3_ref, base_ref, inverse_ref, planes_ref, rows_ref,
    cplanes_ref, crows_ref,
    out_hbm, w_ref, out_ref, sems,
):
    core = core_ref[0]
    modes = own_ref[...] + other_ref[...]
    coarse = jnp.dot(modes, out_table_ref[...], precision=lax.Precision.HIGHEST, preferred_element_type=F32)
    outer, middle, inner = (coarse[m * OUT_Y : (m + 1) * OUT_Y, :] for m in range(3))
    low = jnp.where(core == 0, outer, inner)
    high = jnp.where(core == 0, inner, outer)

    def rows_of(plane):
        return jnp.concatenate([jnp.broadcast_to(plane[j : j + 1, :], (8, NZ)) for j in range(1, OUT_Y - 1)], 0)

    def side_sum(plane, fine):
        return shifted_sum(fine, plane[0:1, :], plane[OUT_Y - 1 : OUT_Y, :]) + zsum(fine)

    s, s_low, s_high = rows_of(middle), rows_of(low), rows_of(high)
    beside = side_sum(middle, s)
    for side, fine, plane in ((0, s_low, low), (1, s_high, high)):
        value = cplanes_ref[side] + fine + s + side_sum(plane, fine)
        w_ref[(BX + 1) * side] = w2 * (planes_ref[side] * value - fine)
    y_w = []
    for side, edge, near_edge in ((0, 0, 1), (1, OUT_Y - 1, OUT_Y - 2)):
        fine = jnp.broadcast_to(middle[edge : edge + 1, :], (BX, NZ))
        value = crows_ref[side] + fine + middle[near_edge : near_edge + 1, :] + zsum(fine)
        value = value + shifted_sum(fine, low[edge : edge + 1, :], high[edge : edge + 1, :])
        y_w.append(w2 * (rows_ref[side] * value - fine))
    for x in range(BX):
        around = beside + (s_low if x == 0 else s) + (s_high if x == BX - 1 else s)
        w_ref[x + 1] = w2 * (inverse_ref[x] * (c3_ref[x] + around) - s)
    copies = []
    for x in range(BX):
        w = w_ref[x + 1]
        near = w_ref[x] + w_ref[x + 2] + zsum(w)
        near = near + shifted_sum(w, y_w[0][x : x + 1, :], y_w[1][x : x + 1, :])
        out_ref[x] = base_ref[x] + s + w + w1 * ((1.0 - w2) / w2 * w + inverse_ref[x] * near)
        copies += fetch([(out_ref.at[x], out_hbm.at[x])], sems, x)
    wait(copies)


def call(kernel, outs, ins, in_specs, out_specs, scratch=(), sems=0, cost=None):
    scratch = [pltpu.VMEM(shape, F32) for shape in scratch]
    if sems:
        scratch.append(pltpu.SemaphoreType.DMA((sems,)))
    ins = [
        x if spec is SMEM else pltpu.with_memory_space_constraint(x, spec.memory_space)
        for x, spec in zip(ins, in_specs)
    ]
    return pl.pallas_call(
        kernel,
        out_shape=[spec.memory_space(shape, F32) for shape, spec in zip(outs, out_specs)],
        in_specs=in_specs,
        out_specs=out_specs,
        scratch_shapes=scratch,
        cost_estimate=cost,
        compiler_params=pltpu.CompilerParams(vmem_limit_bytes=20 * 1024 * 1024),
    )(*ins)


def body(cotangent, coefficient):
    table, into, out_table = tables()
    along_x = ("x", "y", "core")
    core = lax.axis_index("core")
    place = jnp.stack([core, lax.axis_index("x") * 4 + lax.axis_index("y"), lax.axis_index("gy")])
    place = place.astype(jnp.int32)
    near_pairs = [(i, i ^ 1) for i in range(GX)]
    far_pairs = [(i, (i + 1) % GX if i % 2 else (i - 1) % GX) for i in range(GX)]
    up = [(i, (i + 1) % GY) for i in range(GY)]
    down = [(i, (i - 1) % GY) for i in range(GY)]

    def near_swap(v):
        return lax.ppermute(v, along_x, near_pairs)

    def far_swap(v):
        return lax.ppermute(v, along_x, far_pairs)

    brick, plane, rows = (BX, BY, NZ), (BY, NZ), (BX, NZ)
    near, far, tiny_near, tiny_far, y_low, y_high, cot, coef = call(
        pack_kernel,
        [(3,) + plane, (3,) + plane, (2, NZ), (2, NZ), (24, NZ), (24, NZ), brick, brick],
        [place, cotangent, coefficient],
        [SMEM, HBM, HBM],
        [VMEM] * 8,
        sems=2 * BX,
    )
    tiny_near, tiny_far = near_swap(tiny_near), far_swap(tiny_far)
    near, far = near_swap(near), far_swap(far)
    corner_low = jnp.where(core == 0, tiny_far, tiny_near)
    corner_high = jnp.where(core == 0, tiny_near, tiny_far)
    y_low = jnp.concatenate([y_low, corner_low[0:1], corner_high[0:1]], 0)
    y_high = jnp.concatenate([y_high, corner_low[1:2], corner_high[1:2]], 0)
    from_low = lax.ppermute(y_high, "gy", up)
    from_high = lax.ppermute(y_low, "gy", down)
    w5, inverse, part = call(
        local_kernel,
        [brick, brick, brick],
        [cot, coef],
        [VMEM] * 2,
        [VMEM] * 3,
        cost=pl.CostEstimate(flops=40 * BX * BY * NZ, bytes_accessed=5 * 4 * BX * BY * NZ, transcendentals=0),
    )
    c3, base, inverse, planes, edge_rows, c_near, c_far, cy_low, cy_high, send = call(
        first_kernel,
        [brick, brick, brick, (2,) + plane, (2,) + rows, plane, plane, rows, rows, (CHIPS * GY, 4, 2 * CZ)],
        [place, w5, inverse, part, near, far, from_low, from_high, jnp.asarray(into)],
        [SMEM] + [VMEM] * 7 + [HBM],
        [HBM] * 5 + [VMEM] * 5,
        scratch=[(2,) + plane, (BX + 2,) + plane, brick, brick, (NZ, CZ)],
        sems=3 * BX + 5,
    )
    got = lax.all_to_all(send, ("x", "y", "gy"), 0, 0, tiled=True)
    c_near, c_far = near_swap(c_near), far_swap(c_far)
    c_from_low = lax.ppermute(cy_high, "gy", up)
    c_from_high = lax.ppermute(cy_low, "gy", down)
    got = got.reshape(CHIPS, ROWS, 2 * CZ)
    own, other, *rest = call(
        coarse_kernel,
        [(3 * OUT_Y, 2 * CZ)] * 2
        + [(2 * CZ, NZ), brick, brick, brick, (2,) + plane, (2,) + rows, (2,) + plane, (2,) + rows],
        [place, got, jnp.asarray(table), jnp.asarray(out_table), c3, base, inverse, planes, edge_rows]
        + [c_near, c_far, c_from_low, c_from_high],
        [SMEM, VMEM] + [HBM] * 11,
        [VMEM] * 10,
        scratch=[(CX // 2 + 1, OUT_Y + 3, GY, 2 * CZ), (CHIPS, 4, GY, 2 * CZ), (OUT_X * OUT_Y, 2 * CZ)],
        sems=CX // 2 + 1 + 3 * BX + 7,
    )
    other = near_swap(other)
    return call(
        last_kernel,
        [brick],
        [place, own, other, *rest],
        [SMEM] + [VMEM] * 10,
        [HBM],
        scratch=[(BX + 2,) + plane, brick],
        sems=BX,
    )[0]


def solution(mesh):
    split = Mesh(np.asarray(mesh.devices).reshape(4, 4, 2, GY), ("x", "y", "core", "gy"))
    spec = P(("x", "y", "core"), "gy", None)
    return jax.shard_map(body, mesh=split, in_specs=(spec, spec), out_specs=spec, check_vma=False)
```

time: 65.3 us -> 57.6 us (0.88)
  local copies, waits for them, and re-layouts: 10.6 us -> 0.03 us
  Pallas kernels: 9.63 us -> 13.5 us
  waiting for transfers between devices: 13.6 us -> 12.7 us
    unnamed x30 -> x8, local copies, waits for them, and re-layouts: 10.5 us -> 0.02 us
    pallas_call x4 -> x5, Pallas kernels: 9.63 us -> 13.5 us  [call(): pl.pallas_call(kernel, out_shape=[spec.memory_space(shape, F32) for shape...]
    all_to_all x1, waiting for transfers between devices: 10.1 us -> 7.82 us  [body(): got = lax.all_to_all(send, ('x', 'y', 'gy'), 0, 0, tiled=True)]
    ppermute x1, waiting for transfers between devices: 0.01 us -> 2.24 us  [body(): c_from_low = lax.ppermute(cy_high, 'gy', up)]
    ppermute x1, waiting for transfers between devices: 1.83 us -> 0.97 us  [body(): from_low = lax.ppermute(y_high, 'gy', up)]
  transfers between devices with their start and end apart: 12 -> 12, of which waited for: 4 -> 5; matrix products, arithmetic and copies ran while one was open for 0% -> 0% of each run, Pallas kernels for 2% -> 2%
where the time goes in v2:
time: 57.6 us; the launch traced here: 57.4 us
  starting transfers between devices  30.9 us (54%)
  Pallas kernels  13.5 us (23%)
  waiting for transfers between devices  12.7 us (22%)
    pallas_call x5, Pallas kernels, call(): pl.pallas_call(kernel, out_shape=[spec.memory_space(shape, F32) for shape...  13.5 us
    all_to_all x1, starting transfers between devices, body(): got = lax.all_to_all(send, ('x', 'y', 'gy'), 0, 0, tiled=True)  12.7 us
    all_to_all x1, waiting for transfers between devices, body(): got = lax.all_to_all(send, ('x', 'y', 'gy'), 0, 0, tiled=True)  7.82 us
    ppermute x4, starting transfers between devices, near_swap(): return lax.ppermute(v, along_x, near_pairs)  6.13 us
    ppermute x1, starting transfers between devices, body(): from_high = lax.ppermute(y_low, 'gy', down)  4.03 us
    ppermute x3, starting transfers between devices, far_swap(): return lax.ppermute(v, along_x, far_pairs)  3.62 us
    ppermute x1, waiting for transfers between devices, body(): c_from_low = lax.ppermute(cy_high, 'gy', up)  2.24 us
    ppermute x1, starting transfers between devices, body(): from_low = lax.ppermute(y_high, 'gy', up)  1.71 us
  transfers between devices with their start and end apart: 12, of which 5 were waited for; matrix products, arithmetic and copies ran while one was open for 0% of the time, Pallas kernels for 2%

profile of v2, /device:TPU:1, one launch (start us, length us, event | category | flops | bytes accessed | tf_op | source)
XLA Modules:
  0.0 57.4 jit_solution(7217876913687885994)
XLA Ops:
  0.0 0.1 pad_add_fusion.core_ref.place_ref
  0.1 3.0 %shard_map.55 = (f32[3,64,512]{2,1,0:T(8,128)}, f32[3,64,512]{2,1,0:T(8,128)S(1)}, f32[2,512]{1,0:T(2,128)S(1)}, f32[2,512]{1,0:T(2,128)S(1)}, f32[24,512]{1,0:T...) custom-call(s32[3]{0:T(128)S(1)} %pad_add_fusion.core_ref.place_ref, ...), custom_call_target="tpu_custom_call" | custom-call | tf_op jit(solution)/shard_map/pallas_call | solution.py:309
  3.1 2.8 %collective-permute-start.2 = (f32[2,512]{1,0:T(2,128)S(1)}, f32[2,512]{1,0:T(2,128)S(1)}, u32[]{:S(2)}, u32[]{:S(2)}) collective-permute-start(f32[2,512]{1,0:T(2,128)S(1)} %get-tuple-element.44), channel_id=1, source_target_pairs={{0,248},{8,16},{16,8},{24,32},{32,24},{40,48},{48,40},{56,64},{64,... | collective-permute-start | bytes 12296 | tf_op jit(solution)/shard_map/ppermute | solution.py:335
  5.9 3.5 %collective-permute-start.3 = (f32[2,512]{1,0:T(2,128)S(1)}, f32[2,512]{1,0:T(2,128)S(1)}, u32[]{:S(2)}, u32[]{:S(2)}) collective-permute-start(f32[2,512]{1,0:T(2,128)S(1)} %get-tuple-element.45), channel_id=1, source_target_pairs={{0,8},{8,0},{16,24},{24,16},{32,40},{40,32},{48,56},{56,48},{64,72... | collective-permute-start | bytes 12296 | tf_op jit(solution)/shard_map/ppermute | solution.py:332
  9.3 0.0 collective-permute-start
  9.4 0.0 collective-permute-start.1
  9.4 0.0 collective-permute-done.2
  9.4 0.8 %collective-permute-done.3 = f32[2,512]{1,0:T(2,128)S(1)} collective-permute-done((f32[2,512]{1,0:T(2,128)S(1)}, f32[2,512]{1,0:T(2,128)S(1)}, u32[]{:S(2)}, u32[]{:S(2)}) %collective-permute-start.3) | collective-permute-done | bytes 4128 | tf_op jit(solution)/shard_map/ppermute | solution.py:332
  10.2 1.7 %collective-permute-start.4 = (f32[26,512]{1,0:T(8,128)S(1)}, f32[26,512]{1,0:T(8,128)S(1)}, u32[]{:S(2)}, u32[]{:S(2)}) collective-permute-start(f32[26,512]{1,0:T(8,128)S(1)} %pad_maximum_fusion), channel_id=1, source_target_pairs={{0,1},{1,2},{2,3},{3,4},{4,5},{5,6},{6,7},{7,0},{8,9},{9,10},{10,1... | collective-permute-start | bytes 159752 | tf_op jit(solution)/shard_map/ppermute | solution.py:352
  11.9 4.0 %collective-permute-start.5 = (f32[26,512]{1,0:T(8,128)S(1)}, f32[26,512]{1,0:T(8,128)S(1)}, u32[]{:S(2)}, u32[]{:S(2)}) collective-permute-start(f32[26,512]{1,0:T(8,128)S(1)} %pad_maximum_fusion.1), channel_id=1, source_target_pairs={{0,7},{1,0},{2,1},{3,2},{4,3},{5,4},{6,5},{7,6},{8,15},{9,8},{10,9... | collective-permute-start | bytes 159752 | tf_op jit(solution)/shard_map/ppermute | solution.py:353
  16.0 0.9 %shard_map.56 = (f32[8,64,512]{2,1,0:T(8,128)S(1)}, f32[8,64,512]{2,1,0:T(8,128)S(1)}, f32[8,64,512]{2,1,0:T(8,128)S(1)}) custom-call(f32[8,64,512]{2,1,0:T(8,128)S(1)} %get-tuple-element.36.cot_ref, f32[8,64,512]{2,1,0:T(8,128)S(1)} %get-tuple-element.37.coef_ref), custom_call_target="tpu_custom_call" | custom-call | flops 10485760 | bytes 5242880 | tf_op jit(solution)/shard_map/pallas_call | solution.py:309
  16.8 1.0 %collective-permute-done.4.ylow_ref = f32[26,512]{1,0:T(8,128)S(1)} collective-permute-done((f32[26,512]{1,0:T(8,128)S(1)}, f32[26,512]{1,0:T(8,128)S(1)}, u32[]{:S(2)}, u32[]{:S(2)}) %collective-permute-start.4) | collective-permute-done | bytes 53280 | tf_op jit(solution)/shard_map/ppermute | solution.py:352
  17.8 0.0 collective-permute-done.5.yhigh_ref
  17.8 0.0 collective-permute-done.near_ref
  17.8 0.0 collective-permute-done.1.far_ref
  17.8 3.4 %shard_map.57 = (f32[8,64,512]{2,1,0:T(8,128)}, f32[8,64,512]{2,1,0:T(8,128)}, f32[8,64,512]{2,1,0:T(8,128)}, f32[2,64,512]{2,1,0:T(8,128)}, f32[2,8,512]{2,1,0:...) custom-call(s32[3]{0:T(128)S(1)} %pad_add_fusion.core_ref.place_ref,, ...), custom_call_target="tpu_custom_call" | custom-call | tf_op jit(solution)/shard_map/pallas_call | solution.py:309
  21.3 12.7 %all-to-all-start = ((f32[128,4,128]{2,1,0:T(4,128)}), f32[128,4,128]{2,1,0:T(4,128)S(1)}, u32[]{:S(2)}, u32[]{:S(2)}) async-start(f32[128,4,128]{2,1,0:T(4,128)} %get-tuple-element.47), calls=%async_computation | async-start | bytes 524288 | tf_op jit(solution)/shard_map/all_to_all | solution.py:371
  34.0 0.6 %collective-permute-start.6 = (f32[64,512]{1,0:T(8,128)S(1)}, f32[64,512]{1,0:T(8,128)S(1)}, u32[]{:S(2)}, u32[]{:S(2)}) collective-permute-start(f32[64,512]{1,0:T(8,128)S(1)} %get-tuple-element.53), channel_id=1, source_target_pairs={{0,8},{8,0},{16,24},{24,16},{32,40},{40,32},{48,56},{56,48},{64,72... | collective-permute-start | bytes 393224 | tf_op jit(solution)/shard_map/ppermute | solution.py:332
  34.6 0.8 %collective-permute-start.7 = (f32[64,512]{1,0:T(8,128)S(1)}, f32[64,512]{1,0:T(8,128)S(1)}, u32[]{:S(2)}, u32[]{:S(2)}) collective-permute-start(f32[64,512]{1,0:T(8,128)S(1)} %get-tuple-element.54), channel_id=1, source_target_pairs={{0,248},{8,16},{16,8},{24,32},{32,24},{40,48},{48,40},{56,64},{64,... | collective-permute-start | bytes 393224 | tf_op jit(solution)/shard_map/ppermute | solution.py:335
  35.5 1.2 %collective-permute-start.8 = (f32[8,512]{1,0:T(8,128)S(1)}, f32[8,512]{1,0:T(8,128)S(1)}, u32[]{:S(2)}, u32[]{:S(2)}) collective-permute-start(f32[8,512]{1,0:T(8,128)S(1)} %get-tuple-element.55), channel_id=1, source_target_pairs={{0,1},{1,2},{2,3},{3,4},{4,5},{5,6},{6,7},{7,0},{8,9},{9,10},{10,1... | collective-permute-start | bytes 49160 | tf_op jit(solution)/shard_map/ppermute | solution.py:373
  36.6 1.5 %collective-permute-start.9 = (f32[8,512]{1,0:T(8,128)S(1)}, f32[8,512]{1,0:T(8,128)S(1)}, u32[]{:S(2)}, u32[]{:S(2)}) collective-permute-start(f32[8,512]{1,0:T(8,128)S(1)} %get-tuple-element.56), channel_id=1, source_target_pairs={{0,7},{1,0},{2,1},{3,2},{4,3},{5,4},{6,5},{7,6},{8,15},{9,8},{10,9... | collective-permute-start | bytes 49160 | tf_op jit(solution)/shard_map/ppermute | solution.py:374
  38.1 2.2 %collective-permute-done.8.cylow_hbm = f32[8,512]{1,0:T(8,128)S(1)} collective-permute-done((f32[8,512]{1,0:T(8,128)S(1)}, f32[8,512]{1,0:T(8,128)S(1)}, u32[]{:S(2)}, u32[]{:S(2)}) %collective-permute-start.8) | collective-permute-done | bytes 16416 | tf_op jit(solution)/shard_map/ppermute | solution.py:373
  40.4 0.0 copy-start.2
  40.4 0.0 collective-permute-done.9.cyhigh_hbm
  40.4 0.0 copy-start.3
  40.4 0.0 collective-permute-done.6.cnear_hbm
  40.4 0.0 copy-start
  40.4 0.0 collective-permute-done.7.cfar_hbm
  40.4 0.0 copy-start.1
  40.4 7.8 %all-to-all-done = f32[128,4,128]{2,1,0:T(4,128)S(1)} async-done(((f32[128,4,128]{2,1,0:T(4,128)}), f32[128,4,128]{2,1,0:T(4,128)S(1)}, u32[]{:S(2)}, u32[]{:S(2)}) %all-to-all-start) | async-done | bytes 262176 | tf_op jit(solution)/shard_map/all_to_all | solution.py:371
  48.2 0.0 copy-done.2
  48.2 0.0 copy-done.3
  48.2 0.0 copy-done
  48.3 0.0 copy-done.1
  48.3 3.4 %shard_map.58 = (f32[30,128]{1,0:T(8,128)S(1)}, f32[30,128]{1,0:T(8,128)S(1)}, f32[128,512]{1,0:T(8,128)S(1)}, f32[8,64,512]{2,1,0:T(8,128)S(1)}, f32[8,64,512]{...) custom-call(s32[3]{0:T(128)S(1)} %pad_add_fusion.core_ref.place_ref,, ...), custom_call_target="tpu_custom_call" | custom-call | tf_op jit(solution)/shard_map/pallas_call | solution.py:309
  51.7 2.0 %collective-permute-start.10 = (f32[30,128]{1,0:T(8,128)S(1)}, f32[30,128]{1,0:T(8,128)S(1)}, u32[]{:S(2)}, u32[]{:S(2)}) collective-permute-start(f32[30,128]{1,0:T(8,128)S(1)} %get-tuple-element.58), channel_id=1, source_target_pairs={{0,8},{8,0},{16,24},{24,16},{32,40},{40,32},{48,56},{56,48},{64,72... | collective-permute-start | bytes 46088 | tf_op jit(solution)/shard_map/ppermute | solution.py:332
  53.7 0.8 %collective-permute-done.10.other_ref = f32[30,128]{1,0:T(8,128)S(1)} collective-permute-done((f32[30,128]{1,0:T(8,128)S(1)}, f32[30,128]{1,0:T(8,128)S(1)}, u32[]{:S(2)}, u32[]{:S(2)}) %collective-permute-start.10) | collective-permute-done | bytes 15392 | tf_op jit(solution)/shard_map/ppermute | solution.py:332
  54.6 2.8 %shard_map.59 = f32[8,64,512]{2,1,0:T(8,128)} custom-call(s32[3]{0:T(128)S(1)} %pad_add_fusion.core_ref.place_ref, f32[30,128]{1,0:T(8,128)S(1)} %get-tuple-element.57.own_ref, f32[30,128]{1,0:T(8,128)S(1)} %collective-permute-done.10.other_ref, f32[128,512]{1,0:T(8,128)S(1)} %get-tuple-element.59.out_table_ref, f32[8,64,512]{2,1,0:T(8,128)S(1)} %get-tuple-element.60.c3_ref, ...), custom_call_target="tpu_custom_call" | custom-call | tf_op jit(solution)/shard_map/pallas_call | solution.py:309
  (4 shorter events, 0.0 us)
Async XLA Ops:
  3.1 6.2 %collective-permute-start.2 = (f32[2,512]{1,0:T(2,128)S(1)}, f32[2,512]{1,0:T(2,128)S(1)}, u32[]{:S(2)}, u32[]{:S(2)}) collective-permute-start(f32[2,512]{1,0:T(2,128)S(1)} %get-tuple-element.44), channel_id=1, source_target_pairs={{0,248},{8,16},{16,8},{24,32},{32,24},{40,48},{48,40},{56,64},{64,... | collective-permute-start | bytes 12296 | tf_op jit(solution)/shard_map/ppermute | solution.py:335
  5.9 4.3 %collective-permute-start.3 = (f32[2,512]{1,0:T(2,128)S(1)}, f32[2,512]{1,0:T(2,128)S(1)}, u32[]{:S(2)}, u32[]{:S(2)}) collective-permute-start(f32[2,512]{1,0:T(2,128)S(1)} %get-tuple-element.45), channel_id=1, source_target_pairs={{0,8},{8,0},{16,24},{24,16},{32,40},{40,32},{48,56},{56,48},{64,72... | collective-permute-start | bytes 12296 | tf_op jit(solution)/shard_map/ppermute | solution.py:332
  9.3 8.5 %collective-permute-start = (f32[3,64,512]{2,1,0:T(8,128)}, f32[3,64,512]{2,1,0:T(8,128)S(1)}, u32[]{:S(2)}, u32[]{:S(2)}) collective-permute-start(f32[3,64,512]{2,1,0:T(8,128)} %get-tuple-element.41), channel_id=1, source_target_pairs={{0,8},{8,0},{16,24},{24,16},{32,40},{40,32},{48,56},{56,48},{64,72... | collective-permute-start | bytes 1179656 | tf_op jit(solution)/shard_map/ppermute | solution.py:332
  9.4 8.5 %collective-permute-start.1 = (f32[3,64,512]{2,1,0:T(8,128)S(1)}, f32[3,64,512]{2,1,0:T(8,128)S(1)}, u32[]{:S(2)}, u32[]{:S(2)}) collective-permute-start(f32[3,64,512]{2,1,0:T(8,128)S(1)} %get-tuple-element.42), channel_id=1, source_target_pairs={{0,248},{8,16},{16,8},{24,32},{32,24},{40,48},{48,40},{56,64},{64,... | collective-permute-start | bytes 1179656 | tf_op jit(solution)/shard_map/ppermute | solution.py:335
  10.2 7.6 %collective-permute-start.4 = (f32[26,512]{1,0:T(8,128)S(1)}, f32[26,512]{1,0:T(8,128)S(1)}, u32[]{:S(2)}, u32[]{:S(2)}) collective-permute-start(f32[26,512]{1,0:T(8,128)S(1)} %pad_maximum_fusion), channel_id=1, source_target_pairs={{0,1},{1,2},{2,3},{3,4},{4,5},{5,6},{6,7},{7,0},{8,9},{9,10},{10,1... | collective-permute-start | bytes 159752 | tf_op jit(solution)/shard_map/ppermute | solution.py:352
  11.9 5.9 %collective-permute-start.5 = (f32[26,512]{1,0:T(8,128)S(1)}, f32[26,512]{1,0:T(8,128)S(1)}, u32[]{:S(2)}, u32[]{:S(2)}) collective-permute-start(f32[26,512]{1,0:T(8,128)S(1)} %pad_maximum_fusion.1), channel_id=1, source_target_pairs={{0,7},{1,0},{2,1},{3,2},{4,3},{5,4},{6,5},{7,6},{8,15},{9,8},{10,9... | collective-permute-start | bytes 159752 | tf_op jit(solution)/shard_map/ppermute | solution.py:353
  21.3 27.0 %all-to-all-start = ((f32[128,4,128]{2,1,0:T(4,128)}), f32[128,4,128]{2,1,0:T(4,128)S(1)}, u32[]{:S(2)}, u32[]{:S(2)}) async-start(f32[128,4,128]{2,1,0:T(4,128)} %get-tuple-element.47), calls=%async_computation | async-start | bytes 524288 | tf_op jit(solution)/shard_map/all_to_all | solution.py:371
  34.0 6.4 %collective-permute-start.6 = (f32[64,512]{1,0:T(8,128)S(1)}, f32[64,512]{1,0:T(8,128)S(1)}, u32[]{:S(2)}, u32[]{:S(2)}) collective-permute-start(f32[64,512]{1,0:T(8,128)S(1)} %get-tuple-element.53), channel_id=1, source_target_pairs={{0,8},{8,0},{16,24},{24,16},{32,40},{40,32},{48,56},{56,48},{64,72... | collective-permute-start | bytes 393224 | tf_op jit(solution)/shard_map/ppermute | solution.py:332
  34.6 5.8 %collective-permute-start.7 = (f32[64,512]{1,0:T(8,128)S(1)}, f32[64,512]{1,0:T(8,128)S(1)}, u32[]{:S(2)}, u32[]{:S(2)}) collective-permute-start(f32[64,512]{1,0:T(8,128)S(1)} %get-tuple-element.54), channel_id=1, source_target_pairs={{0,248},{8,16},{16,8},{24,32},{32,24},{40,48},{48,40},{56,64},{64,... | collective-permute-start | bytes 393224 | tf_op jit(solution)/shard_map/ppermute | solution.py:335
  35.5 4.9 %collective-permute-start.8 = (f32[8,512]{1,0:T(8,128)S(1)}, f32[8,512]{1,0:T(8,128)S(1)}, u32[]{:S(2)}, u32[]{:S(2)}) collective-permute-start(f32[8,512]{1,0:T(8,128)S(1)} %get-tuple-element.55), channel_id=1, source_target_pairs={{0,1},{1,2},{2,3},{3,4},{4,5},{5,6},{6,7},{7,0},{8,9},{9,10},{10,1... | collective-permute-start | bytes 49160 | tf_op jit(solution)/shard_map/ppermute | solution.py:373
  36.6 3.7 %collective-permute-start.9 = (f32[8,512]{1,0:T(8,128)S(1)}, f32[8,512]{1,0:T(8,128)S(1)}, u32[]{:S(2)}, u32[]{:S(2)}) collective-permute-start(f32[8,512]{1,0:T(8,128)S(1)} %get-tuple-element.56), channel_id=1, source_target_pairs={{0,7},{1,0},{2,1},{3,2},{4,3},{5,4},{6,5},{7,6},{8,15},{9,8},{10,9... | collective-permute-start | bytes 49160 | tf_op jit(solution)/shard_map/ppermute | solution.py:374
  40.4 7.9 %copy-start.2 = (f32[8,512]{1,0:T(8,128)}, f32[8,512]{1,0:T(8,128)S(1)}, u32[]{:S(2)}) copy-start(f32[8,512]{1,0:T(8,128)S(1)} %collective-permute-done.8.cylow_hbm) | copy-start | bytes 49156
  40.4 7.9 %copy-start.3 = (f32[8,512]{1,0:T(8,128)}, f32[8,512]{1,0:T(8,128)S(1)}, u32[]{:S(2)}) copy-start(f32[8,512]{1,0:T(8,128)S(1)} %collective-permute-done.9.cyhigh_hbm) | copy-start | bytes 49156
  40.4 7.9 %copy-start = (f32[64,512]{1,0:T(8,128)}, f32[64,512]{1,0:T(8,128)S(1)}, u32[]{:S(2)}) copy-start(f32[64,512]{1,0:T(8,128)S(1)} %collective-permute-done.6.cnear_hbm) | copy-start | bytes 393220
  40.4 7.8 %copy-start.1 = (f32[64,512]{1,0:T(8,128)}, f32[64,512]{1,0:T(8,128)S(1)}, u32[]{:S(2)}) copy-start(f32[64,512]{1,0:T(8,128)S(1)} %collective-permute-done.7.cfar_hbm) | copy-start | bytes 393220
  51.7 2.9 %collective-permute-start.10 = (f32[30,128]{1,0:T(8,128)S(1)}, f32[30,128]{1,0:T(8,128)S(1)}, u32[]{:S(2)}, u32[]{:S(2)}) collective-permute-start(f32[30,128]{1,0:T(8,128)S(1)} %get-tuple-element.58), channel_id=1, source_target_pairs={{0,8},{8,0},{16,24},{24,16},{32,40},{40,32},{48,56},{56,48},{64,72... | collective-permute-start | bytes 46088 | tf_op jit(solution)/shard_map/ppermute | solution.py:332

commit v3 on v2

v3 whole, which is shorter than its diff:
```python
import math

import jax
import jax.numpy as jnp
import numpy as np
from jax import lax
from jax.experimental import pallas as pl
from jax.experimental.pallas import tpu as pltpu
from jax.sharding import Mesh
from jax.sharding import PartitionSpec as P

screen = 0.02
w1 = 1.0 / (1.25 + 0.75 * math.cos(math.pi / 4.0))
w2 = 1.0 / (1.25 - 0.75 * math.cos(math.pi / 4.0))

BX, BY, NZ = 8, 64, 512
CX, CY, CZ = 32, 64, 64
GX, GY = 32, 8
CHIPS = GX // 2
ROWS = CY // 2
OUT_Y = BY // 8 + 2
OUT_X = 4

VMEM = pl.BlockSpec(memory_space=pltpu.VMEM)
SMEM = pl.BlockSpec(memory_space=pltpu.SMEM)
HBM = pl.BlockSpec(memory_space=pltpu.HBM)
F32 = jnp.float32


def basis():
    place = np.arange(CZ)
    columns, freq = [], []
    for k in range(CZ // 2 + 1):
        scale = math.sqrt((1.0 if k in (0, CZ // 2) else 2.0) / CZ)
        columns.append(scale * np.cos(2.0 * math.pi * k * place / CZ))
        freq.append(k)
    for k in range(1, CZ // 2):
        columns.append(math.sqrt(2.0 / CZ) * np.sin(2.0 * math.pi * k * place / CZ))
        freq.append(k)
    return np.stack(columns, 1), np.array(freq)


def symbol(length):
    return 2.0 - 2.0 * np.cos(2.0 * math.pi * np.arange(length) / length)


def tables():
    columns, freq = basis()
    spectrum = (
        screen
        + symbol(CX)[:, None, None]
        + symbol(CY)[None, :, None]
        + symbol(CZ)[freq][None, None, :]
    )
    green = np.real(np.fft.ifft2(1.0 / spectrum, axes=(0, 1)))
    t, d, h = np.meshgrid(np.arange(OUT_Y + 3), np.arange(GY), np.arange(2), indexing="ij")
    shift = (t - 4 - 8 * d - 4 * h) % CY
    table = green[: CX // 2 + 1][:, shift].reshape(CX // 2 + 1, OUT_Y + 3, GY, 2 * CZ)
    table = table.astype(np.float32)
    into = np.repeat(columns, NZ // CZ, axis=0).astype(np.float32)
    out = np.concatenate([into.T, into.T], 0) / 8.0
    return table, into, out.astype(np.float32)


def zsum(v):
    return pltpu.roll(v, 1, 1) + pltpu.roll(v, NZ - 1, 1)


def shifted_sum(v, low, high):
    size = v.shape[0]
    row = lax.broadcasted_iota(jnp.int32, v.shape, 0)
    before = jnp.where(row == 0, low, pltpu.roll(v, 1, 0))
    after = jnp.where(row == size - 1, high, pltpu.roll(v, size - 1, 0))
    return before + after


def fetch(pairs, sems, first=0):
    copies = [pltpu.make_async_copy(s, d, sems.at[first + i]) for i, (s, d) in enumerate(pairs)]
    for copy in copies:
        copy.start()
    return copies


def wait(copies):
    for copy in copies:
        copy.wait()


def strip_kernel(core_ref, cot_ref, coef_ref, tnear_ref, tfar_ref, ylow_ref, yhigh_ref):
    core = core_ref[0]
    for side, out in ((0, ylow_ref), (1, yhigh_ref)):
        order = (0, 1, 2) if side == 0 else (7, 6, 5)
        cot = [cot_ref[side, :, r, :] for r in order]
        inverse = [1.0 / (6.0 + coef_ref[side, :, r, :]) for r in order]
        w5 = [w2 * v * i for v, i in zip(cot, inverse)]
        none = jnp.zeros((1, NZ), F32)
        kept = (1.0 - w2) * cot[0] + w5[1]
        out[0:8, :] = w5[0]
        out[8:16, :] = inverse[0]
        out[16:24, :] = kept
        c4 = (1.0 - w2) * cot[1] + w5[0] + w5[2] + zsum(w5[1]) + shifted_sum(w5[1], none, none)
        out[24:32, :] = w1 * inverse[1] * c4
        out[32:33, :] = inverse[1][0:1, :]
        out[33:34, :] = inverse[1][7:8, :]

        def corner(edge, inner):
            at = slice(edge, edge + 1)
            return w5[0][at], inverse[0][at], kept[at] + w5[0][inner : inner + 1], w5[1][at]

        for i, (low, high) in enumerate(zip(corner(0, 1), corner(BX - 1, BX - 2))):
            place = slice(4 * side + i, 4 * side + i + 1)
            tnear_ref[place, :] = jnp.where(core == 0, high, low)
            tfar_ref[place, :] = jnp.where(core == 0, low, high)


def edge_kernel(core_ref, cot_hbm, coef_hbm, near_ref, far_ref, cot_strip_ref, coef_strip_ref, cot_ref, coef_ref, sems):
    core = core_ref[0]
    pairs = []
    for hbm, ref, strip in ((cot_hbm, cot_ref, cot_strip_ref), (coef_hbm, coef_ref, coef_strip_ref)):
        pairs += [(hbm.at[pl.ds((BX - 2) * i, 2)], ref.at[pl.ds(2 * i, 2)]) for i in range(2)]
        pairs += [(hbm.at[:, pl.ds((BY - 8) * i, 8), :], strip.at[i]) for i in range(2)]
    copies = fetch(pairs, sems)
    wait(copies[0:2] + copies[4:6])
    for out, edge, step in (
        (far_ref, 3 * core, 1 - 2 * core),
        (near_ref, 3 * (1 - core), 2 * core - 1),
    ):
        cot = cot_ref[edge]
        inverse = 1.0 / (6.0 + coef_ref[edge])
        out[0] = w2 * cot * inverse
        out[1] = inverse
        out[2] = (1.0 - w2) * cot + w2 * cot_ref[edge + step] / (6.0 + coef_ref[edge + step])
    wait(copies[2:4] + copies[6:8])


def local_kernel(cot_ref, coef_ref, w5_ref, inverse_ref, c4_ref):
    for x in range(BX):
        inverse = 1.0 / (6.0 + coef_ref[x])
        inverse_ref[x] = inverse
        w5_ref[x] = w2 * cot_ref[x] * inverse
    none = jnp.zeros((1, NZ), F32)
    for x in range(BX):
        w5 = w5_ref[x]
        c4 = (1.0 - w2) * cot_ref[x] + zsum(w5) + shifted_sum(w5, none, none)
        if x > 0:
            c4 = c4 + w5_ref[x - 1]
        if x < BX - 1:
            c4 = c4 + w5_ref[x + 1]
        c4_ref[x] = c4


def first_kernel(
    core_ref, w5_ref, inverse_ref, part_ref, near_ref, far_ref, ylow_ref, yhigh_ref, into_ref,
    rows_ref, cnear_ref, cfar_ref, send_ref, c3_hbm, base_hbm, inverse_hbm, planes_hbm,
    halo_ref, w4_ref, base_ref, c3_ref, sems,
):
    core = core_ref[0]
    copies = fetch(
        [
            (inverse_ref, inverse_hbm),
            (near_ref.at[1], planes_hbm.at[1 - core]),
            (far_ref.at[1], planes_hbm.at[core]),
        ],
        sems,
    )
    for halo, side, at_high in ((near_ref, 1 - core, core == 0), (far_ref, core, core == 1)):
        halo_ref[side] = halo[0]
        low = jnp.where(at_high, ylow_ref[36:37, :], ylow_ref[32:33, :])
        high = jnp.where(at_high, yhigh_ref[36:37, :], yhigh_ref[32:33, :])
        w5 = halo[0]
        c4 = halo[2] + w5_ref[(BX - 1) * side] + zsum(w5) + shifted_sum(w5, low, high)
        w4_ref[(BX + 1) * side] = w1 * halo[1] * c4
    row = lax.broadcasted_iota(jnp.int32, (8, NZ), 0)
    for x in range(BX):
        low = jnp.where(row == 0, ylow_ref[x : x + 1, :], 0.0)
        high = jnp.where(row == 7, yhigh_ref[x : x + 1, :], 0.0)
        part = part_ref[x]
        c4 = jnp.concatenate([part[0:8, :] + low, part[8 : BY - 8, :], part[BY - 8 : BY, :] + high], 0)
        if x == 0:
            c4 = c4 + halo_ref[0]
        if x == BX - 1:
            c4 = c4 + halo_ref[1]
        w4 = w1 * inverse_ref[x] * c4
        w4_ref[x + 1] = w4
        base_ref[x] = w5_ref[x] + w4
        c3_ref[x] = c4
        copies += fetch([(base_ref.at[x], base_hbm.at[x])], sems, 3 + x)
    y4 = []
    for side, packet, edge in ((0, ylow_ref, 0), (1, yhigh_ref, BY - 1)):
        w5, corners = packet[0:8, :], packet[32:40, :]
        inverse = packet[8:16, :]
        c4 = packet[16:24, :] + w5_ref[:, edge, :] + zsum(w5)
        c4 = c4 + shifted_sum(w5, corners[0:1, :], corners[4:5, :])
        w4 = w1 * inverse * c4
        y4.append(w4)
        beside = zsum(corners)
        ends = []
        for i, at, x_side in ((0, 0, 0), (4, BX - 1, 1)):
            c4_corner = corners[i + 2 : i + 3, :] + beside[i : i + 1, :] + w5[at : at + 1, :]
            c4_corner = c4_corner + halo_ref[x_side, edge : edge + 1, :]
            ends.append(w1 * corners[i + 1 : i + 2, :] * c4_corner)
        beyond = packet[24:32, :]
        beyond = beyond + jnp.where(row == 0, w1 * packet[40:41, :] * corners[3:4, :], 0.0)
        beyond = beyond + jnp.where(row == BX - 1, w1 * packet[41:42, :] * corners[7:8, :], 0.0)
        c3 = (1.0 - w1) * c4 + beyond + w4_ref[1 : BX + 1, edge, :] + zsum(w4) + shifted_sum(w4, *ends)
        rows_ref[side] = c3
        rows_ref[2 + side] = inverse
    total = jnp.zeros((BY, NZ), F32)
    for x in range(BX):
        w4 = w4_ref[x + 1]
        c3 = (1.0 - w1) * c3_ref[x] + w4_ref[x] + w4_ref[x + 2] + zsum(w4)
        c3 = c3 + shifted_sum(w4, y4[0][x : x + 1, :], y4[1][x : x + 1, :])
        c3_ref[x] = c3
        copies += fetch([(c3_ref.at[x], c3_hbm.at[x])], sems, 3 + BX + x)
        total = total + c3
    sums = jnp.sum(total.reshape(BY // 8, 8, NZ), axis=1)
    modes = jnp.dot(sums, into_ref[...], precision=lax.Precision.HIGHEST, preferred_element_type=F32)
    packed = jnp.concatenate([modes[0:4, :], modes[4:8, :]], axis=1)
    send_ref[...] = jnp.broadcast_to(packed[None], send_ref.shape)
    cnear_ref[...] = c3_ref[(BX - 1) * (1 - core)]
    cfar_ref[...] = c3_ref[(BX - 1) * core]
    wait(copies)


def coarse_kernel(place_ref, got_ref, table_ref, own_ref, other_ref, rolled_ref):
    core, chip, gy = place_ref[0], place_ref[1], place_ref[2]
    turn = lax.rem(GY - gy, GY)
    for q in range(CHIPS):
        plane = lax.rem(chip + (1 - 2 * core) * q + CHIPS, CHIPS)
        for r in range(4):
            rolled_ref[q, r] = pltpu.roll(got_ref[plane, pl.ds(r, GY, stride=4), :], turn, 0)
    for m in range(-1, OUT_X - 1):
        at_distance = {}
        for q in range(CHIPS):
            away = (m - 2 * q) % CX
            at_distance.setdefault(min(away, CX - away), []).append(q)
        totals = [jnp.zeros((8, 2 * CZ), F32)] * OUT_Y
        for away, planes in at_distance.items():
            source = [sum(rolled_ref[q, r] for q in planes[1:]) + rolled_ref[planes[0], r] for r in range(4)]
            weight = [table_ref[away, t] for t in range(OUT_Y + 3)]
            for j in range(OUT_Y):
                for r in range(4):
                    totals[j] = totals[j] + weight[j + 3 - r] * source[r]
        for j in range(OUT_Y):
            total = jnp.sum(totals[j], axis=0, keepdims=True)
            if m < OUT_X - 2:
                at = (m + 1) * OUT_Y + j
                own_ref[at : at + 1, :] = total
            if m > -1:
                at = (OUT_X - 2 - m) * OUT_Y + j
                other_ref[at : at + 1, :] = total


def last_kernel(
    core_ref, own_ref, other_ref, out_table_ref, c3_ref, base_ref, inverse_ref, planes_ref, rows_ref, cnear_ref, cfar_ref,
    out_hbm, w_ref, out_ref, sems,
):
    core = core_ref[0]
    modes = own_ref[...] + other_ref[...]
    coarse = jnp.dot(modes, out_table_ref[...], precision=lax.Precision.HIGHEST, preferred_element_type=F32)
    outer, middle, inner = (coarse[m * OUT_Y : (m + 1) * OUT_Y, :] for m in range(3))
    low = jnp.where(core == 0, outer, inner)
    high = jnp.where(core == 0, inner, outer)

    def rows_of(plane):
        return jnp.concatenate([jnp.broadcast_to(plane[j : j + 1, :], (8, NZ)) for j in range(1, OUT_Y - 1)], 0)

    def side_sum(plane, fine):
        return shifted_sum(fine, plane[0:1, :], plane[OUT_Y - 1 : OUT_Y, :]) + zsum(fine)

    s, s_low, s_high = rows_of(middle), rows_of(low), rows_of(high)
    beside = side_sum(middle, s)
    for side, fine, plane in ((0, s_low, low), (1, s_high, high)):
        beyond = jnp.where((core == 0) == (side == 1), cnear_ref[...], cfar_ref[...])
        value = beyond + fine + s + side_sum(plane, fine)
        w_ref[(BX + 1) * side] = w2 * (planes_ref[side] * value - fine)
    y_w = []
    for side, edge, near_edge in ((0, 0, 1), (1, OUT_Y - 1, OUT_Y - 2)):
        fine = jnp.broadcast_to(middle[edge : edge + 1, :], (BX, NZ))
        value = rows_ref[side] + fine + middle[near_edge : near_edge + 1, :] + zsum(fine)
        value = value + shifted_sum(fine, low[edge : edge + 1, :], high[edge : edge + 1, :])
        y_w.append(w2 * (rows_ref[2 + side] * value - fine))
    for x in range(BX):
        around = beside + (s_low if x == 0 else s) + (s_high if x == BX - 1 else s)
        w_ref[x + 1] = w2 * (inverse_ref[x] * (c3_ref[x] + around) - s)
    copies = []
    for x in range(BX):
        w = w_ref[x + 1]
        near = w_ref[x] + w_ref[x + 2] + zsum(w)
        near = near + shifted_sum(w, y_w[0][x : x + 1, :], y_w[1][x : x + 1, :])
        out_ref[x] = base_ref[x] + s + w + w1 * ((1.0 - w2) / w2 * w + inverse_ref[x] * near)
        copies += fetch([(out_ref.at[x], out_hbm.at[x])], sems, x)
    wait(copies)


def call(kernel, outs, ins, in_specs, out_specs, scratch=(), sems=0, cost=None, aliases=None):
    scratch = [pltpu.VMEM(shape, F32) for shape in scratch]
    if sems:
        scratch.append(pltpu.SemaphoreType.DMA((sems,)))
    ins = [
        x if spec is SMEM else pltpu.with_memory_space_constraint(x, spec.memory_space)
        for x, spec in zip(ins, in_specs)
    ]
    return pl.pallas_call(
        kernel,
        out_shape=[spec.memory_space(shape, F32) for shape, spec in zip(outs, out_specs)],
        in_specs=in_specs,
        out_specs=out_specs,
        scratch_shapes=scratch,
        cost_estimate=cost,
        input_output_aliases=aliases or {},
        compiler_params=pltpu.CompilerParams(vmem_limit_bytes=12 * 1024 * 1024),
    )(*ins)


def hold_kernel(*refs):
    pass


def body(cotangent, coefficient):
    table, into, out_table = tables()
    along_x = ("x", "y", "core")
    core = lax.axis_index("core")
    place = jnp.stack([core, lax.axis_index("x") * 4 + lax.axis_index("y"), lax.axis_index("gy")])
    place = place.astype(jnp.int32)
    near_pairs = [(i, i ^ 1) for i in range(GX)]
    far_pairs = [(i, (i + 1) % GX if i % 2 else (i - 1) % GX) for i in range(GX)]
    up = [(i, (i + 1) % GY) for i in range(GY)]
    down = [(i, (i - 1) % GY) for i in range(GY)]

    def near_swap(v):
        return lax.ppermute(v, along_x, near_pairs)

    def far_swap(v):
        return lax.ppermute(v, along_x, far_pairs)

    brick, plane = (BX, BY, NZ), (BY, NZ)
    strips = (2, BX, 8, NZ)
    near, far, cot_strips, coef_strips = call(
        edge_kernel,
        [(3,) + plane, (3,) + plane, strips, strips],
        [place, cotangent, coefficient],
        [SMEM, HBM, HBM],
        [VMEM] * 4,
        scratch=[(4,) + plane, (4,) + plane],
        sems=8,
    )
    far, near = far_swap(far), near_swap(near)
    tiny_near, tiny_far, y_low, y_high = call(
        strip_kernel,
        [(8, NZ), (8, NZ), (34, NZ), (34, NZ)],
        [place, cot_strips, coef_strips],
        [SMEM, VMEM, VMEM],
        [VMEM] * 4,
        cost=pl.CostEstimate(flops=40 * BX * BY * NZ, bytes_accessed=5 * 4 * BX * BY * NZ, transcendentals=0),
    )
    tiny_near, tiny_far = near_swap(tiny_near), far_swap(tiny_far)
    corner_low = jnp.where(core == 0, tiny_far, tiny_near)
    corner_high = jnp.where(core == 0, tiny_near, tiny_far)
    y_low = jnp.concatenate([y_low[:32], corner_low[:4], corner_high[:4], y_low[32:]], 0)
    y_high = jnp.concatenate([y_high[:32], corner_low[4:], corner_high[4:], y_high[32:]], 0)
    from_low = lax.ppermute(y_high, "gy", up)
    from_high = lax.ppermute(y_low, "gy", down)
    w5, inverse, part = call(
        local_kernel,
        [brick, brick, brick],
        [cotangent, coefficient],
        [VMEM] * 2,
        [VMEM] * 3,
        cost=pl.CostEstimate(flops=40 * BX * BY * NZ, bytes_accessed=5 * 4 * BX * BY * NZ, transcendentals=0),
    )
    rows, c_near, c_far, send, c3, base, inverse, planes = call(
        first_kernel,
        [(4, BX, NZ), plane, plane, (CHIPS * GY, 4, 2 * CZ), brick, brick, brick, (2,) + plane],
        [place, w5, inverse, part, near, far, from_low, from_high, jnp.asarray(into)],
        [SMEM] + [VMEM] * 8,
        [VMEM] * 4 + [HBM] * 4,
        scratch=[(2,) + plane, (BX + 2,) + plane, brick, brick],
        sems=2 * BX + 3,
    )
    got = lax.all_to_all(send, ("x", "y", "gy"), 0, 0, tiled=True)
    c_near, c_far = near_swap(c_near), far_swap(c_far)
    table = jnp.asarray(table)
    got, c3, base, inverse, planes = call(
        hold_kernel,
        [got.shape, brick, brick, brick, (2,) + plane],
        [got, c3, base, inverse, planes, table],
        [VMEM] + [HBM] * 4 + [VMEM],
        [VMEM] + [HBM] * 4,
        aliases={i: i for i in range(5)},
    )
    own, other = call(
        coarse_kernel,
        [(3 * OUT_Y, 2 * CZ)] * 2,
        [place, got.reshape(CHIPS, ROWS, 2 * CZ), table],
        [SMEM, VMEM, VMEM],
        [VMEM] * 2,
        scratch=[(CHIPS, 4, GY, 2 * CZ)],
        cost=pl.CostEstimate(flops=10**11, bytes_accessed=10**7, transcendentals=0),
    )
    other = near_swap(other)
    return call(
        last_kernel,
        [brick],
        [place, own, other, jnp.asarray(out_table), c3, base, inverse, planes, rows, c_near, c_far],
        [SMEM] + [VMEM] * 10,
        [HBM],
        scratch=[(BX + 2,) + plane, brick],
        sems=BX,
    )[0]


def solution(mesh):
    split = Mesh(np.asarray(mesh.devices).reshape(4, 4, 2, GY), ("x", "y", "core", "gy"))
    spec = P(("x", "y", "core"), "gy", None)
    return jax.shard_map(body, mesh=split, in_specs=(spec, spec), out_specs=spec, check_vma=False)
```

time: 57.6 us -> 55.8 us (0.969)
  waiting for transfers between devices: 12.7 us -> 16.1 us
  starting transfers between devices: 30.9 us -> 27.5 us
  Pallas kernels: 13.5 us -> 11.7 us
    all_to_all x1, waiting for transfers between devices: 7.82 us -> 13.2 us  [body(): got = lax.all_to_all(send, ('x', 'y', 'gy'), 0, 0, tiled=True)]
    ppermute x2 -> x0, starting transfers between devices: 2.68 us -> none  [the longest x1 1.49 us: body(): c_from_high = lax.ppermute(cy_low, 'gy', down)]
    ppermute x2 -> x0, waiting for transfers between devices: 2.24 us -> none  [the longest x1 2.24 us: body(): c_from_low = lax.ppermute(cy_high, 'gy', up)]
    pallas_call x5 -> x7, Pallas kernels: 13.5 us -> 11.7 us  [call(): pl.pallas_call(kernel, out_shape=[spec.memory_space(shape, F32) for shape...]
  transfers between devices with their start and end apart: 12 -> 10, of which waited for: 5 -> 4; matrix products, arithmetic and copies ran while one was open for 0% -> 0% of each run, Pallas kernels for 2% -> 3%
where the time goes in v3:
time: 55.8 us; the launch traced here: 55.7 us
  starting transfers between devices  27.5 us (49%)
  waiting for transfers between devices  16.1 us (29%)
  Pallas kernels  11.7 us (21%)
    all_to_all x1, waiting for transfers between devices, body(): got = lax.all_to_all(send, ('x', 'y', 'gy'), 0, 0, tiled=True)  13.2 us
    all_to_all x1, starting transfers between devices, body(): got = lax.all_to_all(send, ('x', 'y', 'gy'), 0, 0, tiled=True)  12.6 us
    pallas_call x7, Pallas kernels, call(): pl.pallas_call(kernel, out_shape=[spec.memory_space(shape, F32) for shape...  11.7 us
    ppermute x4, starting transfers between devices, near_swap(): return lax.ppermute(v, along_x, near_pairs)  5.58 us
    ppermute x1, starting transfers between devices, body(): from_high = lax.ppermute(y_low, 'gy', down)  4.03 us
    ppermute x3, starting transfers between devices, far_swap(): return lax.ppermute(v, along_x, far_pairs)  3.62 us
    ppermute x1, starting transfers between devices, body(): from_low = lax.ppermute(y_high, 'gy', up)  1.71 us
    ppermute x4, waiting for transfers between devices, near_swap(): return lax.ppermute(v, along_x, near_pairs)  1.61 us
  transfers between devices with their start and end apart: 10, of which 4 were waited for; matrix products, arithmetic and copies ran while one was open for 0% of the time, Pallas kernels for 3%

profile of v3, /device:TPU:1, one launch (start us, length us, event | category | flops | bytes accessed | tf_op | source)
XLA Modules:
  0.0 55.7 jit_solution(9557368513621446604)
XLA Ops:
  0.0 0.1 pad_add_fusion.core_ref.place_ref
  0.1 0.0 copy-start.1
  0.1 2.7 %shard_map.56 = (f32[3,64,512]{2,1,0:T(8,128)}, f32[3,64,512]{2,1,0:T(8,128)S(1)}, f32[2,8,8,512]{3,2,1,0:T(8,128)S(1)}, f32[2,8,8,512]{3,2,1,0:T(8,128)S(1)}) custom-call(s32[3]{0:T(128)S(1)} %pad_add_fusion.core_ref.place_ref, f32[8,64,512]{2,1,0:T(8,128)} %cot_hbm.1, f32[8,64,512]{2,1,0:T(8,128)} %coef_hbm.1), custom_call_target="tpu_custom_call" | custom-call | tf_op jit(solution)/shard_map/pallas_call | solution.py:304
  2.8 0.0 copy-start
  2.8 0.7 %shard_map.57 = (f32[8,512]{1,0:T(8,128)S(1)}, f32[8,512]{1,0:T(8,128)S(1)}, f32[34,512]{1,0:T(8,128)S(1)}, f32[34,512]{1,0:T(8,128)S(1)}) custom-call(s32[3]{0:T(128)S(1)} %pad_add_fusion.core_ref.place_ref, f32[2,8,8,512]{3,2,1,0:T(8,128)S(1)} %get-tuple-element.36.cot_ref, f32[2,8,8,512]{3,2,1,0:T(8,128)S(1)} %get-tuple-element.37.coef_ref), custom_call_target="tpu_custom_call" | custom-call | flops 10485760 | bytes 5242880 | tf_op jit(solution)/shard_map/pallas_call | solution.py:304
  3.5 2.8 %collective-permute-start.2 = (f32[8,512]{1,0:T(8,128)S(1)}, f32[8,512]{1,0:T(8,128)S(1)}, u32[]{:S(2)}, u32[]{:S(2)}) collective-permute-start(f32[8,512]{1,0:T(8,128)S(1)} %get-tuple-element.39), channel_id=1, source_target_pairs={{0,248},{8,16},{16,8},{24,32},{32,24},{40,48},{48,40},{56,64},{64,... | collective-permute-start | bytes 49160 | tf_op jit(solution)/shard_map/ppermute | solution.py:335
  6.3 3.5 %collective-permute-start.3 = (f32[8,512]{1,0:T(8,128)S(1)}, f32[8,512]{1,0:T(8,128)S(1)}, u32[]{:S(2)}, u32[]{:S(2)}) collective-permute-start(f32[8,512]{1,0:T(8,128)S(1)} %get-tuple-element.40), channel_id=1, source_target_pairs={{0,8},{8,0},{16,24},{24,16},{32,40},{40,32},{48,56},{56,48},{64,72... | collective-permute-start | bytes 49160 | tf_op jit(solution)/shard_map/ppermute | solution.py:332
  9.7 0.0 collective-permute-start
  9.7 0.0 collective-permute-start.1
  9.8 0.0 collective-permute-done.2
  9.8 0.8 %collective-permute-done.3 = f32[8,512]{1,0:T(8,128)S(1)} collective-permute-done((f32[8,512]{1,0:T(8,128)S(1)}, f32[8,512]{1,0:T(8,128)S(1)}, u32[]{:S(2)}, u32[]{:S(2)}) %collective-permute-start.3) | collective-permute-done | bytes 16416 | tf_op jit(solution)/shard_map/ppermute | solution.py:332
  10.6 1.7 %collective-permute-start.4 = (f32[42,512]{1,0:T(8,128)S(1)}, f32[42,512]{1,0:T(8,128)S(1)}, u32[]{:S(2)}, u32[]{:S(2)}) collective-permute-start(f32[42,512]{1,0:T(8,128)S(1)} %pad_maximum_fusion), channel_id=1, source_target_pairs={{0,1},{1,2},{2,3},{3,4},{4,5},{5,6},{6,7},{7,0},{8,9},{9,10},{10,1... | collective-permute-start | bytes 258056 | tf_op jit(solution)/shard_map/ppermute | solution.py:362
  12.3 0.0 copy-start.7
  12.3 4.0 %collective-permute-start.5 = (f32[42,512]{1,0:T(8,128)S(1)}, f32[42,512]{1,0:T(8,128)S(1)}, u32[]{:S(2)}, u32[]{:S(2)}) collective-permute-start(f32[42,512]{1,0:T(8,128)S(1)} %pad_maximum_fusion.1), channel_id=1, source_target_pairs={{0,7},{1,0},{2,1},{3,2},{4,3},{5,4},{6,5},{7,6},{8,15},{9,8},{10,9... | collective-permute-start | bytes 258056 | tf_op jit(solution)/shard_map/ppermute | solution.py:363
  16.4 0.0 copy-done.1
  16.4 0.0 copy-done
  16.4 0.9 %shard_map.55 = (f32[8,64,512]{2,1,0:T(8,128)S(1)}, f32[8,64,512]{2,1,0:T(8,128)S(1)}, f32[8,64,512]{2,1,0:T(8,128)S(1)}) custom-call(f32[8,64,512]{2,1,0:T(8,128)S(1)} %copy-done, f32[8,64,512]{2,1,0:T(8,128)S(1)} %copy-done.1), custom_call_target="tpu_custom_call" | custom-call | flops 10485760 | bytes 5242880 | tf_op jit(solution)/shard_map/pallas_call | solution.py:304
  17.3 1.3 %collective-permute-done.4.ylow_ref = f32[42,512]{1,0:T(8,128)S(1)} collective-permute-done((f32[42,512]{1,0:T(8,128)S(1)}, f32[42,512]{1,0:T(8,128)S(1)}, u32[]{:S(2)}, u32[]{:S(2)}) %collective-permute-start.4) | collective-permute-done | bytes 86048 | tf_op jit(solution)/shard_map/ppermute | solution.py:362
  18.6 0.0 collective-permute-done.5.yhigh_ref
  18.6 0.0 collective-permute-done.near_ref
  18.6 0.0 collective-permute-done.1.far_ref
  18.6 0.0 copy-done.7
  18.6 0.0 copy-start.6
  18.6 3.6 %shard_map.58 = (f32[4,8,512]{2,1,0:T(8,128)S(1)}, f32[64,512]{1,0:T(8,128)S(1)}, f32[64,512]{1,0:T(8,128)S(1)}, f32[128,4,128]{2,1,0:T(4,128)}, f32[8,64,512]{2...) custom-call(s32[3]{0:T(128)S(1)} %pad_add_fusion.core_ref.place_ref, ...), custom_call_target="tpu_custom_call" | custom-call | tf_op jit(solution)/shard_map/pallas_call | solution.py:304
  22.2 12.6 %all-to-all-start = ((f32[128,4,128]{2,1,0:T(4,128)}), f32[128,4,128]{2,1,0:T(4,128)S(1)}, u32[]{:S(2)}, u32[]{:S(2)}) async-start(f32[128,4,128]{2,1,0:T(4,128)} %get-tuple-element.42), calls=%async_computation | async-start | bytes 524288 | tf_op jit(solution)/shard_map/all_to_all | solution.py:381
  34.8 0.4 collective-permute-start.7
  35.2 0.8 %collective-permute-start.8 = (f32[64,512]{1,0:T(8,128)S(1)}, f32[64,512]{1,0:T(8,128)S(1)}, u32[]{:S(2)}, u32[]{:S(2)}) collective-permute-start(f32[64,512]{1,0:T(8,128)S(1)} %get-tuple-element.56), channel_id=1, source_target_pairs={{0,248},{8,16},{16,8},{24,32},{32,24},{40,48},{48,40},{56,64},{64,... | collective-permute-start | bytes 393224 | tf_op jit(solution)/shard_map/ppermute | solution.py:335
  36.0 13.2 %all-to-all-done.refs_0_ = f32[128,4,128]{2,1,0:T(4,128)S(1)} async-done(((f32[128,4,128]{2,1,0:T(4,128)}), f32[128,4,128]{2,1,0:T(4,128)S(1)}, u32[]{:S(2)}, u32[]{:S(2)}) %all-to-all-start) | async-done | bytes 262176 | tf_op jit(solution)/shard_map/all_to_all | solution.py:381
  49.2 0.0 copy-done.6
  49.2 0.0 copy-start.2
  49.2 0.0 copy-start.3
  49.2 0.0 copy-start.4
  49.2 0.0 copy-start.5
  49.2 0.0 copy-start.8
  49.2 1.0 %shard_map.60 = (f32[30,128]{1,0:T(8,128)S(1)}, f32[30,128]{1,0:T(8,128)S(1)}) custom-call(s32[3]{0:T(128)S(1)} %pad_add_fusion.core_ref.place_ref, f32[16,32,128]{2,1,0:T(8,128)S(1)} %bitcast.4, f32[17,13,8,128]{3,2,1,0:T(8,128)S(1)} %copy-done.6), custom_call_target="tpu_custom_call" | custom-call | flops 99999997952 | bytes 10000000 | tf_op jit(solution)/shard_map/pallas_call | solution.py:304
  50.3 1.7 %collective-permute-start.6 = (f32[30,128]{1,0:T(8,128)S(1)}, f32[30,128]{1,0:T(8,128)S(1)}, u32[]{:S(2)}, u32[]{:S(2)}) collective-permute-start(f32[30,128]{1,0:T(8,128)S(1)} %get-tuple-element.49), channel_id=1, source_target_pairs={{0,8},{8,0},{16,24},{24,16},{32,40},{40,32},{48,56},{56,48},{64,72... | collective-permute-start | bytes 46088 | tf_op jit(solution)/shard_map/ppermute | solution.py:332
  52.0 0.0 collective-permute-done.7.cnear_ref
  52.0 0.0 collective-permute-done.8.cfar_ref
  52.0 0.8 %collective-permute-done.6.other_ref = f32[30,128]{1,0:T(8,128)S(1)} collective-permute-done((f32[30,128]{1,0:T(8,128)S(1)}, f32[30,128]{1,0:T(8,128)S(1)}, u32[]{:S(2)}, u32[]{:S(2)}) %collective-permute-start.6) | collective-permute-done | bytes 15392 | tf_op jit(solution)/shard_map/ppermute | solution.py:332
  52.8 0.0 copy-done.2
  52.8 0.0 copy-done.3
  52.8 0.0 copy-done.4
  52.8 0.0 copy-done.5
  52.8 0.0 copy-done.8
  52.9 2.8 %shard_map.61 = f32[8,64,512]{2,1,0:T(8,128)} custom-call(s32[3]{0:T(128)S(1)} %pad_add_fusion.core_ref.place_ref, f32[30,128]{1,0:T(8,128)S(1)} %get-tuple-element.48.own_ref, f32[30,128]{1,0:T(8,128)S(1)} %collective-permute-done.6.other_ref, f32[128,512]{1,0:T(8,128)S(1)} %copy-done.8, f32[8,64,512]{2,1,0:T(8,128)S(1)} %copy-done.2, ...), custom_call_target="tpu_custom_call" | custom-call | tf_op jit(solution)/shard_map/pallas_call | solution.py:304
  (9 shorter events, 0.1 us)
Async XLA Ops:
  0.1 16.3 %copy-start.1 = (f32[8,64,512]{2,1,0:T(8,128)S(1)}, f32[8,64,512]{2,1,0:T(8,128)}, u32[]{:S(2)}) copy-start(f32[8,64,512]{2,1,0:T(8,128)} %coef_hbm.1) | copy-start | bytes 3145732
  2.8 13.6 %copy-start = (f32[8,64,512]{2,1,0:T(8,128)S(1)}, f32[8,64,512]{2,1,0:T(8,128)}, u32[]{:S(2)}) copy-start(f32[8,64,512]{2,1,0:T(8,128)} %cot_hbm.1) | copy-start | bytes 3145732
  3.5 6.3 %collective-permute-start.2 = (f32[8,512]{1,0:T(8,128)S(1)}, f32[8,512]{1,0:T(8,128)S(1)}, u32[]{:S(2)}, u32[]{:S(2)}) collective-permute-start(f32[8,512]{1,0:T(8,128)S(1)} %get-tuple-element.39), channel_id=1, source_target_pairs={{0,248},{8,16},{16,8},{24,32},{32,24},{40,48},{48,40},{56,64},{64,... | collective-permute-start | bytes 49160 | tf_op jit(solution)/shard_map/ppermute | solution.py:335
  6.3 4.3 %collective-permute-start.3 = (f32[8,512]{1,0:T(8,128)S(1)}, f32[8,512]{1,0:T(8,128)S(1)}, u32[]{:S(2)}, u32[]{:S(2)}) collective-permute-start(f32[8,512]{1,0:T(8,128)S(1)} %get-tuple-element.40), channel_id=1, source_target_pairs={{0,8},{8,0},{16,24},{24,16},{32,40},{40,32},{48,56},{56,48},{64,72... | collective-permute-start | bytes 49160 | tf_op jit(solution)/shard_map/ppermute | solution.py:332
  9.7 8.8 %collective-permute-start = (f32[3,64,512]{2,1,0:T(8,128)}, f32[3,64,512]{2,1,0:T(8,128)S(1)}, u32[]{:S(2)}, u32[]{:S(2)}) collective-permute-start(f32[3,64,512]{2,1,0:T(8,128)} %get-tuple-element.34), channel_id=1, source_target_pairs={{0,8},{8,0},{16,24},{24,16},{32,40},{40,32},{48,56},{56,48},{64,72... | collective-permute-start | bytes 1179656 | tf_op jit(solution)/shard_map/ppermute | solution.py:332
  9.7 8.8 %collective-permute-start.1 = (f32[3,64,512]{2,1,0:T(8,128)S(1)}, f32[3,64,512]{2,1,0:T(8,128)S(1)}, u32[]{:S(2)}, u32[]{:S(2)}) collective-permute-start(f32[3,64,512]{2,1,0:T(8,128)S(1)} %get-tuple-element.35), channel_id=1, source_target_pairs={{0,248},{8,16},{16,8},{24,32},{32,24},{40,48},{48,40},{56,64},{64,... | collective-permute-start | bytes 1179656 | tf_op jit(solution)/shard_map/ppermute | solution.py:335
  10.6 8.0 %collective-permute-start.4 = (f32[42,512]{1,0:T(8,128)S(1)}, f32[42,512]{1,0:T(8,128)S(1)}, u32[]{:S(2)}, u32[]{:S(2)}) collective-permute-start(f32[42,512]{1,0:T(8,128)S(1)} %pad_maximum_fusion), channel_id=1, source_target_pairs={{0,1},{1,2},{2,3},{3,4},{4,5},{5,6},{6,7},{7,0},{8,9},{9,10},{10,1... | collective-permute-start | bytes 258056 | tf_op jit(solution)/shard_map/ppermute | solution.py:362
  12.3 6.2 %copy-start.7 = (f32[512,64]{1,0:T(8,128)S(1)}, f32[512,64]{1,0:T(8,128)}, u32[]{:S(2)}) copy-start(f32[512,64]{1,0:T(8,128)} %constant.28.clone.into_ref) | copy-start | bytes 393220
  12.3 6.2 %collective-permute-start.5 = (f32[42,512]{1,0:T(8,128)S(1)}, f32[42,512]{1,0:T(8,128)S(1)}, u32[]{:S(2)}, u32[]{:S(2)}) collective-permute-start(f32[42,512]{1,0:T(8,128)S(1)} %pad_maximum_fusion.1), channel_id=1, source_target_pairs={{0,7},{1,0},{2,1},{3,2},{4,3},{5,4},{6,5},{7,6},{8,15},{9,8},{10,9... | collective-permute-start | bytes 258056 | tf_op jit(solution)/shard_map/ppermute | solution.py:363
  18.6 30.6 %copy-start.6 = (f32[17,13,8,128]{3,2,1,0:T(8,128)S(1)}, f32[17,13,8,128]{3,2,1,0:T(8,128)}, u32[]{:S(2)}) copy-start(f32[17,13,8,128]{3,2,1,0:T(8,128)} %constant.29.clone.refs_5_.table_ref) | copy-start | bytes 2715652
  22.2 27.0 %all-to-all-start = ((f32[128,4,128]{2,1,0:T(4,128)}), f32[128,4,128]{2,1,0:T(4,128)S(1)}, u32[]{:S(2)}, u32[]{:S(2)}) async-start(f32[128,4,128]{2,1,0:T(4,128)} %get-tuple-element.42), calls=%async_computation | async-start | bytes 524288 | tf_op jit(solution)/shard_map/all_to_all | solution.py:381
  34.8 17.2 %collective-permute-start.7 = (f32[64,512]{1,0:T(8,128)S(1)}, f32[64,512]{1,0:T(8,128)S(1)}, u32[]{:S(2)}, u32[]{:S(2)}) collective-permute-start(f32[64,512]{1,0:T(8,128)S(1)} %get-tuple-element.55), channel_id=1, source_target_pairs={{0,8},{8,0},{16,24},{24,16},{32,40},{40,32},{48,56},{56,48},{64,72... | collective-permute-start | bytes 393224 | tf_op jit(solution)/shard_map/ppermute | solution.py:332
  35.2 16.8 %collective-permute-start.8 = (f32[64,512]{1,0:T(8,128)S(1)}, f32[64,512]{1,0:T(8,128)S(1)}, u32[]{:S(2)}, u32[]{:S(2)}) collective-permute-start(f32[64,512]{1,0:T(8,128)S(1)} %get-tuple-element.56), channel_id=1, source_target_pairs={{0,248},{8,16},{16,8},{24,32},{32,24},{40,48},{48,40},{56,64},{64,... | collective-permute-start | bytes 393224 | tf_op jit(solution)/shard_map/ppermute | solution.py:335
  49.2 3.7 %copy-start.2 = (f32[8,64,512]{2,1,0:T(8,128)S(1)}, f32[8,64,512]{2,1,0:T(8,128)}, u32[]{:S(2)}) copy-start(f32[8,64,512]{2,1,0:T(8,128)} %get-tuple-element.50.c3_ref) | copy-start | bytes 3145732
  49.2 3.7 %copy-start.3 = (f32[8,64,512]{2,1,0:T(8,128)S(1)}, f32[8,64,512]{2,1,0:T(8,128)}, u32[]{:S(2)}) copy-start(f32[8,64,512]{2,1,0:T(8,128)} %get-tuple-element.51.base_ref) | copy-start | bytes 3145732
  49.2 3.7 %copy-start.4 = (f32[8,64,512]{2,1,0:T(8,128)S(1)}, f32[8,64,512]{2,1,0:T(8,128)}, u32[]{:S(2)}) copy-start(f32[8,64,512]{2,1,0:T(8,128)} %get-tuple-element.52.inverse_ref) | copy-start | bytes 3145732
  49.2 3.7 %copy-start.5 = (f32[2,64,512]{2,1,0:T(8,128)S(1)}, f32[2,64,512]{2,1,0:T(8,128)}, u32[]{:S(2)}) copy-start(f32[2,64,512]{2,1,0:T(8,128)} %get-tuple-element.53.planes_ref) | copy-start | bytes 786436
  49.2 3.7 %copy-start.8 = (f32[128,512]{1,0:T(8,128)S(1)}, f32[128,512]{1,0:T(8,128)}, u32[]{:S(2)}) copy-start(f32[128,512]{1,0:T(8,128)} %constant.30.clone.out_table_ref) | copy-start | bytes 786436
  50.3 2.6 %collective-permute-start.6 = (f32[30,128]{1,0:T(8,128)S(1)}, f32[30,128]{1,0:T(8,128)S(1)}, u32[]{:S(2)}, u32[]{:S(2)}) collective-permute-start(f32[30,128]{1,0:T(8,128)S(1)} %get-tuple-element.49), channel_id=1, source_target_pairs={{0,8},{8,0},{16,24},{24,16},{32,40},{40,32},{48,56},{56,48},{64,72... | collective-permute-start | bytes 46088 | tf_op jit(solution)/shard_map/ppermute | solution.py:332

commit v4 on v3

v4 whole, which is shorter than its diff:
```python
import math

import jax
import jax.numpy as jnp
import numpy as np
from jax import lax
from jax.experimental import pallas as pl
from jax.experimental.pallas import tpu as pltpu
from jax.sharding import Mesh
from jax.sharding import PartitionSpec as P

screen = 0.02
w1 = 1.0 / (1.25 + 0.75 * math.cos(math.pi / 4.0))
w2 = 1.0 / (1.25 - 0.75 * math.cos(math.pi / 4.0))

BX, BY, NZ = 8, 64, 512
CX, CY, CZ = 32, 64, 64
GX, GY = 32, 8
MATES = 4
GROUPS = GX // MATES
ROWS = CY // 2
OUT_Y = BY // 8 + 2
OUT_X = MATES + 2

VMEM = pl.BlockSpec(memory_space=pltpu.VMEM)
SMEM = pl.BlockSpec(memory_space=pltpu.SMEM)
HBM = pl.BlockSpec(memory_space=pltpu.HBM)
F32 = jnp.float32


def basis():
    place = np.arange(CZ)
    columns, freq = [], []
    for k in range(CZ // 2 + 1):
        scale = math.sqrt((1.0 if k in (0, CZ // 2) else 2.0) / CZ)
        columns.append(scale * np.cos(2.0 * math.pi * k * place / CZ))
        freq.append(k)
    for k in range(1, CZ // 2):
        columns.append(math.sqrt(2.0 / CZ) * np.sin(2.0 * math.pi * k * place / CZ))
        freq.append(k)
    return np.stack(columns, 1), np.array(freq)


def symbol(length):
    return 2.0 - 2.0 * np.cos(2.0 * math.pi * np.arange(length) / length)


def tables():
    columns, freq = basis()
    spectrum = (
        screen
        + symbol(CX)[:, None, None]
        + symbol(CY)[None, :, None]
        + symbol(CZ)[freq][None, None, :]
    )
    green = np.real(np.fft.ifft2(1.0 / spectrum, axes=(0, 1)))
    t, d, h = np.meshgrid(np.arange(OUT_Y + 3), np.arange(GY), np.arange(2), indexing="ij")
    shift = (t - 4 - 8 * d - 4 * h) % CY
    table = green[: CX // 2 + 1][:, shift].reshape(CX // 2 + 1, OUT_Y + 3, GY, 2 * CZ)
    table = table.astype(np.float32)
    into = np.repeat(columns, NZ // CZ, axis=0).astype(np.float32)
    out = np.concatenate([into.T, into.T], 0) / 8.0
    return table, into, out.astype(np.float32)


def zsum(v):
    return pltpu.roll(v, 1, 1) + pltpu.roll(v, NZ - 1, 1)


def shifted_sum(v, low, high):
    size = v.shape[0]
    row = lax.broadcasted_iota(jnp.int32, v.shape, 0)
    before = jnp.where(row == 0, low, pltpu.roll(v, 1, 0))
    after = jnp.where(row == size - 1, high, pltpu.roll(v, size - 1, 0))
    return before + after


def fetch(pairs, sems, first=0):
    copies = [pltpu.make_async_copy(s, d, sems.at[first + i]) for i, (s, d) in enumerate(pairs)]
    for copy in copies:
        copy.start()
    return copies


def wait(copies):
    for copy in copies:
        copy.wait()


def strip_kernel(core_ref, cot_hbm, coef_hbm, tnear_ref, tfar_ref, ylow_ref, yhigh_ref, cot_ref, coef_ref, sems):
    core = core_ref[0]
    ends = (pl.ds(0, 8), pl.ds(BY - 8, 8))
    wait(
        fetch(
            [(hbm.at[:, ends[i], :], ref.at[i]) for i in range(2) for hbm, ref in ((cot_hbm, cot_ref), (coef_hbm, coef_ref))],
            sems,
        )
    )
    for side, out in ((0, ylow_ref), (1, yhigh_ref)):
        order = (0, 1, 2) if side == 0 else (7, 6, 5)
        cot = [cot_ref[side, :, r, :] for r in order]
        inverse = [1.0 / (6.0 + coef_ref[side, :, r, :]) for r in order]
        w5 = [w2 * v * i for v, i in zip(cot, inverse)]
        none = jnp.zeros((1, NZ), F32)
        kept = (1.0 - w2) * cot[0] + w5[1]
        out[0:8, :] = w5[0]
        out[8:16, :] = inverse[0]
        out[16:24, :] = kept
        c4 = (1.0 - w2) * cot[1] + w5[0] + w5[2] + zsum(w5[1]) + shifted_sum(w5[1], none, none)
        out[24:32, :] = w1 * inverse[1] * c4
        out[32:33, :] = inverse[1][0:1, :]
        out[33:34, :] = inverse[1][7:8, :]

        def corner(edge, inner):
            at = slice(edge, edge + 1)
            return w5[0][at], inverse[0][at], kept[at] + w5[0][inner : inner + 1], w5[1][at]

        for i, (low, high) in enumerate(zip(corner(0, 1), corner(BX - 1, BX - 2))):
            place = slice(4 * side + i, 4 * side + i + 1)
            tnear_ref[place, :] = jnp.where(core == 0, high, low)
            tfar_ref[place, :] = jnp.where(core == 0, low, high)


def edge_kernel(core_ref, cot_ref, coef_ref, after_ref, near_ref, far_ref):
    core = core_ref[0]
    for out, edge, step in (
        (far_ref, (BX - 1) * core, 1 - 2 * core),
        (near_ref, (BX - 1) * (1 - core), 2 * core - 1),
    ):
        cot = cot_ref[edge]
        inverse = 1.0 / (6.0 + coef_ref[edge])
        out[0] = w2 * cot * inverse
        out[1] = inverse
        out[2] = (1.0 - w2) * cot + w2 * cot_ref[edge + step] / (6.0 + coef_ref[edge + step])


def local_kernel(
    cot_ref, coef_ref,
    w5_edges_ref, inverse_edges_ref, c3_edges_ref, rows_ref, sums_ref, c3_ref, base_hbm, inverse_hbm,
    w5_ref, inverse_ref, w4_ref, base_ref, sems,
):
    none = jnp.zeros((1, NZ), F32)
    for x in range(BX):
        inverse = 1.0 / (6.0 + coef_ref[x])
        inverse_ref[x] = inverse
        w5_ref[x] = w2 * cot_ref[x] * inverse
    copies = fetch([(inverse_ref, inverse_hbm)], sems)
    for x in range(BX):
        w5 = w5_ref[x]
        c4 = (1.0 - w2) * cot_ref[x] + zsum(w5) + shifted_sum(w5, none, none)
        if x > 0:
            c4 = c4 + w5_ref[x - 1]
        if x < BX - 1:
            c4 = c4 + w5_ref[x + 1]
        w4 = w1 * inverse_ref[x] * c4
        w4_ref[x] = w4
        base_ref[x] = w5 + w4
        c3_ref[x] = (1.0 - w1) * c4
    copies += fetch([(base_ref, base_hbm)], sems, 1)
    total = jnp.zeros((BY, NZ), F32)
    for x in range(BX):
        w4 = w4_ref[x]
        c3 = c3_ref[x] + zsum(w4) + shifted_sum(w4, none, none)
        if x > 0:
            c3 = c3 + w4_ref[x - 1]
        if x < BX - 1:
            c3 = c3 + w4_ref[x + 1]
        c3_ref[x] = c3
        total = total + c3
    sums_ref[...] = jnp.sum(total.reshape(BY // 8, 8, NZ), axis=1)
    for side, x, y in ((0, 0, 0), (1, BX - 1, BY - 1)):
        w5_edges_ref[side] = w5_ref[x]
        inverse_edges_ref[side] = inverse_ref[x]
        c3_edges_ref[side] = c3_ref[x]
        rows_ref[side] = w5_ref[:, y, :]
        rows_ref[2 + side] = inverse_ref[:, y, :]
        rows_ref[4 + side] = w4_ref[:, y, :]
    wait(copies)


def with_ends(plane, row, ends):
    low = jnp.where(row == 0, ends[0], jnp.where(row == 1, ends[1], 0.0))
    high = jnp.where(row == 6, ends[2], jnp.where(row == 7, ends[3], 0.0))
    return jnp.concatenate([plane[0:8, :] + low, plane[8 : BY - 8, :], plane[BY - 8 : BY, :] + high], 0)


def first_kernel(
    core_ref, w5_edges_ref, inverse_edges_ref, c3_edges_ref, own_rows_ref, part_sums_ref,
    near_ref, far_ref, ylow_ref, yhigh_ref, into_ref,
    rows_ref, cnear_ref, cfar_ref, send_ref, added_ref, planes_hbm,
    sems,
):
    core = core_ref[0]
    copies = fetch(
        [
            (near_ref.at[1], planes_hbm.at[1 - core]),
            (far_ref.at[1], planes_hbm.at[core]),
        ],
        sems,
    )
    none = jnp.zeros((1, NZ), F32)
    row = lax.broadcasted_iota(jnp.int32, (8, NZ), 0)
    plane_total = jnp.zeros((BY, NZ), F32)
    for halo, side, at_high in ((near_ref, 1 - core, core == 0), (far_ref, core, core == 1)):
        low = jnp.where(at_high, ylow_ref[36:37, :], ylow_ref[32:33, :])
        high = jnp.where(at_high, yhigh_ref[36:37, :], yhigh_ref[32:33, :])
        w5 = halo[0]
        c4 = halo[2] + w5_edges_ref[side] + zsum(w5) + shifted_sum(w5, low, high)
        w4_added = w1 * inverse_edges_ref[side] * w5
        c3_added = (1.0 - w1) * w5 + w1 * halo[1] * c4 + zsum(w4_added) + shifted_sum(w4_added, none, none)
        added_ref[side, 0] = c3_added
        added_ref[side, 1] = w4_added
        plane_total = plane_total + c3_added + w4_added
    sums = part_sums_ref[...] + jnp.sum(plane_total.reshape(BY // 8, 8, NZ), axis=1)
    for side, packet, edge in ((0, ylow_ref, 0), (1, yhigh_ref, BY - 1)):
        w5, corners, inverse = packet[0:8, :], packet[32:40, :], packet[8:16, :]
        c4 = packet[16:24, :] + own_rows_ref[side] + zsum(w5)
        c4 = c4 + shifted_sum(w5, corners[0:1, :], corners[4:5, :])
        w4 = w1 * inverse * c4
        w4_added = w1 * own_rows_ref[2 + side] * w5
        c3_added = (1.0 - w1) * w5 + w4 + zsum(w4_added) + shifted_sum(w4_added, none, none)
        beside = zsum(corners)
        ends = []
        inner = own_rows_ref[4 + side] + w4_added
        beyond = packet[24:32, :]
        for i, at, x_side in ((0, 0, 0), (4, BX - 1, 1)):
            halo = jnp.where(
                (core == 0) == (x_side == 0), far_ref[0, edge : edge + 1, :], near_ref[0, edge : edge + 1, :]
            )
            c4_corner = corners[i + 2 : i + 3, :] + beside[i : i + 1, :] + w5[at : at + 1, :] + halo
            ends.append(w1 * corners[i + 1 : i + 2, :] * c4_corner)
            missing = w1 * packet[40 + x_side : 41 + x_side, :] * corners[i + 3 : i + 4, :]
            missing = missing + added_ref[x_side, 1, edge : edge + 1, :]
            beyond = beyond + jnp.where(row == at, missing, 0.0)
        rows_ref[side] = (1.0 - w1) * c4 + beyond + inner + zsum(w4) + shifted_sum(w4, *ends)
        rows_ref[2 + side] = inverse
        rows_ref[4 + side] = c3_added
        rows_ref[6 + side] = w4_added
        more = jnp.sum(c3_added + w4_added, axis=0, keepdims=True)
        sums = sums + jnp.where(row == 7 * side, more, 0.0)
    modes = jnp.dot(sums, into_ref[...], precision=lax.Precision.HIGHEST, preferred_element_type=F32)
    packed = jnp.concatenate([modes[0:4, :], modes[4:8, :]], axis=1)
    send_ref[...] = jnp.broadcast_to(packed[None], send_ref.shape)
    edges = []
    for side, x in ((0, 0), (1, BX - 1)):
        at = slice(x, x + 1)
        ends = (rows_ref[4, at, :], rows_ref[6, at, :], rows_ref[7, at, :], rows_ref[5, at, :])
        edges.append(with_ends(c3_edges_ref[side] + added_ref[side, 0], row, ends))
    cnear_ref[...] = jnp.where(core == 0, edges[1], edges[0])
    cfar_ref[...] = jnp.where(core == 0, edges[0], edges[1])
    wait(copies)


def coarse_kernel(place_ref, got_ref, table_ref, own_ref, one_ref, two_ref, three_ref, rolled_ref, sums_ref):
    mate, group, gy = place_ref[1], place_ref[2], place_ref[3]
    turn = lax.rem(GY - gy, GY)
    for q in range(GROUPS):
        plane = lax.rem(group + q, GROUPS)
        for r in range(4):
            rolled_ref[q, r] = pltpu.roll(got_ref[plane, pl.ds(r, GY, stride=4), :], turn, 0)
    for m in range(OUT_X):
        totals = [jnp.zeros((8, 2 * CZ), F32)] * OUT_Y
        for q in range(GROUPS):
            away = jnp.abs(m - 1 - mate - MATES * q)
            away = jnp.minimum(away, jnp.abs(CX - away))
            source = [rolled_ref[q, r] for r in range(4)]
            weight = [table_ref[away, t] for t in range(OUT_Y + 3)]
            for j in range(OUT_Y):
                for r in range(4):
                    totals[j] = totals[j] + weight[j + 3 - r] * source[r]
        for j in range(OUT_Y):
            sums_ref[m, j : j + 1, :] = jnp.sum(totals[j], axis=0, keepdims=True)
    for flip, out in enumerate((own_ref, one_ref, two_ref, three_ref)):
        first = lax.bitwise_xor(mate, flip)
        for m in range(3):
            out[m * OUT_Y : (m + 1) * OUT_Y, :] = sums_ref[first + m]


def last_kernel(
    core_ref, own_ref, one_ref, two_ref, three_ref, out_table_ref, c3_ref, base_ref, inverse_ref, planes_ref, added_ref, rows_ref, cnear_ref, cfar_ref,
    out_hbm, w_ref, out_ref, sems,
):
    core = core_ref[0]
    modes = (own_ref[...] + one_ref[...]) + (two_ref[...] + three_ref[...])
    coarse = jnp.dot(modes, out_table_ref[...], precision=lax.Precision.HIGHEST, preferred_element_type=F32)
    low, middle, high = (coarse[m * OUT_Y : (m + 1) * OUT_Y, :] for m in range(3))

    def rows_of(plane):
        return jnp.concatenate([jnp.broadcast_to(plane[j : j + 1, :], (8, NZ)) for j in range(1, OUT_Y - 1)], 0)

    def side_sum(plane, fine):
        return shifted_sum(fine, plane[0:1, :], plane[OUT_Y - 1 : OUT_Y, :]) + zsum(fine)

    s, s_low, s_high = rows_of(middle), rows_of(low), rows_of(high)
    beside = side_sum(middle, s)
    row = lax.broadcasted_iota(jnp.int32, (8, NZ), 0)
    none = jnp.zeros((1, NZ), F32)
    added_at = {0: (0, 0), 1: (0, 1), BX - 2: (1, 1), BX - 1: (1, 0)}
    for side, fine, plane in ((0, s_low, low), (1, s_high, high)):
        beyond = jnp.where((core == 0) == (side == 1), cnear_ref[...], cfar_ref[...])
        value = beyond + fine + s + side_sum(plane, fine)
        w_ref[(BX + 1) * side] = w2 * (planes_ref[side] * value - fine)
    y_w = []
    for side, edge, near_edge in ((0, 0, 1), (1, OUT_Y - 1, OUT_Y - 2)):
        fine = jnp.broadcast_to(middle[edge : edge + 1, :], (BX, NZ))
        value = rows_ref[side] + fine + middle[near_edge : near_edge + 1, :] + zsum(fine)
        value = value + shifted_sum(fine, low[edge : edge + 1, :], high[edge : edge + 1, :])
        y_w.append(w2 * (rows_ref[2 + side] * value - fine))
    for x in range(BX):
        around = beside + (s_low if x == 0 else s) + (s_high if x == BX - 1 else s)
        at = slice(x, x + 1)
        ends = (rows_ref[4, at, :], rows_ref[6, at, :], rows_ref[7, at, :], rows_ref[5, at, :])
        c3 = with_ends(c3_ref[x], row, ends)
        if x in added_at:
            c3 = c3 + added_ref[added_at[x]]
        w_ref[x + 1] = w2 * (inverse_ref[x] * (c3 + around) - s)
    copies = []
    for x in range(BX):
        w = w_ref[x + 1]
        near = w_ref[x] + w_ref[x + 2] + zsum(w)
        near = near + shifted_sum(w, y_w[0][x : x + 1, :], y_w[1][x : x + 1, :])
        base = with_ends(base_ref[x], row, (rows_ref[6, x : x + 1, :], none, none, rows_ref[7, x : x + 1, :]))
        if x in (0, BX - 1):
            base = base + added_ref[0 if x == 0 else 1, 1]
        out_ref[x] = base + s + w + w1 * ((1.0 - w2) / w2 * w + inverse_ref[x] * near)
        copies += fetch([(out_ref.at[x], out_hbm.at[x])], sems, x)
    wait(copies)


def call(kernel, outs, ins, in_specs, out_specs, scratch=(), sems=0, cost=None, aliases=None):
    scratch = [pltpu.VMEM(shape, F32) for shape in scratch]
    if sems:
        scratch.append(pltpu.SemaphoreType.DMA((sems,)))
    ins = [
        x if spec is SMEM else pltpu.with_memory_space_constraint(x, spec.memory_space)
        for x, spec in zip(ins, in_specs)
    ]
    return pl.pallas_call(
        kernel,
        out_shape=[spec.memory_space(shape, F32) for shape, spec in zip(outs, out_specs)],
        in_specs=in_specs,
        out_specs=out_specs,
        scratch_shapes=scratch,
        cost_estimate=cost,
        input_output_aliases=aliases or {},
        compiler_params=pltpu.CompilerParams(vmem_limit_bytes=12 * 1024 * 1024),
    )(*ins)


def hold_kernel(*refs):
    pass


def body(cotangent, coefficient):
    table, into, out_table = tables()
    along_x = ("x", "pair", "chip", "core")
    core = lax.axis_index("core")
    mate = lax.axis_index("chip") * 2 + core
    place = jnp.stack([core, mate, lax.axis_index("x") * 2 + lax.axis_index("pair"), lax.axis_index("gy")])
    place = place.astype(jnp.int32)
    near_pairs = [(i, i ^ 1) for i in range(GX)]
    far_pairs = [(i, (i + 1) % GX if i % 2 else (i - 1) % GX) for i in range(GX)]
    up = [(i, (i + 1) % GY) for i in range(GY)]
    down = [(i, (i - 1) % GY) for i in range(GY)]

    def near_swap(v):
        return lax.ppermute(v, along_x, near_pairs)

    def far_swap(v):
        return lax.ppermute(v, along_x, far_pairs)

    brick, plane = (BX, BY, NZ), (BY, NZ)
    tiny_near, tiny_far, y_low, y_high = call(
        strip_kernel,
        [(8, NZ), (8, NZ), (34, NZ), (34, NZ)],
        [place, cotangent, coefficient],
        [SMEM, HBM, HBM],
        [VMEM] * 4,
        scratch=[(2, BX, 8, NZ), (2, BX, 8, NZ)],
        sems=4,
    )
    near, far = call(
        edge_kernel,
        [(3,) + plane, (3,) + plane],
        [place, cotangent, coefficient, y_low],
        [SMEM, VMEM, VMEM, VMEM],
        [VMEM] * 2,
    )
    tiny_far, tiny_near = far_swap(tiny_far), near_swap(tiny_near)
    far, near = far_swap(far), near_swap(near)
    corner_low = jnp.where(core == 0, tiny_far, tiny_near)
    corner_high = jnp.where(core == 0, tiny_near, tiny_far)
    y_low = jnp.concatenate([y_low[:32], corner_low[:4], corner_high[:4], y_low[32:]], 0)
    y_high = jnp.concatenate([y_high[:32], corner_low[4:], corner_high[4:], y_high[32:]], 0)
    from_low = lax.ppermute(y_high, "gy", up)
    from_high = lax.ppermute(y_low, "gy", down)
    edge_planes = (2,) + plane
    w5_edges, inverse_edges, c3_edges, own_rows, sums, c3, base, inverse = call(
        local_kernel,
        [edge_planes, edge_planes, edge_planes, (6, BX, NZ), (8, NZ), brick, brick, brick],
        [cotangent, coefficient],
        [VMEM] * 2,
        [VMEM] * 6 + [HBM] * 2,
        scratch=[brick] * 4,
        sems=2,
        cost=pl.CostEstimate(flops=40 * BX * BY * NZ, bytes_accessed=5 * 4 * BX * BY * NZ, transcendentals=0),
    )
    rows, c_near, c_far, send, added, planes = call(
        first_kernel,
        [(8, BX, NZ), plane, plane, (GROUPS * GY, 4, 2 * CZ), (2,) + edge_planes, edge_planes],
        [place, w5_edges, inverse_edges, c3_edges, own_rows, sums, near, far, from_low, from_high, jnp.asarray(into)],
        [SMEM] + [VMEM] * 10,
        [VMEM] * 5 + [HBM],
        sems=2,
    )
    got = lax.all_to_all(send, ("x", "pair", "gy"), 0, 0, tiled=True)
    c_near, c_far = near_swap(c_near), far_swap(c_far)
    table = jnp.asarray(table)
    got, c3, base, inverse, planes = call(
        hold_kernel,
        [got.shape, brick, brick, brick, edge_planes],
        [got, c3, base, inverse, planes, table],
        [VMEM] + [HBM] * 4 + [VMEM],
        [VMEM] + [HBM] * 4,
        aliases={i: i for i in range(5)},
    )
    own, one, two, three = call(
        coarse_kernel,
        [(3 * OUT_Y, 2 * CZ)] * 4,
        [place, got.reshape(GROUPS, ROWS, 2 * CZ), table],
        [SMEM, VMEM, VMEM],
        [VMEM] * 4,
        scratch=[(GROUPS, 4, GY, 2 * CZ), (OUT_X, OUT_Y, 2 * CZ)],
        cost=pl.CostEstimate(flops=10**11, bytes_accessed=10**7, transcendentals=0),
    )
    one, two, three = (
        lax.ppermute(v, along_x, [(i, i ^ flip) for i in range(GX)]) for flip, v in ((1, one), (2, two), (3, three))
    )
    return call(
        last_kernel,
        [brick],
        [place, own, one, two, three, jnp.asarray(out_table), c3, base, inverse, planes, added, rows, c_near, c_far],
        [SMEM] + [VMEM] * 13,
        [HBM],
        scratch=[(BX + 2,) + plane, brick],
        sems=BX,
    )[0]


def solution(mesh):
    split = Mesh(np.asarray(mesh.devices).reshape(4, 2, 2, 2, GY), ("x", "pair", "chip", "core", "gy"))
    spec = P(("x", "pair", "chip", "core"), "gy", None)
    return jax.shard_map(body, mesh=split, in_specs=(spec, spec), out_specs=spec, check_vma=False)
```

time: 55.8 us -> 53.2 us (0.953)
  waiting for transfers between devices: 16.1 us -> 11.9 us
  local copies, waits for them, and re-layouts: 0.07 us -> 1.03 us
  Pallas kernels: 11.7 us -> 12.3 us
    ppermute x0 -> x3, starting transfers between devices: none -> 5.19 us  [body(): lax.ppermute(v, along_x, [(i, i ^ flip) for i in range(GX)])]
    all_to_all x1, starting transfers between devices: 12.6 us -> 7.58 us  [body(): got = lax.all_to_all(send, ('x', 'pair', 'gy'), 0, 0, tiled=True)]
    all_to_all x1, waiting for transfers between devices: 13.2 us -> 8.81 us  [body(): got = lax.all_to_all(send, ('x', 'pair', 'gy'), 0, 0, tiled=True)]
    ppermute x0 -> x3, waiting for transfers between devices: none -> 1.7 us  [body(): lax.ppermute(v, along_x, [(i, i ^ flip) for i in range(GX)])]
    ppermute x1, starting transfers between devices: 1.71 us -> 0.08 us  [body(): from_low = lax.ppermute(y_high, 'gy', up)]
    ppermute x1, starting transfers between devices: 4.03 us -> 5.65 us  [body(): from_high = lax.ppermute(y_low, 'gy', down)]
    ppermute x4 -> x3, waiting for transfers between devices: 1.61 us -> 0.01 us  [near_swap(): return lax.ppermute(v, along_x, near_pairs)]
    unnamed x18 -> x20, local copies, waits for them, and re-layouts: 0.05 us -> 1 us
  transfers between devices with their start and end apart: 10 -> 12, of which waited for: 4 -> 4; matrix products, arithmetic and copies ran while one was open for 0% -> 0% of each run, Pallas kernels for 3% -> 9%
where the time goes in v4:
time: 53.2 us; the launch traced here: 53.1 us
  starting transfers between devices  27.5 us (52%)
  Pallas kernels  12.3 us (23%)
  waiting for transfers between devices  11.9 us (22%)
  local copies, waits for them, and re-layouts  1.03 us (2%)
    pallas_call x7, Pallas kernels, call(): pl.pallas_call(kernel, out_shape=[spec.memory_space(shape, F32) for shape...  12.3 us
    all_to_all x1, waiting for transfers between devices, body(): got = lax.all_to_all(send, ('x', 'pair', 'gy'), 0, 0, tiled=True)  8.81 us
    all_to_all x1, starting transfers between devices, body(): got = lax.all_to_all(send, ('x', 'pair', 'gy'), 0, 0, tiled=True)  7.58 us
    ppermute x3, starting transfers between devices, near_swap(): return lax.ppermute(v, along_x, near_pairs)  5.82 us
    ppermute x1, starting transfers between devices, body(): from_high = lax.ppermute(y_low, 'gy', down)  5.65 us
    ppermute x3, starting transfers between devices, body(): lax.ppermute(v, along_x, [(i, i ^ flip) for i in range(GX)])  5.19 us
    ppermute x3, starting transfers between devices, far_swap(): return lax.ppermute(v, along_x, far_pairs)  3.22 us
    ppermute x3, waiting for transfers between devices, body(): lax.ppermute(v, along_x, [(i, i ^ flip) for i in range(GX)])  1.7 us
  transfers between devices with their start and end apart: 12, of which 4 were waited for; matrix products, arithmetic and copies ran while one was open for 0% of the time, Pallas kernels for 9%

profile of v4, /device:TPU:1, one launch (start us, length us, event | category | flops | bytes accessed | tf_op | source)
XLA Modules:
  0.0 53.1 jit_solution(6086814272317431820)
XLA Ops:
  0.0 0.1 pad_add_fusion.core_ref.place_ref
  0.1 0.0 copy-start
  0.1 1.9 %shard_map.56 = (f32[8,512]{1,0:T(8,128)S(1)}, f32[8,512]{1,0:T(8,128)S(1)}, f32[34,512]{1,0:T(8,128)S(1)}, f32[34,512]{1,0:T(8,128)S(1)}) custom-call(s32[4]{0:T(128)S(1)} %pad_add_fusion.core_ref.place_ref, f32[8,64,512]{2,1,0:T(8,128)} %cot_ref.3, f32[8,64,512]{2,1,0:T(8,128)} %coef_ref.3), custom_call_target="tpu_custom_call" | custom-call | tf_op jit(solution)/shard_map/pallas_call | solution.py:338
  2.0 2.8 %collective-permute-start.2 = (f32[8,512]{1,0:T(8,128)S(1)}, f32[8,512]{1,0:T(8,128)S(1)}, u32[]{:S(2)}, u32[]{:S(2)}) collective-permute-start(f32[8,512]{1,0:T(8,128)S(1)} %get-tuple-element.43), channel_id=1, source_target_pairs={{0,248},{8,16},{16,8},{24,32},{32,24},{40,48},{48,40},{56,64},{64,... | collective-permute-start | bytes 49160 | tf_op jit(solution)/shard_map/ppermute | solution.py:370
  4.7 3.5 %collective-permute-start.3 = (f32[8,512]{1,0:T(8,128)S(1)}, f32[8,512]{1,0:T(8,128)S(1)}, u32[]{:S(2)}, u32[]{:S(2)}) collective-permute-start(f32[8,512]{1,0:T(8,128)S(1)} %get-tuple-element.44), channel_id=1, source_target_pairs={{0,8},{8,0},{16,24},{24,16},{32,40},{40,32},{48,56},{56,48},{64,72... | collective-permute-start | bytes 49160 | tf_op jit(solution)/shard_map/ppermute | solution.py:367
  8.2 0.0 copy-done
  8.2 0.0 copy-done.1
  8.2 1.3 %shard_map.57 = (f32[3,64,512]{2,1,0:T(8,128)}, f32[3,64,512]{2,1,0:T(8,128)S(1)}) custom-call(s32[4]{0:T(128)S(1)} %pad_add_fusion.core_ref.place_ref, f32[8,64,512]{2,1,0:T(8,128)S(1)} %copy-done, f32[8,64,512]{2,1,0:T(8,128)S(1)} %copy-done.1, f32[34,512]{1,0:T(8,128)S(1)} %get-tuple-element.39.after_ref), custom_call_target="tpu_custom_call" | custom-call | tf_op jit(solution)/shard_map/pallas_call | solution.py:338
  9.6 0.0 collective-permute-start
  9.6 0.0 collective-permute-start.1
  9.6 0.0 collective-permute-done.2
  9.6 0.0 collective-permute-done.3
  9.7 5.7 %collective-permute-start.5 = (f32[42,512]{1,0:T(8,128)S(1)}, f32[42,512]{1,0:T(8,128)S(1)}, u32[]{:S(2)}, u32[]{:S(2)}) collective-permute-start(f32[42,512]{1,0:T(8,128)S(1)} %pad_maximum_fusion.1), channel_id=1, source_target_pairs={{0,7},{1,0},{2,1},{3,2},{4,3},{5,4},{6,5},{7,6},{8,15},{9,8},{10,9... | collective-permute-start | bytes 258056 | tf_op jit(solution)/shard_map/ppermute | solution.py:396
  15.4 0.0 copy-start.9
  15.4 0.1 collective-permute-start.4
  15.5 2.4 %shard_map.55 = (f32[2,64,512]{2,1,0:T(8,128)S(1)}, f32[2,64,512]{2,1,0:T(8,128)S(1)}, f32[2,64,512]{2,1,0:T(8,128)S(1)}, f32[6,8,512]{2,1,0:T(8,128)S(1)}, f32[...) custom-call(f32[8,64,512]{2,1,0:T(8,128)S(1)} %copy-done, ...), custom_call_target="tpu_custom_call" | custom-call | flops 10485760 | bytes 5242880 | tf_op jit(solution)/shard_map/pallas_call | solution.py:338
  17.9 0.0 copy-start.2
  17.9 1.0 %copy-done.2 = f32[8,64,512]{2,1,0:T(8,128)} copy-done((f32[8,64,512]{2,1,0:T(8,128)}, f32[8,64,512]{2,1,0:T(8,128)S(1)}, u32[]{:S(2)}) %copy-start.2) | copy-done | bytes 1048600
  18.8 0.0 collective-permute-done.5.yhigh_ref
  18.8 1.4 %collective-permute-done.4.ylow_ref = f32[42,512]{1,0:T(8,128)S(1)} collective-permute-done((f32[42,512]{1,0:T(8,128)S(1)}, f32[42,512]{1,0:T(8,128)S(1)}, u32[]{:S(2)}, u32[]{:S(2)}) %collective-permute-start.4) | collective-permute-done | bytes 86048 | tf_op jit(solution)/shard_map/ppermute | solution.py:395
  20.2 0.0 collective-permute-done.near_ref
  20.2 0.0 collective-permute-done.1.far_ref
  20.2 0.0 copy-done.9
  20.2 0.0 copy-start.7
  20.2 2.6 %shard_map.58 = (f32[8,8,512]{2,1,0:T(8,128)S(1)}, f32[64,512]{1,0:T(8,128)S(1)}, f32[64,512]{1,0:T(8,128)S(1)}, f32[64,4,128]{2,1,0:T(4,128)}, f32[2,2,64,512]{3,2,1,0:T(8,128)S(1)}, /*index=5*/f32[2,64,512]{2,1,0:T(8,128)}) custom-call(s32[4]{0:T(128)S(1)} %pad_add_fusion.core_ref.place_ref, f32[2,64,512]{2,1,0:T(8,128)S(1)} %get-tuple-element.34.w5_edges_ref, ...), custom_call_target="tpu_custom_call" | custom-call | tf_op jit(solution)/shard_map/pallas_call | solution.py:338
  22.8 7.6 %all-to-all-start = ((f32[64,4,128]{2,1,0:T(4,128)}), f32[64,4,128]{2,1,0:T(4,128)S(1)}, u32[]{:S(2)}, u32[]{:S(2)}) async-start(f32[64,4,128]{2,1,0:T(4,128)} %get-tuple-element.45), calls=%async_computation | async-start | bytes 262144 | tf_op jit(solution)/shard_map/all_to_all | solution.py:416
  30.4 2.3 %collective-permute-start.9 = (f32[64,512]{1,0:T(8,128)S(1)}, f32[64,512]{1,0:T(8,128)S(1)}, u32[]{:S(2)}, u32[]{:S(2)}) collective-permute-start(f32[64,512]{1,0:T(8,128)S(1)} %get-tuple-element.61), channel_id=1, source_target_pairs={{0,8},{8,0},{16,24},{24,16},{32,40},{40,32},{48,56},{56,48},{64,72... | collective-permute-start | bytes 393224 | tf_op jit(solution)/shard_map/ppermute | solution.py:367
  32.8 0.4 collective-permute-start.10
  33.2 8.8 %all-to-all-done.refs_0_ = f32[64,4,128]{2,1,0:T(4,128)S(1)} async-done(((f32[64,4,128]{2,1,0:T(4,128)}), f32[64,4,128]{2,1,0:T(4,128)S(1)}, u32[]{:S(2)}, u32[]{:S(2)}) %all-to-all-start) | async-done | bytes 131104 | tf_op jit(solution)/shard_map/all_to_all | solution.py:416
  42.0 0.0 copy-done.7
  42.0 0.0 copy-start.5
  42.0 0.0 copy-start.6
  42.1 0.0 copy-start.8
  42.1 1.1 %shard_map.60 = (f32[30,128]{1,0:T(8,128)S(1)}, f32[30,128]{1,0:T(8,128)S(1)}, f32[30,128]{1,0:T(8,128)S(1)}, f32[30,128]{1,0:T(8,128)S(1)}) custom-call(s32[4]{0:T(128)S(1)} %pad_add_fusion.core_ref.place_ref, f32[8,32,128]{2,1,0:T(8,128)S(1)} %bitcast.5, f32[17,13,8,128]{3,2,1,0:T(8,128)S(1)} %copy-done.7), custom_call_target="tpu_custom_call" | custom-call | flops 99999997952 | bytes 10000000 | tf_op jit(solution)/shard_map/pallas_call | solution.py:338
  43.2 3.5 %collective-permute-start.6 = (f32[30,128]{1,0:T(8,128)S(1)}, f32[30,128]{1,0:T(8,128)S(1)}, u32[]{:S(2)}, u32[]{:S(2)}) collective-permute-start(f32[30,128]{1,0:T(8,128)S(1)} %get-tuple-element.52), channel_id=1, source_target_pairs={{0,8},{8,0},{16,24},{24,16},{32,40},{40,32},{48,56},{56,48},{64,72... | collective-permute-start | bytes 46088 | tf_op jit(solution)/shard_map/ppermute | solution.py:437
  46.7 0.0 collective-permute-start.7
  46.7 1.7 %collective-permute-start.8 = (f32[30,128]{1,0:T(8,128)S(1)}, f32[30,128]{1,0:T(8,128)S(1)}, u32[]{:S(2)}, u32[]{:S(2)}) collective-permute-start(f32[30,128]{1,0:T(8,128)S(1)} %get-tuple-element.54), channel_id=1, source_target_pairs={{0,24},{8,16},{16,8},{24,0},{32,56},{40,48},{48,40},{56,32},{64,88... | collective-permute-start | bytes 46088 | tf_op jit(solution)/shard_map/ppermute | solution.py:437
  48.4 0.0 collective-permute-done.9.cnear_ref
  48.4 0.0 collective-permute-done.10.cfar_ref
  48.4 0.0 collective-permute-done.6.one_ref
  48.4 0.9 %collective-permute-done.7.two_ref = f32[30,128]{1,0:T(8,128)S(1)} collective-permute-done((f32[30,128]{1,0:T(8,128)S(1)}, f32[30,128]{1,0:T(8,128)S(1)}, u32[]{:S(2)}, u32[]{:S(2)}) %collective-permute-start.7) | collective-permute-done | bytes 15392 | tf_op jit(solution)/shard_map/ppermute | solution.py:437
  49.3 0.8 %collective-permute-done.8.three_ref = f32[30,128]{1,0:T(8,128)S(1)} collective-permute-done((f32[30,128]{1,0:T(8,128)S(1)}, f32[30,128]{1,0:T(8,128)S(1)}, u32[]{:S(2)}, u32[]{:S(2)}) %collective-permute-start.8) | collective-permute-done | bytes 15392 | tf_op jit(solution)/shard_map/ppermute | solution.py:437
  50.1 0.0 copy-done.3
  50.1 0.0 copy-done.4
  50.1 0.0 copy-done.5
  50.1 0.0 copy-done.6
  50.1 0.0 copy-done.8
  50.1 2.9 %shard_map.61 = f32[8,64,512]{2,1,0:T(8,128)} custom-call(s32[4]{0:T(128)S(1)} %pad_add_fusion.core_ref.place_ref, f32[30,128]{1,0:T(8,128)S(1)} %get-tuple-element.51.own_ref, f32[30,128]{1,0:T(8,128)S(1)} %collective-permute-done.6.one_ref, f32[30,128]{1,0:T(8,128)S(1)} %collective-permute-done.7.two_ref, f32[30,128]{1,0:T(8,128)S(1)} %collective-permute-done.8.three_ref, ...), custom_call_target="tpu_custom_call" | custom-call | tf_op jit(solution)/shard_map/pallas_call | solution.py:338
  (12 shorter events, 0.1 us)
Async XLA Ops:
  0.1 8.1 %copy-start = (f32[8,64,512]{2,1,0:T(8,128)S(1)}, f32[8,64,512]{2,1,0:T(8,128)}, u32[]{:S(2)}) copy-start(f32[8,64,512]{2,1,0:T(8,128)} %cot_ref.3) | copy-start | bytes 3145732
  0.1 8.1 %copy-start.1 = (f32[8,64,512]{2,1,0:T(8,128)S(1)}, f32[8,64,512]{2,1,0:T(8,128)}, u32[]{:S(2)}) copy-start(f32[8,64,512]{2,1,0:T(8,128)} %coef_ref.3) | copy-start | bytes 3145732
  2.0 7.7 %collective-permute-start.2 = (f32[8,512]{1,0:T(8,128)S(1)}, f32[8,512]{1,0:T(8,128)S(1)}, u32[]{:S(2)}, u32[]{:S(2)}) collective-permute-start(f32[8,512]{1,0:T(8,128)S(1)} %get-tuple-element.43), channel_id=1, source_target_pairs={{0,248},{8,16},{16,8},{24,32},{32,24},{40,48},{48,40},{56,64},{64,... | collective-permute-start | bytes 49160 | tf_op jit(solution)/shard_map/ppermute | solution.py:370
  4.7 4.9 %collective-permute-start.3 = (f32[8,512]{1,0:T(8,128)S(1)}, f32[8,512]{1,0:T(8,128)S(1)}, u32[]{:S(2)}, u32[]{:S(2)}) collective-permute-start(f32[8,512]{1,0:T(8,128)S(1)} %get-tuple-element.44), channel_id=1, source_target_pairs={{0,8},{8,0},{16,24},{24,16},{32,40},{40,32},{48,56},{56,48},{64,72... | collective-permute-start | bytes 49160 | tf_op jit(solution)/shard_map/ppermute | solution.py:367
  9.6 10.6 %collective-permute-start = (f32[3,64,512]{2,1,0:T(8,128)}, f32[3,64,512]{2,1,0:T(8,128)S(1)}, u32[]{:S(2)}, u32[]{:S(2)}) collective-permute-start(f32[3,64,512]{2,1,0:T(8,128)} %get-tuple-element.40), channel_id=1, source_target_pairs={{0,8},{8,0},{16,24},{24,16},{32,40},{40,32},{48,56},{56,48},{64,72... | collective-permute-start | bytes 1179656 | tf_op jit(solution)/shard_map/ppermute | solution.py:367
  9.6 10.6 %collective-permute-start.1 = (f32[3,64,512]{2,1,0:T(8,128)S(1)}, f32[3,64,512]{2,1,0:T(8,128)S(1)}, u32[]{:S(2)}, u32[]{:S(2)}) collective-permute-start(f32[3,64,512]{2,1,0:T(8,128)S(1)} %get-tuple-element.41), channel_id=1, source_target_pairs={{0,248},{8,16},{16,8},{24,32},{32,24},{40,48},{48,40},{56,64},{64,... | collective-permute-start | bytes 1179656 | tf_op jit(solution)/shard_map/ppermute | solution.py:370
  9.7 9.2 %collective-permute-start.5 = (f32[42,512]{1,0:T(8,128)S(1)}, f32[42,512]{1,0:T(8,128)S(1)}, u32[]{:S(2)}, u32[]{:S(2)}) collective-permute-start(f32[42,512]{1,0:T(8,128)S(1)} %pad_maximum_fusion.1), channel_id=1, source_target_pairs={{0,7},{1,0},{2,1},{3,2},{4,3},{5,4},{6,5},{7,6},{8,15},{9,8},{10,9... | collective-permute-start | bytes 258056 | tf_op jit(solution)/shard_map/ppermute | solution.py:396
  15.4 4.9 %copy-start.9 = (f32[512,64]{1,0:T(8,128)S(1)}, f32[512,64]{1,0:T(8,128)}, u32[]{:S(2)}) copy-start(f32[512,64]{1,0:T(8,128)} %constant.32.clone.into_ref) | copy-start | bytes 393220
  15.4 4.8 %collective-permute-start.4 = (f32[42,512]{1,0:T(8,128)S(1)}, f32[42,512]{1,0:T(8,128)S(1)}, u32[]{:S(2)}, u32[]{:S(2)}) collective-permute-start(f32[42,512]{1,0:T(8,128)S(1)} %pad_maximum_fusion), channel_id=1, source_target_pairs={{0,1},{1,2},{2,3},{3,4},{4,5},{5,6},{6,7},{7,0},{8,9},{9,10},{10,1... | collective-permute-start | bytes 258056 | tf_op jit(solution)/shard_map/ppermute | solution.py:395
  17.9 1.0 %copy-start.2 = (f32[8,64,512]{2,1,0:T(8,128)}, f32[8,64,512]{2,1,0:T(8,128)S(1)}, u32[]{:S(2)}) copy-start(f32[8,64,512]{2,1,0:T(8,128)S(1)} %get-tuple-element.46.refs_1_) | copy-start | bytes 3145732
  20.2 21.8 %copy-start.7 = (f32[17,13,8,128]{3,2,1,0:T(8,128)S(1)}, f32[17,13,8,128]{3,2,1,0:T(8,128)}, u32[]{:S(2)}) copy-start(f32[17,13,8,128]{3,2,1,0:T(8,128)} %constant.33.clone.refs_5_.table_ref) | copy-start | bytes 2715652
  22.8 19.2 %all-to-all-start = ((f32[64,4,128]{2,1,0:T(4,128)}), f32[64,4,128]{2,1,0:T(4,128)S(1)}, u32[]{:S(2)}, u32[]{:S(2)}) async-start(f32[64,4,128]{2,1,0:T(4,128)} %get-tuple-element.45), calls=%async_computation | async-start | bytes 262144 | tf_op jit(solution)/shard_map/all_to_all | solution.py:416
  30.4 18.0 %collective-permute-start.9 = (f32[64,512]{1,0:T(8,128)S(1)}, f32[64,512]{1,0:T(8,128)S(1)}, u32[]{:S(2)}, u32[]{:S(2)}) collective-permute-start(f32[64,512]{1,0:T(8,128)S(1)} %get-tuple-element.61), channel_id=1, source_target_pairs={{0,8},{8,0},{16,24},{24,16},{32,40},{40,32},{48,56},{56,48},{64,72... | collective-permute-start | bytes 393224 | tf_op jit(solution)/shard_map/ppermute | solution.py:367
  32.8 15.6 %collective-permute-start.10 = (f32[64,512]{1,0:T(8,128)S(1)}, f32[64,512]{1,0:T(8,128)S(1)}, u32[]{:S(2)}, u32[]{:S(2)}) collective-permute-start(f32[64,512]{1,0:T(8,128)S(1)} %get-tuple-element.62), channel_id=1, source_target_pairs={{0,248},{8,16},{16,8},{24,32},{32,24},{40,48},{48,40},{56,64},{64,... | collective-permute-start | bytes 393224 | tf_op jit(solution)/shard_map/ppermute | solution.py:370
  42.0 8.1 %copy-start.3 = (f32[8,64,512]{2,1,0:T(8,128)S(1)}, f32[8,64,512]{2,1,0:T(8,128)}, u32[]{:S(2)}) copy-start(f32[8,64,512]{2,1,0:T(8,128)} %get-tuple-element.55.c3_ref) | copy-start | bytes 3145732
  42.0 8.1 %copy-start.4 = (f32[8,64,512]{2,1,0:T(8,128)S(1)}, f32[8,64,512]{2,1,0:T(8,128)}, u32[]{:S(2)}) copy-start(f32[8,64,512]{2,1,0:T(8,128)} %get-tuple-element.56.base_ref) | copy-start | bytes 3145732
  42.0 8.1 %copy-start.5 = (f32[8,64,512]{2,1,0:T(8,128)S(1)}, f32[8,64,512]{2,1,0:T(8,128)}, u32[]{:S(2)}) copy-start(f32[8,64,512]{2,1,0:T(8,128)} %get-tuple-element.57.inverse_ref) | copy-start | bytes 3145732
  42.0 8.1 %copy-start.6 = (f32[2,64,512]{2,1,0:T(8,128)S(1)}, f32[2,64,512]{2,1,0:T(8,128)}, u32[]{:S(2)}) copy-start(f32[2,64,512]{2,1,0:T(8,128)} %get-tuple-element.58.planes_ref) | copy-start | bytes 786436
  42.1 8.1 %copy-start.8 = (f32[128,512]{1,0:T(8,128)S(1)}, f32[128,512]{1,0:T(8,128)}, u32[]{:S(2)}) copy-start(f32[128,512]{1,0:T(8,128)} %constant.34.clone.out_table_ref) | copy-start | bytes 786436
  43.2 5.2 %collective-permute-start.6 = (f32[30,128]{1,0:T(8,128)S(1)}, f32[30,128]{1,0:T(8,128)S(1)}, u32[]{:S(2)}, u32[]{:S(2)}) collective-permute-start(f32[30,128]{1,0:T(8,128)S(1)} %get-tuple-element.52), channel_id=1, source_target_pairs={{0,8},{8,0},{16,24},{24,16},{32,40},{40,32},{48,56},{56,48},{64,72... | collective-permute-start | bytes 46088 | tf_op jit(solution)/shard_map/ppermute | solution.py:437
  46.7 2.6 %collective-permute-start.7 = (f32[30,128]{1,0:T(8,128)S(1)}, f32[30,128]{1,0:T(8,128)S(1)}, u32[]{:S(2)}, u32[]{:S(2)}) collective-permute-start(f32[30,128]{1,0:T(8,128)S(1)} %get-tuple-element.53), channel_id=1, source_target_pairs={{0,16},{8,24},{16,0},{24,8},{32,48},{40,56},{48,32},{56,40},{64,80... | collective-permute-start | bytes 46088 | tf_op jit(solution)/shard_map/ppermute | solution.py:437
  46.7 3.4 %collective-permute-start.8 = (f32[30,128]{1,0:T(8,128)S(1)}, f32[30,128]{1,0:T(8,128)S(1)}, u32[]{:S(2)}, u32[]{:S(2)}) collective-permute-start(f32[30,128]{1,0:T(8,128)S(1)} %get-tuple-element.54), channel_id=1, source_target_pairs={{0,24},{8,16},{16,8},{24,0},{32,56},{40,48},{48,40},{56,32},{64,88... | collective-permute-start | bytes 46088 | tf_op jit(solution)/shard_map/ppermute | solution.py:437

commit v5 on v4

--- a/solution.py
+++ b/solution.py
@@ -185,14 +185,15 @@
 
 
 def first_kernel(
-    core_ref, w5_edges_ref, inverse_edges_ref, c3_edges_ref, own_rows_ref, part_sums_ref,
+    core_ref, w5_edges_ref, inverse_edges_ref, c3_edges_ref, own_rows_ref, part_sums_ref, c3_ref,
     near_ref, far_ref, ylow_ref, yhigh_ref, into_ref,
-    rows_ref, cnear_ref, cfar_ref, send_ref, added_ref, planes_hbm,
-    sems,
+    rows_ref, cnear_ref, cfar_ref, added_ref, send_hbm, planes_hbm, c3_hbm,
+    send_ref, sems,
 ):
     core = core_ref[0]
     copies = fetch(
         [
+            (c3_ref, c3_hbm),
             (near_ref.at[1], planes_hbm.at[1 - core]),
             (far_ref.at[1], planes_hbm.at[core]),
         ],
@@ -241,6 +242,7 @@
     modes = jnp.dot(sums, into_ref[...], precision=lax.Precision.HIGHEST, preferred_element_type=F32)
     packed = jnp.concatenate([modes[0:4, :], modes[4:8, :]], axis=1)
     send_ref[...] = jnp.broadcast_to(packed[None], send_ref.shape)
+    copies += fetch([(send_ref, send_hbm)], sems, 3)
     edges = []
     for side, x in ((0, 0), (1, BX - 1)):
         at = slice(x, x + 1)
@@ -379,14 +381,14 @@
         scratch=[(2, BX, 8, NZ), (2, BX, 8, NZ)],
         sems=4,
     )
+    tiny_far, tiny_near = far_swap(tiny_far), near_swap(tiny_near)
     near, far = call(
         edge_kernel,
         [(3,) + plane, (3,) + plane],
-        [place, cotangent, coefficient, y_low],
+        [place, cotangent, coefficient, tiny_near],
         [SMEM, VMEM, VMEM, VMEM],
         [VMEM] * 2,
     )
-    tiny_far, tiny_near = far_swap(tiny_far), near_swap(tiny_near)
     far, near = far_swap(far), near_swap(near)
     corner_low = jnp.where(core == 0, tiny_far, tiny_near)
     corner_high = jnp.where(core == 0, tiny_near, tiny_far)
@@ -405,13 +407,14 @@
         sems=2,
         cost=pl.CostEstimate(flops=40 * BX * BY * NZ, bytes_accessed=5 * 4 * BX * BY * NZ, transcendentals=0),
     )
-    rows, c_near, c_far, send, added, planes = call(
+    rows, c_near, c_far, added, send, planes, c3 = call(
         first_kernel,
-        [(8, BX, NZ), plane, plane, (GROUPS * GY, 4, 2 * CZ), (2,) + edge_planes, edge_planes],
-        [place, w5_edges, inverse_edges, c3_edges, own_rows, sums, near, far, from_low, from_high, jnp.asarray(into)],
-        [SMEM] + [VMEM] * 10,
-        [VMEM] * 5 + [HBM],
-        sems=2,
+        [(8, BX, NZ), plane, plane, (2,) + edge_planes, (GROUPS * GY, 4, 2 * CZ), edge_planes, brick],
+        [place, w5_edges, inverse_edges, c3_edges, own_rows, sums, c3, near, far, from_low, from_high, jnp.asarray(into)],
+        [SMEM] + [VMEM] * 11,
+        [VMEM] * 4 + [HBM] * 3,
+        scratch=[(GROUPS * GY, 4, 2 * CZ)],
+        sems=4,
     )
     got = lax.all_to_all(send, ("x", "pair", "gy"), 0, 0, tiled=True)
     c_near, c_far = near_swap(c_near), far_swap(c_far)

time: 53.2 us -> 52.4 us (0.985)
  starting transfers between devices: 27.5 us -> 30.5 us
  waiting for transfers between devices: 11.9 us -> 10.3 us
  Pallas kernels: 12.3 us -> 11.1 us
  local copies, waits for them, and re-layouts: 1.03 us -> 0.07 us
    ppermute x3, starting transfers between devices: 5.82 us -> 8.94 us  [near_swap(): return lax.ppermute(v, along_x, near_pairs)]
    ppermute x3, starting transfers between devices: 3.22 us -> 1.03 us  [far_swap(): return lax.ppermute(v, along_x, far_pairs)]
    ppermute x1, starting transfers between devices: 0.08 us -> 1.71 us  [body(): from_low = lax.ppermute(y_high, 'gy', up)]
    ppermute x1, starting transfers between devices: 5.65 us -> 4.03 us  [body(): from_high = lax.ppermute(y_low, 'gy', down)]
    all_to_all x1, starting transfers between devices: 7.58 us -> 9.1 us  [body(): got = lax.all_to_all(send, ('x', 'pair', 'gy'), 0, 0, tiled=True)]
    ppermute x1, waiting for transfers between devices: 1.35 us -> 0.01 us  [body(): from_low = lax.ppermute(y_high, 'gy', up)]
    pallas_call x7, Pallas kernels: 12.3 us -> 11.1 us  [call(): pl.pallas_call(kernel, out_shape=[spec.memory_space(shape, F32) for shape...]
    all_to_all x1, waiting for transfers between devices: 8.81 us -> 7.76 us  [body(): got = lax.all_to_all(send, ('x', 'pair', 'gy'), 0, 0, tiled=True)]
  transfers between devices with their start and end apart: 12 -> 12, of which waited for: 4 -> 4; matrix products, arithmetic and copies ran while one was open for 0% -> 0% of each run, Pallas kernels for 9% -> 8%
where the time goes in v5:
time: 52.4 us; the launch traced here: 52.3 us
  starting transfers between devices  30.5 us (58%)
  Pallas kernels  11.1 us (21%)
  waiting for transfers between devices  10.3 us (20%)
    pallas_call x7, Pallas kernels, call(): pl.pallas_call(kernel, out_shape=[spec.memory_space(shape, F32) for shape...  11.1 us
    all_to_all x1, starting transfers between devices, body(): got = lax.all_to_all(send, ('x', 'pair', 'gy'), 0, 0, tiled=True)  9.1 us
    ppermute x3, starting transfers between devices, near_swap(): return lax.ppermute(v, along_x, near_pairs)  8.94 us
    all_to_all x1, waiting for transfers between devices, body(): got = lax.all_to_all(send, ('x', 'pair', 'gy'), 0, 0, tiled=True)  7.76 us
    ppermute x3, starting transfers between devices, body(): lax.ppermute(v, along_x, [(i, i ^ flip) for i in range(GX)])  5.65 us
    ppermute x1, starting transfers between devices, body(): from_high = lax.ppermute(y_low, 'gy', down)  4.03 us
    ppermute x1, starting transfers between devices, body(): from_low = lax.ppermute(y_high, 'gy', up)  1.71 us
    ppermute x3, waiting for transfers between devices, body(): lax.ppermute(v, along_x, [(i, i ^ flip) for i in range(GX)])  1.7 us
  transfers between devices with their start and end apart: 12, of which 4 were waited for; matrix products, arithmetic and copies ran while one was open for 0% of the time, Pallas kernels for 8%

profile of v5, /device:TPU:1, one launch (start us, length us, event | category | flops | bytes accessed | tf_op | source)
XLA Modules:
  0.0 52.3 jit_solution(2663746588240199529)
XLA Ops:
  0.0 0.1 pad_add_fusion.core_ref.place_ref
  0.1 0.0 copy-start
  0.1 0.0 copy-start.1
  0.1 1.9 %shard_map.56 = (f32[8,512]{1,0:T(8,128)S(1)}, f32[8,512]{1,0:T(8,128)S(1)}, f32[34,512]{1,0:T(8,128)S(1)}, f32[34,512]{1,0:T(8,128)S(1)}) custom-call(s32[4]{0:T(128)S(1)} %pad_add_fusion.core_ref.place_ref, f32[8,64,512]{2,1,0:T(8,128)} %cot_ref.3, f32[8,64,512]{2,1,0:T(8,128)} %coef_ref.3), custom_call_target="tpu_custom_call" | custom-call | tf_op jit(solution)/shard_map/pallas_call | solution.py:340
  2.0 3.3 %collective-permute-start = (f32[8,512]{1,0:T(8,128)S(1)}, f32[8,512]{1,0:T(8,128)S(1)}, u32[]{:S(2)}, u32[]{:S(2)}) collective-permute-start(f32[8,512]{1,0:T(8,128)S(1)} %get-tuple-element.41), channel_id=1, source_target_pairs={{0,8},{8,0},{16,24},{24,16},{32,40},{40,32},{48,56},{56,48},{64,72... | collective-permute-start | bytes 49160 | tf_op jit(solution)/shard_map/ppermute | solution.py:369
  5.3 0.0 collective-permute-start.3
  5.3 0.8 %collective-permute-done.after_ref = f32[8,512]{1,0:T(8,128)S(1)} collective-permute-done((f32[8,512]{1,0:T(8,128)S(1)}, f32[8,512]{1,0:T(8,128)S(1)}, u32[]{:S(2)}, u32[]{:S(2)}) %collective-permute-start) | collective-permute-done | bytes 16416 | tf_op jit(solution)/shard_map/ppermute | solution.py:369
  6.1 0.0 copy-done
  6.1 0.0 copy-done.1
  6.1 0.6 %shard_map.57 = (f32[3,64,512]{2,1,0:T(8,128)S(1)}, f32[3,64,512]{2,1,0:T(8,128)S(1)}) custom-call(s32[4]{0:T(128)S(1)} %pad_add_fusion.core_ref.place_ref, f32[8,64,512]{2,1,0:T(8,128)S(1)} %copy-done, f32[8,64,512]{2,1,0:T(8,128)S(1)} %copy-done.1, f32[8,512]{1,0:T(8,128)S(1)} %collective-permute-done.after_ref), custom_call_target="tpu_custom_call" | custom-call | tf_op jit(solution)/shard_map/pallas_call | solution.py:340
  6.8 2.9 %collective-permute-start.1 = (f32[3,64,512]{2,1,0:T(8,128)S(1)}, f32[3,64,512]{2,1,0:T(8,128)S(1)}, u32[]{:S(2)}, u32[]{:S(2)}) collective-permute-start(f32[3,64,512]{2,1,0:T(8,128)S(1)} %get-tuple-element.42), channel_id=1, source_target_pairs={{0,8},{8,0},{16,24},{24,16},{32,40},{40,32},{48,56},{56,48},{64,72... | collective-permute-start | bytes 1179656 | tf_op jit(solution)/shard_map/ppermute | solution.py:369
  9.7 0.0 collective-permute-start.2
  9.7 0.0 collective-permute-done.3
  9.7 1.7 %collective-permute-start.4 = (f32[42,512]{1,0:T(8,128)S(1)}, f32[42,512]{1,0:T(8,128)S(1)}, u32[]{:S(2)}, u32[]{:S(2)}) collective-permute-start(f32[42,512]{1,0:T(8,128)S(1)} %pad_maximum_fusion), channel_id=1, source_target_pairs={{0,1},{1,2},{2,3},{3,4},{4,5},{5,6},{6,7},{7,0},{8,9},{9,10},{10,1... | collective-permute-start | bytes 258056 | tf_op jit(solution)/shard_map/ppermute | solution.py:397
  11.5 0.0 copy-start.8
  11.5 4.0 %collective-permute-start.5 = (f32[42,512]{1,0:T(8,128)S(1)}, f32[42,512]{1,0:T(8,128)S(1)}, u32[]{:S(2)}, u32[]{:S(2)}) collective-permute-start(f32[42,512]{1,0:T(8,128)S(1)} %pad_maximum_fusion.1), channel_id=1, source_target_pairs={{0,7},{1,0},{2,1},{3,2},{4,3},{5,4},{6,5},{7,6},{8,15},{9,8},{10,9... | collective-permute-start | bytes 258056 | tf_op jit(solution)/shard_map/ppermute | solution.py:398
  15.5 2.5 %shard_map.55 = (f32[2,64,512]{2,1,0:T(8,128)S(1)}, f32[2,64,512]{2,1,0:T(8,128)S(1)}, f32[2,64,512]{2,1,0:T(8,128)S(1)}, f32[6,8,512]{2,1,0:T(8,128)S(1)}, f32[...) custom-call(f32[8,64,512]{2,1,0:T(8,128)S(1)} %copy-done, ...), custom_call_target="tpu_custom_call" | custom-call | flops 10485760 | bytes 5242880 | tf_op jit(solution)/shard_map/pallas_call | solution.py:340
  18.0 0.0 collective-permute-done.4.ylow_ref
  18.0 0.0 collective-permute-done.5.yhigh_ref
  18.0 0.0 collective-permute-done.1.near_ref
  18.0 0.0 collective-permute-done.2.far_ref
  18.1 0.0 copy-done.8
  18.1 0.0 copy-start.6
  18.1 2.2 %shard_map.58 = (f32[8,8,512]{2,1,0:T(8,128)S(1)}, f32[64,512]{1,0:T(8,128)S(1)}, f32[64,512]{1,0:T(8,128)S(1)}, f32[2,2,64,512]{3,2,1,0:T(8,128)S(1)}, f32[64,4...) custom-call(s32[4]{0:T(128)S(1)} %pad_add_fusion.core_ref.place_ref, ...), custom_call_target="tpu_custom_call" | custom-call | tf_op jit(solution)/shard_map/pallas_call | solution.py:340
  20.3 9.1 %all-to-all-start = ((f32[64,4,128]{2,1,0:T(4,128)}), f32[64,4,128]{2,1,0:T(4,128)S(1)}, u32[]{:S(2)}, u32[]{:S(2)}) async-start(f32[64,4,128]{2,1,0:T(4,128)} %get-tuple-element.47), calls=%async_computation | async-start | bytes 262144 | tf_op jit(solution)/shard_map/all_to_all | solution.py:419
  29.4 2.7 %collective-permute-start.9 = (f32[64,512]{1,0:T(8,128)S(1)}, f32[64,512]{1,0:T(8,128)S(1)}, u32[]{:S(2)}, u32[]{:S(2)}) collective-permute-start(f32[64,512]{1,0:T(8,128)S(1)} %get-tuple-element.63), channel_id=1, source_target_pairs={{0,8},{8,0},{16,24},{24,16},{32,40},{40,32},{48,56},{56,48},{64,72... | collective-permute-start | bytes 393224 | tf_op jit(solution)/shard_map/ppermute | solution.py:369
  32.1 1.0 %collective-permute-start.10 = (f32[64,512]{1,0:T(8,128)S(1)}, f32[64,512]{1,0:T(8,128)S(1)}, u32[]{:S(2)}, u32[]{:S(2)}) collective-permute-start(f32[64,512]{1,0:T(8,128)S(1)} %get-tuple-element.64), channel_id=1, source_target_pairs={{0,248},{8,16},{16,8},{24,32},{32,24},{40,48},{48,40},{56,64},{64,... | collective-permute-start | bytes 393224 | tf_op jit(solution)/shard_map/ppermute | solution.py:372
  33.1 7.8 %all-to-all-done.refs_0_ = f32[64,4,128]{2,1,0:T(4,128)S(1)} async-done(((f32[64,4,128]{2,1,0:T(4,128)}), f32[64,4,128]{2,1,0:T(4,128)S(1)}, u32[]{:S(2)}, u32[]{:S(2)}) %all-to-all-start) | async-done | bytes 131104 | tf_op jit(solution)/shard_map/all_to_all | solution.py:419
  40.9 0.0 copy-done.6
  40.9 0.0 copy-start.2
  40.9 0.0 copy-start.4
  40.9 0.0 copy-start.5
  40.9 0.0 copy-start.7
  40.9 1.1 %shard_map.60 = (f32[30,128]{1,0:T(8,128)S(1)}, f32[30,128]{1,0:T(8,128)S(1)}, f32[30,128]{1,0:T(8,128)S(1)}, f32[30,128]{1,0:T(8,128)S(1)}) custom-call(s32[4]{0:T(128)S(1)} %pad_add_fusion.core_ref.place_ref, f32[8,32,128]{2,1,0:T(8,128)S(1)} %bitcast.5, f32[17,13,8,128]{3,2,1,0:T(8,128)S(1)} %copy-done.6), custom_call_target="tpu_custom_call" | custom-call | flops 99999997952 | bytes 10000000 | tf_op jit(solution)/shard_map/pallas_call | solution.py:340
  42.1 3.9 %collective-permute-start.6 = (f32[30,128]{1,0:T(8,128)S(1)}, f32[30,128]{1,0:T(8,128)S(1)}, u32[]{:S(2)}, u32[]{:S(2)}) collective-permute-start(f32[30,128]{1,0:T(8,128)S(1)} %get-tuple-element.54), channel_id=1, source_target_pairs={{0,8},{8,0},{16,24},{24,16},{32,40},{40,32},{48,56},{56,48},{64,72... | collective-permute-start | bytes 46088 | tf_op jit(solution)/shard_map/ppermute | solution.py:440
  46.0 0.0 collective-permute-start.7
  46.0 1.7 %collective-permute-start.8 = (f32[30,128]{1,0:T(8,128)S(1)}, f32[30,128]{1,0:T(8,128)S(1)}, u32[]{:S(2)}, u32[]{:S(2)}) collective-permute-start(f32[30,128]{1,0:T(8,128)S(1)} %get-tuple-element.56), channel_id=1, source_target_pairs={{0,24},{8,16},{16,8},{24,0},{32,56},{40,48},{48,40},{56,32},{64,88... | collective-permute-start | bytes 46088 | tf_op jit(solution)/shard_map/ppermute | solution.py:440
  47.7 0.0 collective-permute-done.9.cnear_ref
  47.7 0.0 collective-permute-done.10.cfar_ref
  47.7 0.0 collective-permute-done.6.one_ref
  47.7 0.9 %collective-permute-done.7.two_ref = f32[30,128]{1,0:T(8,128)S(1)} collective-permute-done((f32[30,128]{1,0:T(8,128)S(1)}, f32[30,128]{1,0:T(8,128)S(1)}, u32[]{:S(2)}, u32[]{:S(2)}) %collective-permute-start.7) | collective-permute-done | bytes 15392 | tf_op jit(solution)/shard_map/ppermute | solution.py:440
  48.6 0.8 %collective-permute-done.8.three_ref = f32[30,128]{1,0:T(8,128)S(1)} collective-permute-done((f32[30,128]{1,0:T(8,128)S(1)}, f32[30,128]{1,0:T(8,128)S(1)}, u32[]{:S(2)}, u32[]{:S(2)}) %collective-permute-start.8) | collective-permute-done | bytes 15392 | tf_op jit(solution)/shard_map/ppermute | solution.py:440
  49.4 0.0 copy-done.2
  49.4 0.0 copy-done.3
  49.4 0.0 copy-done.4
  49.4 0.0 copy-done.5
  49.4 0.0 copy-done.7
  49.5 2.8 %shard_map.61 = f32[8,64,512]{2,1,0:T(8,128)} custom-call(s32[4]{0:T(128)S(1)} %pad_add_fusion.core_ref.place_ref, f32[30,128]{1,0:T(8,128)S(1)} %get-tuple-element.53.own_ref, f32[30,128]{1,0:T(8,128)S(1)} %collective-permute-done.6.one_ref, f32[30,128]{1,0:T(8,128)S(1)} %collective-permute-done.7.two_ref, f32[30,128]{1,0:T(8,128)S(1)} %collective-permute-done.8.three_ref, ...), custom_call_target="tpu_custom_call" | custom-call | tf_op jit(solution)/shard_map/pallas_call | solution.py:340
  (10 shorter events, 0.1 us)
Async XLA Ops:
  0.1 6.1 %copy-start = (f32[8,64,512]{2,1,0:T(8,128)S(1)}, f32[8,64,512]{2,1,0:T(8,128)}, u32[]{:S(2)}) copy-start(f32[8,64,512]{2,1,0:T(8,128)} %cot_ref.3) | copy-start | bytes 3145732
  0.1 6.1 %copy-start.1 = (f32[8,64,512]{2,1,0:T(8,128)S(1)}, f32[8,64,512]{2,1,0:T(8,128)}, u32[]{:S(2)}) copy-start(f32[8,64,512]{2,1,0:T(8,128)} %coef_ref.3) | copy-start | bytes 3145732
  2.0 4.2 %collective-permute-start = (f32[8,512]{1,0:T(8,128)S(1)}, f32[8,512]{1,0:T(8,128)S(1)}, u32[]{:S(2)}, u32[]{:S(2)}) collective-permute-start(f32[8,512]{1,0:T(8,128)S(1)} %get-tuple-element.41), channel_id=1, source_target_pairs={{0,8},{8,0},{16,24},{24,16},{32,40},{40,32},{48,56},{56,48},{64,72... | collective-permute-start | bytes 49160 | tf_op jit(solution)/shard_map/ppermute | solution.py:369
  5.3 4.4 %collective-permute-start.3 = (f32[8,512]{1,0:T(8,128)S(1)}, f32[8,512]{1,0:T(8,128)S(1)}, u32[]{:S(2)}, u32[]{:S(2)}) collective-permute-start(f32[8,512]{1,0:T(8,128)S(1)} %get-tuple-element.45), channel_id=1, source_target_pairs={{0,248},{8,16},{16,8},{24,32},{32,24},{40,48},{48,40},{56,64},{64,... | collective-permute-start | bytes 49160 | tf_op jit(solution)/shard_map/ppermute | solution.py:372
  6.8 11.2 %collective-permute-start.1 = (f32[3,64,512]{2,1,0:T(8,128)S(1)}, f32[3,64,512]{2,1,0:T(8,128)S(1)}, u32[]{:S(2)}, u32[]{:S(2)}) collective-permute-start(f32[3,64,512]{2,1,0:T(8,128)S(1)} %get-tuple-element.42), channel_id=1, source_target_pairs={{0,8},{8,0},{16,24},{24,16},{32,40},{40,32},{48,56},{56,48},{64,72... | collective-permute-start | bytes 1179656 | tf_op jit(solution)/shard_map/ppermute | solution.py:369
  9.7 8.4 %collective-permute-start.2 = (f32[3,64,512]{2,1,0:T(8,128)S(1)}, f32[3,64,512]{2,1,0:T(8,128)S(1)}, u32[]{:S(2)}, u32[]{:S(2)}) collective-permute-start(f32[3,64,512]{2,1,0:T(8,128)S(1)} %get-tuple-element.43), channel_id=1, source_target_pairs={{0,248},{8,16},{16,8},{24,32},{32,24},{40,48},{48,40},{56,64},{64,... | collective-permute-start | bytes 1179656 | tf_op jit(solution)/shard_map/ppermute | solution.py:372
  9.7 8.3 %collective-permute-start.4 = (f32[42,512]{1,0:T(8,128)S(1)}, f32[42,512]{1,0:T(8,128)S(1)}, u32[]{:S(2)}, u32[]{:S(2)}) collective-permute-start(f32[42,512]{1,0:T(8,128)S(1)} %pad_maximum_fusion), channel_id=1, source_target_pairs={{0,1},{1,2},{2,3},{3,4},{4,5},{5,6},{6,7},{7,0},{8,9},{9,10},{10,1... | collective-permute-start | bytes 258056 | tf_op jit(solution)/shard_map/ppermute | solution.py:397
  11.5 6.6 %copy-start.8 = (f32[512,64]{1,0:T(8,128)S(1)}, f32[512,64]{1,0:T(8,128)}, u32[]{:S(2)}) copy-start(f32[512,64]{1,0:T(8,128)} %constant.32.clone.into_ref) | copy-start | bytes 393220
  11.5 6.5 %collective-permute-start.5 = (f32[42,512]{1,0:T(8,128)S(1)}, f32[42,512]{1,0:T(8,128)S(1)}, u32[]{:S(2)}, u32[]{:S(2)}) collective-permute-start(f32[42,512]{1,0:T(8,128)S(1)} %pad_maximum_fusion.1), channel_id=1, source_target_pairs={{0,7},{1,0},{2,1},{3,2},{4,3},{5,4},{6,5},{7,6},{8,15},{9,8},{10,9... | collective-permute-start | bytes 258056 | tf_op jit(solution)/shard_map/ppermute | solution.py:398
  18.1 22.8 %copy-start.6 = (f32[17,13,8,128]{3,2,1,0:T(8,128)S(1)}, f32[17,13,8,128]{3,2,1,0:T(8,128)}, u32[]{:S(2)}) copy-start(f32[17,13,8,128]{3,2,1,0:T(8,128)} %constant.33.clone.refs_5_.table_ref) | copy-start | bytes 2715652
  20.3 20.6 %all-to-all-start = ((f32[64,4,128]{2,1,0:T(4,128)}), f32[64,4,128]{2,1,0:T(4,128)S(1)}, u32[]{:S(2)}, u32[]{:S(2)}) async-start(f32[64,4,128]{2,1,0:T(4,128)} %get-tuple-element.47), calls=%async_computation | async-start | bytes 262144 | tf_op jit(solution)/shard_map/all_to_all | solution.py:419
  29.4 18.3 %collective-permute-start.9 = (f32[64,512]{1,0:T(8,128)S(1)}, f32[64,512]{1,0:T(8,128)S(1)}, u32[]{:S(2)}, u32[]{:S(2)}) collective-permute-start(f32[64,512]{1,0:T(8,128)S(1)} %get-tuple-element.63), channel_id=1, source_target_pairs={{0,8},{8,0},{16,24},{24,16},{32,40},{40,32},{48,56},{56,48},{64,72... | collective-permute-start | bytes 393224 | tf_op jit(solution)/shard_map/ppermute | solution.py:369
  32.1 15.6 %collective-permute-start.10 = (f32[64,512]{1,0:T(8,128)S(1)}, f32[64,512]{1,0:T(8,128)S(1)}, u32[]{:S(2)}, u32[]{:S(2)}) collective-permute-start(f32[64,512]{1,0:T(8,128)S(1)} %get-tuple-element.64), channel_id=1, source_target_pairs={{0,248},{8,16},{16,8},{24,32},{32,24},{40,48},{48,40},{56,64},{64,... | collective-permute-start | bytes 393224 | tf_op jit(solution)/shard_map/ppermute | solution.py:372
  40.9 8.5 %copy-start.2 = (f32[8,64,512]{2,1,0:T(8,128)S(1)}, f32[8,64,512]{2,1,0:T(8,128)}, u32[]{:S(2)}) copy-start(f32[8,64,512]{2,1,0:T(8,128)} %get-tuple-element.58.base_ref) | copy-start | bytes 3145732
  40.9 8.5 %copy-start.3 = (f32[8,64,512]{2,1,0:T(8,128)S(1)}, f32[8,64,512]{2,1,0:T(8,128)}, u32[]{:S(2)}) copy-start(f32[8,64,512]{2,1,0:T(8,128)} %get-tuple-element.59.inverse_ref) | copy-start | bytes 3145732
  40.9 8.5 %copy-start.4 = (f32[8,64,512]{2,1,0:T(8,128)S(1)}, f32[8,64,512]{2,1,0:T(8,128)}, u32[]{:S(2)}) copy-start(f32[8,64,512]{2,1,0:T(8,128)} %get-tuple-element.57.c3_ref) | copy-start | bytes 3145732
  40.9 8.5 %copy-start.5 = (f32[2,64,512]{2,1,0:T(8,128)S(1)}, f32[2,64,512]{2,1,0:T(8,128)}, u32[]{:S(2)}) copy-start(f32[2,64,512]{2,1,0:T(8,128)} %get-tuple-element.60.planes_ref) | copy-start | bytes 786436
  40.9 8.5 %copy-start.7 = (f32[128,512]{1,0:T(8,128)S(1)}, f32[128,512]{1,0:T(8,128)}, u32[]{:S(2)}) copy-start(f32[128,512]{1,0:T(8,128)} %constant.34.clone.out_table_ref) | copy-start | bytes 786436
  42.1 5.7 %collective-permute-start.6 = (f32[30,128]{1,0:T(8,128)S(1)}, f32[30,128]{1,0:T(8,128)S(1)}, u32[]{:S(2)}, u32[]{:S(2)}) collective-permute-start(f32[30,128]{1,0:T(8,128)S(1)} %get-tuple-element.54), channel_id=1, source_target_pairs={{0,8},{8,0},{16,24},{24,16},{32,40},{40,32},{48,56},{56,48},{64,72... | collective-permute-start | bytes 46088 | tf_op jit(solution)/shard_map/ppermute | solution.py:440
  46.0 2.6 %collective-permute-start.7 = (f32[30,128]{1,0:T(8,128)S(1)}, f32[30,128]{1,0:T(8,128)S(1)}, u32[]{:S(2)}, u32[]{:S(2)}) collective-permute-start(f32[30,128]{1,0:T(8,128)S(1)} %get-tuple-element.55), channel_id=1, source_target_pairs={{0,16},{8,24},{16,0},{24,8},{32,48},{40,56},{48,32},{56,40},{64,80... | collective-permute-start | bytes 46088 | tf_op jit(solution)/shard_map/ppermute | solution.py:440
  46.0 3.4 %collective-permute-start.8 = (f32[30,128]{1,0:T(8,128)S(1)}, f32[30,128]{1,0:T(8,128)S(1)}, u32[]{:S(2)}, u32[]{:S(2)}) collective-permute-start(f32[30,128]{1,0:T(8,128)S(1)} %get-tuple-element.56), channel_id=1, source_target_pairs={{0,24},{8,16},{16,8},{24,0},{32,56},{40,48},{48,40},{56,32},{64,88... | collective-permute-start | bytes 46088 | tf_op jit(solution)/shard_map/ppermute | solution.py:440

commit v6 on v5

--- a/solution.py
+++ b/solution.py
@@ -23,7 +23,6 @@
 OUT_X = MATES + 2
 
 VMEM = pl.BlockSpec(memory_space=pltpu.VMEM)
-SMEM = pl.BlockSpec(memory_space=pltpu.SMEM)
 HBM = pl.BlockSpec(memory_space=pltpu.HBM)
 F32 = jnp.float32
 
@@ -87,8 +86,8 @@
         copy.wait()
 
 
-def strip_kernel(core_ref, cot_hbm, coef_hbm, tnear_ref, tfar_ref, ylow_ref, yhigh_ref, cot_ref, coef_ref, sems):
-    core = core_ref[0]
+def strip_kernel(cot_hbm, coef_hbm, tnear_ref, tfar_ref, ylow_ref, yhigh_ref, cot_ref, coef_ref, sems):
+    core = lax.axis_index("core")
     ends = (pl.ds(0, 8), pl.ds(BY - 8, 8))
     wait(
         fetch(
@@ -121,8 +120,8 @@
             tfar_ref[place, :] = jnp.where(core == 0, low, high)
 
 
-def edge_kernel(core_ref, cot_ref, coef_ref, after_ref, near_ref, far_ref):
-    core = core_ref[0]
+def edge_kernel(cot_ref, coef_ref, after_ref, near_ref, far_ref):
+    core = lax.axis_index("core")
     for out, edge, step in (
         (far_ref, (BX - 1) * core, 1 - 2 * core),
         (near_ref, (BX - 1) * (1 - core), 2 * core - 1),
@@ -185,12 +184,12 @@
 
 
 def first_kernel(
-    core_ref, w5_edges_ref, inverse_edges_ref, c3_edges_ref, own_rows_ref, part_sums_ref, c3_ref,
+    w5_edges_ref, inverse_edges_ref, c3_edges_ref, own_rows_ref, part_sums_ref, c3_ref,
     near_ref, far_ref, ylow_ref, yhigh_ref, into_ref,
     rows_ref, cnear_ref, cfar_ref, added_ref, send_hbm, planes_hbm, c3_hbm,
     send_ref, sems,
 ):
-    core = core_ref[0]
+    core = lax.axis_index("core")
     copies = fetch(
         [
             (c3_ref, c3_hbm),
@@ -253,8 +252,10 @@
     wait(copies)
 
 
-def coarse_kernel(place_ref, got_ref, table_ref, own_ref, one_ref, two_ref, three_ref, rolled_ref, sums_ref):
-    mate, group, gy = place_ref[1], place_ref[2], place_ref[3]
+def coarse_kernel(got_ref, table_ref, own_ref, one_ref, two_ref, three_ref, rolled_ref, sums_ref):
+    mate = lax.axis_index("chip") * 2 + lax.axis_index("core")
+    group = lax.axis_index("x") * 2 + lax.axis_index("pair")
+    gy = lax.axis_index("gy")
     turn = lax.rem(GY - gy, GY)
     for q in range(GROUPS):
         plane = lax.rem(group + q, GROUPS)
@@ -279,10 +280,10 @@
 
 
 def last_kernel(
-    core_ref, own_ref, one_ref, two_ref, three_ref, out_table_ref, c3_ref, base_ref, inverse_ref, planes_ref, added_ref, rows_ref, cnear_ref, cfar_ref,
+    own_ref, one_ref, two_ref, three_ref, out_table_ref, c3_ref, base_ref, inverse_ref, planes_ref, added_ref, rows_ref, cnear_ref, cfar_ref,
     out_hbm, w_ref, out_ref, sems,
 ):
-    core = core_ref[0]
+    core = lax.axis_index("core")
     modes = (own_ref[...] + one_ref[...]) + (two_ref[...] + three_ref[...])
     coarse = jnp.dot(modes, out_table_ref[...], precision=lax.Precision.HIGHEST, preferred_element_type=F32)
     low, middle, high = (coarse[m * OUT_Y : (m + 1) * OUT_Y, :] for m in range(3))
@@ -334,8 +335,7 @@
     if sems:
         scratch.append(pltpu.SemaphoreType.DMA((sems,)))
     ins = [
-        x if spec is SMEM else pltpu.with_memory_space_constraint(x, spec.memory_space)
-        for x, spec in zip(ins, in_specs)
+        pltpu.with_memory_space_constraint(x, spec.memory_space) for x, spec in zip(ins, in_specs)
     ]
     return pl.pallas_call(
         kernel,
@@ -357,9 +357,6 @@
     table, into, out_table = tables()
     along_x = ("x", "pair", "chip", "core")
     core = lax.axis_index("core")
-    mate = lax.axis_index("chip") * 2 + core
-    place = jnp.stack([core, mate, lax.axis_index("x") * 2 + lax.axis_index("pair"), lax.axis_index("gy")])
-    place = place.astype(jnp.int32)
     near_pairs = [(i, i ^ 1) for i in range(GX)]
     far_pairs = [(i, (i + 1) % GX if i % 2 else (i - 1) % GX) for i in range(GX)]
     up = [(i, (i + 1) % GY) for i in range(GY)]
@@ -375,8 +372,8 @@
     tiny_near, tiny_far, y_low, y_high = call(
         strip_kernel,
         [(8, NZ), (8, NZ), (34, NZ), (34, NZ)],
-        [place, cotangent, coefficient],
-        [SMEM, HBM, HBM],
+        [cotangent, coefficient],
+        [HBM, HBM],
         [VMEM] * 4,
         scratch=[(2, BX, 8, NZ), (2, BX, 8, NZ)],
         sems=4,
@@ -385,8 +382,8 @@
     near, far = call(
         edge_kernel,
         [(3,) + plane, (3,) + plane],
-        [place, cotangent, coefficient, tiny_near],
-        [SMEM, VMEM, VMEM, VMEM],
+        [cotangent, coefficient, tiny_near],
+        [VMEM, VMEM, VMEM],
         [VMEM] * 2,
     )
     far, near = far_swap(far), near_swap(near)
@@ -410,8 +407,8 @@
     rows, c_near, c_far, added, send, planes, c3 = call(
         first_kernel,
         [(8, BX, NZ), plane, plane, (2,) + edge_planes, (GROUPS * GY, 4, 2 * CZ), edge_planes, brick],
-        [place, w5_edges, inverse_edges, c3_edges, own_rows, sums, c3, near, far, from_low, from_high, jnp.asarray(into)],
-        [SMEM] + [VMEM] * 11,
+        [w5_edges, inverse_edges, c3_edges, own_rows, sums, c3, near, far, from_low, from_high, jnp.asarray(into)],
+        [VMEM] * 11,
         [VMEM] * 4 + [HBM] * 3,
         scratch=[(GROUPS * GY, 4, 2 * CZ)],
         sems=4,
@@ -430,8 +427,8 @@
     own, one, two, three = call(
         coarse_kernel,
         [(3 * OUT_Y, 2 * CZ)] * 4,
-        [place, got.reshape(GROUPS, ROWS, 2 * CZ), table],
-        [SMEM, VMEM, VMEM],
+        [got.reshape(GROUPS, ROWS, 2 * CZ), table],
+        [VMEM, VMEM],
         [VMEM] * 4,
         scratch=[(GROUPS, 4, GY, 2 * CZ), (OUT_X, OUT_Y, 2 * CZ)],
         cost=pl.CostEstimate(flops=10**11, bytes_accessed=10**7, transcendentals=0),
@@ -442,8 +439,8 @@
     return call(
         last_kernel,
         [brick],
-        [place, own, one, two, three, jnp.asarray(out_table), c3, base, inverse, planes, added, rows, c_near, c_far],
-        [SMEM] + [VMEM] * 13,
+        [own, one, two, three, jnp.asarray(out_table), c3, base, inverse, planes, added, rows, c_near, c_far],
+        [VMEM] * 13,
         [HBM],
         scratch=[(BX + 2,) + plane, brick],
         sems=BX,

time: 52.4 us -> 49.6 us (0.947)
  Pallas kernels: 11.1 us -> 8.27 us
    pallas_call x7, Pallas kernels: 11.1 us -> 8.27 us  [call(): pl.pallas_call(kernel, out_shape=[spec.memory_space(shape, F32) for shape...]
  transfers between devices with their start and end apart: 12 -> 12, of which waited for: 4 -> 4; matrix products, arithmetic and copies ran while one was open for 0% -> 0% of each run, Pallas kernels for 8% -> 6%
where the time goes in v6:
time: 49.6 us; the launch traced here: 49.4 us
  starting transfers between devices  30.4 us (61%)
  waiting for transfers between devices  10.5 us (21%)
  Pallas kernels  8.27 us (17%)
    all_to_all x1, starting transfers between devices, body(): got = lax.all_to_all(send, ('x', 'pair', 'gy'), 0, 0, tiled=True)  9.32 us
    ppermute x3, starting transfers between devices, near_swap(): return lax.ppermute(v, along_x, near_pairs)  8.8 us
    pallas_call x7, Pallas kernels, call(): pl.pallas_call(kernel, out_shape=[spec.memory_space(shape, F32) for shape...  8.27 us
    all_to_all x1, waiting for transfers between devices, body(): got = lax.all_to_all(send, ('x', 'pair', 'gy'), 0, 0, tiled=True)  7.93 us
    ppermute x3, starting transfers between devices, body(): lax.ppermute(v, along_x, [(i, i ^ flip) for i in range(GX)])  5.5 us
    ppermute x1, starting transfers between devices, body(): from_high = lax.ppermute(y_low, 'gy', down)  4.03 us
    ppermute x3, waiting for transfers between devices, body(): lax.ppermute(v, along_x, [(i, i ^ flip) for i in range(GX)])  1.74 us
    ppermute x1, starting transfers between devices, body(): from_low = lax.ppermute(y_high, 'gy', up)  1.71 us
  transfers between devices with their start and end apart: 12, of which 4 were waited for; matrix products, arithmetic and copies ran while one was open for 0% of the time, Pallas kernels for 6%

profile of v6, /device:TPU:1, one launch (start us, length us, event | category | flops | bytes accessed | tf_op | source)
XLA Modules:
  0.0 49.4 jit_solution(10643106653452312484)
XLA Ops:
  0.0 0.0 copy-start.1
  0.0 0.0 copy-start
  0.0 1.4 %shard_map.56 = (f32[8,512]{1,0:T(8,128)S(1)}, f32[8,512]{1,0:T(8,128)S(1)}, f32[34,512]{1,0:T(8,128)S(1)}, f32[34,512]{1,0:T(8,128)S(1)}) custom-call(f32[8,64,512]{2,1,0:T(8,128)} %cot_ref.3, f32[8,64,512]{2,1,0:T(8,128)} %coef_ref.3), custom_call_target="tpu_custom_call" | custom-call | tf_op jit(solution)/shard_map/pallas_call | solution.py:340
  1.4 3.3 %collective-permute-start = (f32[8,512]{1,0:T(8,128)S(1)}, f32[8,512]{1,0:T(8,128)S(1)}, u32[]{:S(2)}, u32[]{:S(2)}) collective-permute-start(f32[8,512]{1,0:T(8,128)S(1)} %get-tuple-element.41), channel_id=1, source_target_pairs={{0,8},{8,0},{16,24},{24,16},{32,40},{40,32},{48,56},{56,48},{64,72... | collective-permute-start | bytes 49160 | tf_op jit(solution)/shard_map/ppermute | solution.py:366
  4.7 0.0 collective-permute-start.3
  4.8 0.8 %collective-permute-done.after_ref = f32[8,512]{1,0:T(8,128)S(1)} collective-permute-done((f32[8,512]{1,0:T(8,128)S(1)}, f32[8,512]{1,0:T(8,128)S(1)}, u32[]{:S(2)}, u32[]{:S(2)}) %collective-permute-start) | collective-permute-done | bytes 16416 | tf_op jit(solution)/shard_map/ppermute | solution.py:366
  5.6 0.0 copy-done.1
  5.6 0.0 copy-done
  5.6 0.1 shard_map.57
  5.7 2.9 %collective-permute-start.1 = (f32[3,64,512]{2,1,0:T(8,128)S(1)}, f32[3,64,512]{2,1,0:T(8,128)S(1)}, u32[]{:S(2)}, u32[]{:S(2)}) collective-permute-start(f32[3,64,512]{2,1,0:T(8,128)S(1)} %get-tuple-element.42), channel_id=1, source_target_pairs={{0,8},{8,0},{16,24},{24,16},{32,40},{40,32},{48,56},{56,48},{64,72... | collective-permute-start | bytes 1179656 | tf_op jit(solution)/shard_map/ppermute | solution.py:366
  8.6 0.0 collective-permute-start.2
  8.6 0.0 collective-permute-done.3
  8.7 1.7 %collective-permute-start.4 = (f32[42,512]{1,0:T(8,128)S(1)}, f32[42,512]{1,0:T(8,128)S(1)}, u32[]{:S(2)}, u32[]{:S(2)}) collective-permute-start(f32[42,512]{1,0:T(8,128)S(1)} %pad_maximum_fusion), channel_id=1, source_target_pairs={{0,1},{1,2},{2,3},{3,4},{4,5},{5,6},{6,7},{7,0},{8,9},{9,10},{10,1... | collective-permute-start | bytes 258056 | tf_op jit(solution)/shard_map/ppermute | solution.py:394
  10.4 0.0 copy-start.8
  10.4 4.0 %collective-permute-start.5 = (f32[42,512]{1,0:T(8,128)S(1)}, f32[42,512]{1,0:T(8,128)S(1)}, u32[]{:S(2)}, u32[]{:S(2)}) collective-permute-start(f32[42,512]{1,0:T(8,128)S(1)} %pad_maximum_fusion.1), channel_id=1, source_target_pairs={{0,7},{1,0},{2,1},{3,2},{4,3},{5,4},{6,5},{7,6},{8,15},{9,8},{10,9... | collective-permute-start | bytes 258056 | tf_op jit(solution)/shard_map/ppermute | solution.py:395
  14.4 2.4 %shard_map.55 = (f32[2,64,512]{2,1,0:T(8,128)S(1)}, f32[2,64,512]{2,1,0:T(8,128)S(1)}, f32[2,64,512]{2,1,0:T(8,128)S(1)}, f32[6,8,512]{2,1,0:T(8,128)S(1)}, f32[...) custom-call(f32[8,64,512]{2,1,0:T(8,128)S(1)} %copy-done, ...), custom_call_target="tpu_custom_call" | custom-call | flops 10485760 | bytes 5242880 | tf_op jit(solution)/shard_map/pallas_call | solution.py:340
  16.9 0.0 collective-permute-done.4.ylow_ref
  16.9 0.0 collective-permute-done.5.yhigh_ref
  16.9 0.0 collective-permute-done.1.near_ref
  16.9 0.0 collective-permute-done.2.far_ref
  16.9 0.0 copy-done.8
  16.9 0.0 copy-start.6
  16.9 1.6 %shard_map.58 = (f32[8,8,512]{2,1,0:T(8,128)S(1)}, f32[64,512]{1,0:T(8,128)S(1)}, f32[64,512]{1,0:T(8,128)S(1)}, f32[2,2,64,512]{3,2,1,0:T(8,128)S(1)}, f32[64,4...) custom-call(f32[2,64,512]{2,1,0:T(8,128)S(1)} %get-tuple-element.35.w5_edges_ref, ...), custom_call_target="tpu_custom_call" | custom-call | tf_op jit(solution)/shard_map/pallas_call | solution.py:340
  18.5 9.3 %all-to-all-start = ((f32[64,4,128]{2,1,0:T(4,128)}), f32[64,4,128]{2,1,0:T(4,128)S(1)}, u32[]{:S(2)}, u32[]{:S(2)}) async-start(f32[64,4,128]{2,1,0:T(4,128)} %get-tuple-element.47), calls=%async_computation | async-start | bytes 262144 | tf_op jit(solution)/shard_map/all_to_all | solution.py:416
  27.8 2.6 %collective-permute-start.9 = (f32[64,512]{1,0:T(8,128)S(1)}, f32[64,512]{1,0:T(8,128)S(1)}, u32[]{:S(2)}, u32[]{:S(2)}) collective-permute-start(f32[64,512]{1,0:T(8,128)S(1)} %get-tuple-element.63), channel_id=1, source_target_pairs={{0,8},{8,0},{16,24},{24,16},{32,40},{40,32},{48,56},{56,48},{64,72... | collective-permute-start | bytes 393224 | tf_op jit(solution)/shard_map/ppermute | solution.py:366
  30.4 1.0 %collective-permute-start.10 = (f32[64,512]{1,0:T(8,128)S(1)}, f32[64,512]{1,0:T(8,128)S(1)}, u32[]{:S(2)}, u32[]{:S(2)}) collective-permute-start(f32[64,512]{1,0:T(8,128)S(1)} %get-tuple-element.64), channel_id=1, source_target_pairs={{0,248},{8,16},{16,8},{24,32},{32,24},{40,48},{48,40},{56,64},{64,... | collective-permute-start | bytes 393224 | tf_op jit(solution)/shard_map/ppermute | solution.py:369
  31.4 7.9 %all-to-all-done.refs_0_ = f32[64,4,128]{2,1,0:T(4,128)S(1)} async-done(((f32[64,4,128]{2,1,0:T(4,128)}), f32[64,4,128]{2,1,0:T(4,128)S(1)}, u32[]{:S(2)}, u32[]{:S(2)}) %all-to-all-start) | async-done | bytes 131104 | tf_op jit(solution)/shard_map/all_to_all | solution.py:416
  39.3 0.0 copy-done.6
  39.3 0.0 copy-start.2
  39.3 0.0 copy-start.3
  39.3 0.0 copy-start.4
  39.3 0.0 copy-start.5
  39.3 0.0 copy-start.7
  39.3 0.6 %shard_map.60 = (f32[30,128]{1,0:T(8,128)S(1)}, f32[30,128]{1,0:T(8,128)S(1)}, f32[30,128]{1,0:T(8,128)S(1)}, f32[30,128]{1,0:T(8,128)S(1)}) custom-call(f32[8,32,128]{2,1,0:T(8,128)S(1)} %bitcast.1, f32[17,13,8,128]{3,2,1,0:T(8,128)S(1)} %copy-done.6), custom_call_target="tpu_custom_call" | custom-call | flops 99999997952 | bytes 10000000 | tf_op jit(solution)/shard_map/pallas_call | solution.py:340
  40.0 3.8 %collective-permute-start.6 = (f32[30,128]{1,0:T(8,128)S(1)}, f32[30,128]{1,0:T(8,128)S(1)}, u32[]{:S(2)}, u32[]{:S(2)}) collective-permute-start(f32[30,128]{1,0:T(8,128)S(1)} %get-tuple-element.54), channel_id=1, source_target_pairs={{0,8},{8,0},{16,24},{24,16},{32,40},{40,32},{48,56},{56,48},{64,72... | collective-permute-start | bytes 46088 | tf_op jit(solution)/shard_map/ppermute | solution.py:437
  43.7 0.0 collective-permute-start.7
  43.7 1.7 %collective-permute-start.8 = (f32[30,128]{1,0:T(8,128)S(1)}, f32[30,128]{1,0:T(8,128)S(1)}, u32[]{:S(2)}, u32[]{:S(2)}) collective-permute-start(f32[30,128]{1,0:T(8,128)S(1)} %get-tuple-element.56), channel_id=1, source_target_pairs={{0,24},{8,16},{16,8},{24,0},{32,56},{40,48},{48,40},{56,32},{64,88... | collective-permute-start | bytes 46088 | tf_op jit(solution)/shard_map/ppermute | solution.py:437
  45.5 0.0 collective-permute-done.9.cnear_ref
  45.5 0.0 collective-permute-done.10.cfar_ref
  45.5 0.0 collective-permute-done.6.one_ref
  45.5 0.9 %collective-permute-done.7.two_ref = f32[30,128]{1,0:T(8,128)S(1)} collective-permute-done((f32[30,128]{1,0:T(8,128)S(1)}, f32[30,128]{1,0:T(8,128)S(1)}, u32[]{:S(2)}, u32[]{:S(2)}) %collective-permute-start.7) | collective-permute-done | bytes 15392 | tf_op jit(solution)/shard_map/ppermute | solution.py:437
  46.3 0.9 %collective-permute-done.8.three_ref = f32[30,128]{1,0:T(8,128)S(1)} collective-permute-done((f32[30,128]{1,0:T(8,128)S(1)}, f32[30,128]{1,0:T(8,128)S(1)}, u32[]{:S(2)}, u32[]{:S(2)}) %collective-permute-start.8) | collective-permute-done | bytes 15392 | tf_op jit(solution)/shard_map/ppermute | solution.py:437
  47.2 0.0 copy-done.2
  47.2 0.0 copy-done.3
  47.2 0.0 copy-done.4
  47.2 0.0 copy-done.5
  47.2 0.0 copy-done.7
  47.2 2.2 %shard_map.61 = f32[8,64,512]{2,1,0:T(8,128)} custom-call(f32[30,128]{1,0:T(8,128)S(1)} %get-tuple-element.53.own_ref, f32[30,128]{1,0:T(8,128)S(1)} %collective-permute-done.6.one_ref, f32[30,128]{1,0:T(8,128)S(1)} %collective-permute-done.7.two_ref, f32[30,128]{1,0:T(8,128)S(1)} %collective-permute-done.8.three_ref, f32[128,512]{1,0:T(8,128)S(1)} %copy-done.7, ...), custom_call_target="tpu_custom_call" | custom-call | tf_op jit(solution)/shard_map/pallas_call | solution.py:340
  (9 shorter events, 0.1 us)
Async XLA Ops:
  0.0 5.6 %copy-start.1 = (f32[8,64,512]{2,1,0:T(8,128)S(1)}, f32[8,64,512]{2,1,0:T(8,128)}, u32[]{:S(2)}) copy-start(f32[8,64,512]{2,1,0:T(8,128)} %coef_ref.3) | copy-start | bytes 3145732
  0.0 5.6 %copy-start = (f32[8,64,512]{2,1,0:T(8,128)S(1)}, f32[8,64,512]{2,1,0:T(8,128)}, u32[]{:S(2)}) copy-start(f32[8,64,512]{2,1,0:T(8,128)} %cot_ref.3) | copy-start | bytes 3145732
  1.4 4.2 %collective-permute-start = (f32[8,512]{1,0:T(8,128)S(1)}, f32[8,512]{1,0:T(8,128)S(1)}, u32[]{:S(2)}, u32[]{:S(2)}) collective-permute-start(f32[8,512]{1,0:T(8,128)S(1)} %get-tuple-element.41), channel_id=1, source_target_pairs={{0,8},{8,0},{16,24},{24,16},{32,40},{40,32},{48,56},{56,48},{64,72... | collective-permute-start | bytes 49160 | tf_op jit(solution)/shard_map/ppermute | solution.py:366
  4.7 3.9 %collective-permute-start.3 = (f32[8,512]{1,0:T(8,128)S(1)}, f32[8,512]{1,0:T(8,128)S(1)}, u32[]{:S(2)}, u32[]{:S(2)}) collective-permute-start(f32[8,512]{1,0:T(8,128)S(1)} %get-tuple-element.45), channel_id=1, source_target_pairs={{0,248},{8,16},{16,8},{24,32},{32,24},{40,48},{48,40},{56,64},{64,... | collective-permute-start | bytes 49160 | tf_op jit(solution)/shard_map/ppermute | solution.py:369
  5.7 11.2 %collective-permute-start.1 = (f32[3,64,512]{2,1,0:T(8,128)S(1)}, f32[3,64,512]{2,1,0:T(8,128)S(1)}, u32[]{:S(2)}, u32[]{:S(2)}) collective-permute-start(f32[3,64,512]{2,1,0:T(8,128)S(1)} %get-tuple-element.42), channel_id=1, source_target_pairs={{0,8},{8,0},{16,24},{24,16},{32,40},{40,32},{48,56},{56,48},{64,72... | collective-permute-start | bytes 1179656 | tf_op jit(solution)/shard_map/ppermute | solution.py:366
  8.6 8.3 %collective-permute-start.2 = (f32[3,64,512]{2,1,0:T(8,128)S(1)}, f32[3,64,512]{2,1,0:T(8,128)S(1)}, u32[]{:S(2)}, u32[]{:S(2)}) collective-permute-start(f32[3,64,512]{2,1,0:T(8,128)S(1)} %get-tuple-element.43), channel_id=1, source_target_pairs={{0,248},{8,16},{16,8},{24,32},{32,24},{40,48},{48,40},{56,64},{64,... | collective-permute-start | bytes 1179656 | tf_op jit(solution)/shard_map/ppermute | solution.py:369
  8.7 8.2 %collective-permute-start.4 = (f32[42,512]{1,0:T(8,128)S(1)}, f32[42,512]{1,0:T(8,128)S(1)}, u32[]{:S(2)}, u32[]{:S(2)}) collective-permute-start(f32[42,512]{1,0:T(8,128)S(1)} %pad_maximum_fusion), channel_id=1, source_target_pairs={{0,1},{1,2},{2,3},{3,4},{4,5},{5,6},{6,7},{7,0},{8,9},{9,10},{10,1... | collective-permute-start | bytes 258056 | tf_op jit(solution)/shard_map/ppermute | solution.py:394
  10.4 6.5 %copy-start.8 = (f32[512,64]{1,0:T(8,128)S(1)}, f32[512,64]{1,0:T(8,128)}, u32[]{:S(2)}) copy-start(f32[512,64]{1,0:T(8,128)} %constant.14.clone.into_ref) | copy-start | bytes 393220
  10.4 6.5 %collective-permute-start.5 = (f32[42,512]{1,0:T(8,128)S(1)}, f32[42,512]{1,0:T(8,128)S(1)}, u32[]{:S(2)}, u32[]{:S(2)}) collective-permute-start(f32[42,512]{1,0:T(8,128)S(1)} %pad_maximum_fusion.1), channel_id=1, source_target_pairs={{0,7},{1,0},{2,1},{3,2},{4,3},{5,4},{6,5},{7,6},{8,15},{9,8},{10,9... | collective-permute-start | bytes 258056 | tf_op jit(solution)/shard_map/ppermute | solution.py:395
  16.9 22.4 %copy-start.6 = (f32[17,13,8,128]{3,2,1,0:T(8,128)S(1)}, f32[17,13,8,128]{3,2,1,0:T(8,128)}, u32[]{:S(2)}) copy-start(f32[17,13,8,128]{3,2,1,0:T(8,128)} %constant.15.clone.refs_5_.table_ref) | copy-start | bytes 2715652
  18.5 20.8 %all-to-all-start = ((f32[64,4,128]{2,1,0:T(4,128)}), f32[64,4,128]{2,1,0:T(4,128)S(1)}, u32[]{:S(2)}, u32[]{:S(2)}) async-start(f32[64,4,128]{2,1,0:T(4,128)} %get-tuple-element.47), calls=%async_computation | async-start | bytes 262144 | tf_op jit(solution)/shard_map/all_to_all | solution.py:416
  27.8 17.7 %collective-permute-start.9 = (f32[64,512]{1,0:T(8,128)S(1)}, f32[64,512]{1,0:T(8,128)S(1)}, u32[]{:S(2)}, u32[]{:S(2)}) collective-permute-start(f32[64,512]{1,0:T(8,128)S(1)} %get-tuple-element.63), channel_id=1, source_target_pairs={{0,8},{8,0},{16,24},{24,16},{32,40},{40,32},{48,56},{56,48},{64,72... | collective-permute-start | bytes 393224 | tf_op jit(solution)/shard_map/ppermute | solution.py:366
  30.4 15.1 %collective-permute-start.10 = (f32[64,512]{1,0:T(8,128)S(1)}, f32[64,512]{1,0:T(8,128)S(1)}, u32[]{:S(2)}, u32[]{:S(2)}) collective-permute-start(f32[64,512]{1,0:T(8,128)S(1)} %get-tuple-element.64), channel_id=1, source_target_pairs={{0,248},{8,16},{16,8},{24,32},{32,24},{40,48},{48,40},{56,64},{64,... | collective-permute-start | bytes 393224 | tf_op jit(solution)/shard_map/ppermute | solution.py:369
  39.3 7.9 %copy-start.2 = (f32[8,64,512]{2,1,0:T(8,128)S(1)}, f32[8,64,512]{2,1,0:T(8,128)}, u32[]{:S(2)}) copy-start(f32[8,64,512]{2,1,0:T(8,128)} %get-tuple-element.58.base_ref) | copy-start | bytes 3145732
  39.3 7.9 %copy-start.3 = (f32[8,64,512]{2,1,0:T(8,128)S(1)}, f32[8,64,512]{2,1,0:T(8,128)}, u32[]{:S(2)}) copy-start(f32[8,64,512]{2,1,0:T(8,128)} %get-tuple-element.59.inverse_ref) | copy-start | bytes 3145732
  39.3 7.9 %copy-start.4 = (f32[8,64,512]{2,1,0:T(8,128)S(1)}, f32[8,64,512]{2,1,0:T(8,128)}, u32[]{:S(2)}) copy-start(f32[8,64,512]{2,1,0:T(8,128)} %get-tuple-element.57.c3_ref) | copy-start | bytes 3145732
  39.3 7.9 %copy-start.5 = (f32[2,64,512]{2,1,0:T(8,128)S(1)}, f32[2,64,512]{2,1,0:T(8,128)}, u32[]{:S(2)}) copy-start(f32[2,64,512]{2,1,0:T(8,128)} %get-tuple-element.60.planes_ref) | copy-start | bytes 786436
  39.3 7.9 %copy-start.7 = (f32[128,512]{1,0:T(8,128)S(1)}, f32[128,512]{1,0:T(8,128)}, u32[]{:S(2)}) copy-start(f32[128,512]{1,0:T(8,128)} %constant.16.clone.out_table_ref) | copy-start | bytes 786436
  40.0 5.5 %collective-permute-start.6 = (f32[30,128]{1,0:T(8,128)S(1)}, f32[30,128]{1,0:T(8,128)S(1)}, u32[]{:S(2)}, u32[]{:S(2)}) collective-permute-start(f32[30,128]{1,0:T(8,128)S(1)} %get-tuple-element.54), channel_id=1, source_target_pairs={{0,8},{8,0},{16,24},{24,16},{32,40},{40,32},{48,56},{56,48},{64,72... | collective-permute-start | bytes 46088 | tf_op jit(solution)/shard_map/ppermute | solution.py:437
  43.7 2.6 %collective-permute-start.7 = (f32[30,128]{1,0:T(8,128)S(1)}, f32[30,128]{1,0:T(8,128)S(1)}, u32[]{:S(2)}, u32[]{:S(2)}) collective-permute-start(f32[30,128]{1,0:T(8,128)S(1)} %get-tuple-element.55), channel_id=1, source_target_pairs={{0,16},{8,24},{16,0},{24,8},{32,48},{40,56},{48,32},{56,40},{64,80... | collective-permute-start | bytes 46088 | tf_op jit(solution)/shard_map/ppermute | solution.py:437
  43.7 3.5 %collective-permute-start.8 = (f32[30,128]{1,0:T(8,128)S(1)}, f32[30,128]{1,0:T(8,128)S(1)}, u32[]{:S(2)}, u32[]{:S(2)}) collective-permute-start(f32[30,128]{1,0:T(8,128)S(1)} %get-tuple-element.56), channel_id=1, source_target_pairs={{0,24},{8,16},{16,8},{24,0},{32,56},{40,48},{48,40},{56,32},{64,88... | collective-permute-start | bytes 46088 | tf_op jit(solution)/shard_map/ppermute | solution.py:437
